TPU v7x, 128 devices: a whole 4x4x4 slice. The times are simulated.
128 devices in a mesh: dp: 32 (over y, x, z_lo), sp: 4 (over z_hi, core).
Axes of the slice: x: 4, y: 4, z: 4 (z_hi: 2, z_lo: 2; z = z_hi * 2 + z_lo), core: 2. Of those that a mesh axis runs over, the one named last changes fastest.
Arguments:
- queries: bfloat16 [32, 1024, 2048], P('dp', 'sp'), may hold values from -80 to 80
- keys: bfloat16 [32, 1024, 512], P('dp', 'sp'), may hold values from -16 to 16
- values: bfloat16 [32, 1024, 512], P('dp', 'sp'), may hold values from -6 to 6
- cotangent: bfloat16 [32, 1024, 2048], P('dp', 'sp'), may hold values from -6 to 6
- doc_ids: int32 [32, 1024], P('dp', 'sp'), may hold values from 0 to 7, as said below
- partners: int32 [16, 32], P(None, 'dp'), may hold values from 0 to 31, as said below
- swap_slots: int32 [32, 4, 16], P('dp', 'sp'), may hold values from 0 to 31, as said below
Outputs:
- attended: bfloat16 [32, 1024, 2048], P('dp', 'sp')
- grad_queries: bfloat16 [32, 1024, 2048], P('dp', 'sp')
- grad_keys: bfloat16 [32, 1024, 512], P('dp', 'sp')
- grad_values: bfloat16 [32, 1024, 512], P('dp', 'sp')
Inputs may be any that keep to these rules, and one draw needn't show every extreme that they name: Each row t is a pairing of the groups: partners[t, partners[t, i]] = i and partners[t, i] != i; no two rounds give a group the same partner. `swap_slots`: for each group and sp index the 16 block numbers are distinct. `doc_ids`: along each group's slice the ids start at 0, never fall, rise only at positions that are multiples of 8, and every id of 0 to 7 occurs.
All inputs are finite; a program needn't handle non-finite values.
Results may differ from a plain program's by a relative error of at most 0.008.
Values may be sent and summed in bfloat16 or wider, within the bound.
No kernel may reach another device: no remote copies, remote signals or barrier semaphores. Data moves between devices by JAX's collectives and lax.ppermute only.
A program may use at most 128 MiB of HBM per device.

v0:
```python
import jax
import jax.numpy as jnp
from jax import lax
from jax.experimental import pallas as pl
from jax.experimental.pallas import tpu as pltpu
from jax.sharding import PartitionSpec as P

KEY_VALUE_HEADS = 4
SHARED = 4
HEAD_SIZE = 128
BLOCK = 8
ROUNDS = 16
ROWS = 256
HALF = ROUNDS * BLOCK
GROUPS = 32
RANKS = 4
WIDE = SHARED * HEAD_SIZE
PAIR = 2 * HEAD_SIZE
BUNDLE = WIDE + PAIR
META = 384
FACTOR = HEAD_SIZE ** (-0.5)
EXP2_FACTOR = FACTOR * 1.4426950408889634
MASKED = -1e30
BF16 = jnp.bfloat16
F32 = jnp.float32

SMEM = pl.BlockSpec(memory_space=pltpu.SMEM)
PARAMS = pltpu.CompilerParams(vmem_limit_bytes=56 * 1024 * 1024)


def iota(shape, axis):
    return lax.broadcasted_iota(jnp.int32, shape, axis)


def onehot(hit):
    return jnp.where(hit, 1.0, 0.0).astype(BF16)


def pick(matrix, rows):
    return jnp.dot(matrix, rows, preferred_element_type=F32).astype(BF16)


def position(axis, count=ROWS):
    return iota((count, 1) if axis == 0 else (1, count), axis)


def sent_row(mate, slot):
    place = position(0)
    block = jnp.zeros_like(place)
    for t in range(ROUNDS):
        block = jnp.where(place >> 3 == mate[t], slot[t], block)
    return block * BLOCK + (place & 7)


def landed_row(mate, slot):
    place = position(0)
    group = jnp.full_like(place, -1)
    for t in range(ROUNDS):
        group = jnp.where(place >> 3 == slot[t], mate[t], group)
    return jnp.where(group >= 0, group * BLOCK + (place & 7), -1)


def packed_row(slot, axis):
    place = position(axis)
    block = place >> 3
    lower = jnp.zeros_like(place)
    turn = jnp.full_like(place, -1)
    for t in range(ROUNDS):
        lower = lower + (block > slot[t]).astype(jnp.int32)
        turn = jnp.where(block == slot[t], t, turn)
    return jnp.where(turn >= 0, HALF + turn * BLOCK, (block - lower) * BLOCK) + (place & 7)


def turn_row(mate):
    place = position(0, HALF)
    group = jnp.zeros_like(place)
    for t in range(ROUNDS):
        group = jnp.where(place >> 3 == t, mate[t], group)
    return group * BLOCK + (place & 7)


def sent_turn(mate):
    place = position(0)
    turn = jnp.zeros_like(place)
    for t in range(ROUNDS):
        turn = jnp.where(place >> 3 == mate[t], t, turn)
    return turn * BLOCK + (place & 7)


def scalars(ref, first, count):
    return [ref[first + t] for t in range(count)]


def lanes(width):
    return iota((1, width), 1)


def outgoing_kernel(mate_ref, slot_ref, q_ref, k_ref, v_ref, g_ref, first_ref, second_ref, stay_ref, choose, keep):
    @pl.when(pl.program_id(0) == 0)
    def _():
        mate, slot = scalars(mate_ref, 0, ROUNDS), scalars(slot_ref, 0, ROUNDS)
        choose[...] = onehot(sent_row(mate, slot) == lanes(ROWS))
        keep[...] = onehot(packed_row(slot, 1) == position(0, HALF))

    pairs = jnp.concatenate([k_ref[...], v_ref[...]], axis=1)
    first_ref[...] = pick(choose[...], jnp.concatenate([q_ref[...], pairs], axis=1))
    second_ref[...] = pick(choose[...], g_ref[...])
    stay_ref[...] = pick(keep[...], pairs)


def outgoing(mate, slot, q, k, v, g):
    return pl.pallas_call(
        outgoing_kernel,
        grid=(KEY_VALUE_HEADS,),
        in_specs=[
            SMEM,
            SMEM,
            pl.BlockSpec((ROWS, WIDE), lambda h: (0, h)),
            pl.BlockSpec((ROWS, HEAD_SIZE), lambda h: (0, h)),
            pl.BlockSpec((ROWS, HEAD_SIZE), lambda h: (0, h)),
            pl.BlockSpec((ROWS, WIDE), lambda h: (0, h)),
        ],
        out_specs=[
            pl.BlockSpec((ROWS, BUNDLE), lambda h: (0, h)),
            pl.BlockSpec((ROWS, WIDE), lambda h: (0, h)),
            pl.BlockSpec((HALF, PAIR), lambda h: (0, h)),
        ],
        out_shape=[
            jax.ShapeDtypeStruct((ROWS, KEY_VALUE_HEADS * BUNDLE), BF16),
            jax.ShapeDtypeStruct((ROWS, KEY_VALUE_HEADS * WIDE), BF16),
            jax.ShapeDtypeStruct((HALF, KEY_VALUE_HEADS * PAIR), BF16),
        ],
        scratch_shapes=[pltpu.VMEM((ROWS, ROWS), BF16), pltpu.VMEM((HALF, ROWS), BF16)],
        compiler_params=PARAMS,
        cost_estimate=pl.CostEstimate(flops=10**9, bytes_accessed=5 * 10**6, transcendentals=0),
        name="outgoing",
    )(mate, slot, q, k, v, g)


def traded_pairs_kernel(mate_ref, landed_ref, out_ref, choose):
    @pl.when(pl.program_id(0) == 0)
    def _():
        choose[...] = onehot(turn_row(scalars(mate_ref, 0, ROUNDS)) == lanes(ROWS))

    out_ref[...] = pick(choose[...], landed_ref[...])


def traded_pairs(mate, landed):
    return pl.pallas_call(
        traded_pairs_kernel,
        grid=(KEY_VALUE_HEADS,),
        in_specs=[SMEM, pl.BlockSpec((ROWS, PAIR), lambda h: (0, 3 * h + 2))],
        out_specs=pl.BlockSpec((HALF, PAIR), lambda h: (0, h)),
        out_shape=jax.ShapeDtypeStruct((HALF, KEY_VALUE_HEADS * PAIR), BF16),
        scratch_shapes=[pltpu.VMEM((HALF, ROWS), BF16)],
        compiler_params=PARAMS,
        cost_estimate=pl.CostEstimate(flops=10**8, bytes_accessed=8 * 10**5, transcendentals=0),
        name="traded_pairs",
    )(mate, landed)


def to_column(row):
    here = iota((ROWS, ROWS), 0) == iota((ROWS, ROWS), 1)
    return jnp.sum(jnp.where(here, row, 0.0), axis=1, keepdims=True)


def key_blocks(metas, rank):
    first = metas[0][0]
    count = jnp.int32(1)
    for x in (1, 2, 3):
        other = rank ^ x
        count = count + jnp.where((other < rank) & (metas[x][ROWS - 1] == first), 1, 0)
    return count


def forward_kernel(
    mate_ref, meta_own, meta_near, meta_far, meta_both, ids_own, ids_near, ids_far, ids_both,
    q_ref, landed_ref, stay_own, stay_far, stay_near, turn_own, turn_far, turn_near,
    out_ref, send_ref, merged_ref, pairs_ref,
    choose, bring, place, bias,
):
    metas = (meta_own, meta_near, meta_far, meta_both)
    rank = metas[0][ROWS + ROUNDS]

    @pl.when(pl.program_id(0) == 0)
    def _():
        mate, slot = scalars(mate_ref, 0, ROUNDS), scalars(metas[0], ROWS, ROUNDS)
        choose[...] = onehot(sent_row(mate, slot) == lanes(ROWS))
        bring[...] = onehot(landed_row(mate, slot) == lanes(ROWS))
        ids = [piece[:, :ROWS].astype(F32) for piece in (ids_own, ids_near, ids_far, ids_both)]
        column = to_column(ids[0])
        for x in range(RANKS):
            place[x] = onehot(packed_row(scalars(metas[x], ROWS, ROUNDS), 0) == lanes(ROWS))
            allowed = column == ids[x]
            if x == 0:
                allowed = allowed & (lanes(ROWS) <= position(0))
            bias[rank ^ x] = jnp.where(allowed, 0.0, MASKED)

    stay = (stay_own[...], stay_near[0], stay_far[...], stay_near[1])
    turn = (turn_own[...], turn_near[0], turn_far[...], turn_near[1])
    for x in range(RANKS):
        pairs_ref[pl.ds(pl.multiple_of((rank ^ x) * ROWS, ROWS), ROWS), :] = pick(
            place[x], jnp.concatenate([stay[x], turn[x]], axis=0)
        )
    came = landed_row(scalars(mate_ref, 0, ROUNDS), scalars(metas[0], ROWS, ROUNDS)) >= 0
    q = jnp.where(came, pick(bring[...], landed_ref[:, :WIDE]), q_ref[...])
    merged_ref[...] = q
    count = key_blocks(metas, rank)

    for n in range(1, RANKS + 1):

        @pl.when(count == n)
        def _(n=n):
            start = rank - (n - 1)
            window = pl.ds(pl.multiple_of(start * ROWS, ROWS), n * ROWS)
            k = pairs_ref[window, :HEAD_SIZE]
            v = pairs_ref[window, HEAD_SIZE:]
            mask = jnp.concatenate([bias[start + i] for i in range(n)], axis=1)
            for h in range(SHARED):
                columns = slice(h * HEAD_SIZE, (h + 1) * HEAD_SIZE)
                logits = lax.dot_general(q[:, columns], k, (((1,), (1,)), ((), ())), preferred_element_type=F32) + mask
                raised = jnp.exp2((logits - jnp.max(logits, axis=1, keepdims=True)) * EXP2_FACTOR)
                share = 1.0 / jnp.sum(raised, axis=1, keepdims=True)
                weights = (raised * share).astype(BF16)
                out_ref[:, columns] = jnp.dot(weights, v, preferred_element_type=F32).astype(BF16)

    send_ref[...] = pick(choose[...], out_ref[...])


def forward(mate, metas, q, landed, stays, turns):
    whole = lambda shape: pl.BlockSpec(shape, lambda h: (0,) * len(shape))
    pieces = [
        pl.BlockSpec((HALF, PAIR), lambda h: (0, h)),
        pl.BlockSpec((HALF, PAIR), lambda h: (0, h)),
        pl.BlockSpec((2, HALF, PAIR), lambda h: (0, 0, h)),
    ]
    return pl.pallas_call(
        forward_kernel,
        grid=(KEY_VALUE_HEADS,),
        in_specs=[SMEM] * 5 + [whole((1, META))] * 4
        + [pl.BlockSpec((ROWS, WIDE), lambda h: (0, h)), pl.BlockSpec((ROWS, BUNDLE), lambda h: (0, h))]
        + pieces
        + pieces,
        out_specs=[
            pl.BlockSpec((ROWS, WIDE), lambda h: (0, h)),
            pl.BlockSpec((ROWS, WIDE), lambda h: (0, h)),
            pl.BlockSpec((ROWS, WIDE), lambda h: (0, h)),
            pl.BlockSpec((RANKS * ROWS, PAIR), lambda h: (0, h)),
        ],
        out_shape=[
            jax.ShapeDtypeStruct((ROWS, KEY_VALUE_HEADS * WIDE), BF16),
            jax.ShapeDtypeStruct((ROWS, KEY_VALUE_HEADS * WIDE), BF16),
            jax.ShapeDtypeStruct((ROWS, KEY_VALUE_HEADS * WIDE), BF16),
            jax.ShapeDtypeStruct((RANKS * ROWS, KEY_VALUE_HEADS * PAIR), BF16),
        ],
        scratch_shapes=[
            pltpu.VMEM((ROWS, ROWS), BF16),
            pltpu.VMEM((ROWS, ROWS), BF16),
            pltpu.VMEM((RANKS, ROWS, ROWS), BF16),
            pltpu.VMEM((RANKS, ROWS, ROWS), F32),
        ],
        compiler_params=PARAMS,
        cost_estimate=pl.CostEstimate(flops=4 * 10**9, bytes_accessed=10**7, transcendentals=4 * 10**6),
        name="forward",
    )(mate, *metas, *[meta.reshape(1, META) for meta in metas], q, landed, *stays, *turns)


def backward_kernel(
    mate_ref, meta_own, meta_near, meta_far, meta_both, ids_own, ids_near, ids_far, ids_both,
    q_ref, g_ref, landed_ref, pairs_ref,
    dq_ref, send_ref, turn_keep, turn_send, stay_keep, stay_send,
    choose, bring, pack, bias, total,
):
    metas = (meta_own, meta_near, meta_far, meta_both)
    rank = metas[0][ROWS + ROUNDS]

    @pl.when(pl.program_id(0) == 0)
    def _():
        mate, slot = scalars(mate_ref, 0, ROUNDS), scalars(metas[0], ROWS, ROUNDS)
        choose[...] = onehot(sent_row(mate, slot) == lanes(ROWS))
        bring[...] = onehot(landed_row(mate, slot) == lanes(ROWS))
        ids = [piece[:, :ROWS].astype(F32) for piece in (ids_own, ids_near, ids_far, ids_both)]
        for x in range(RANKS):
            pack[x] = onehot(packed_row(scalars(metas[x], ROWS, ROUNDS), 1) == position(0))
            allowed = to_column(ids[x]) == ids[0]
            if x == 0:
                allowed = allowed & (position(0) <= lanes(ROWS))
            bias[pl.ds(pl.multiple_of((rank ^ x) * ROWS, ROWS), ROWS), :] = jnp.where(allowed, 0.0, MASKED)

    came = landed_row(scalars(mate_ref, 0, ROUNDS), scalars(metas[0], ROWS, ROUNDS)) >= 0
    g = jnp.where(came, pick(bring[...], landed_ref[...]), g_ref[...])
    count = key_blocks(metas, rank)
    total[...] = jnp.zeros_like(total)

    for n in range(1, RANKS + 1):

        @pl.when(count == n)
        def _(n=n):
            start = rank - (n - 1)
            window = pl.ds(pl.multiple_of(start * ROWS, ROWS), n * ROWS)
            k = pairs_ref[window, :HEAD_SIZE]
            v = pairs_ref[window, HEAD_SIZE:]
            mask = bias[window, :]
            inner_dims = (((1,), (1,)), ((), ()))
            lows, grads, queries, gradients = [], [], [], []
            for h in range(SHARED):
                columns = slice(h * HEAD_SIZE, (h + 1) * HEAD_SIZE)
                q_h, g_h = q_ref[:, columns], g[:, columns]
                logits = lax.dot_general(k, q_h, inner_dims, preferred_element_type=F32) + mask
                raised = jnp.exp2((logits - jnp.max(logits, axis=0, keepdims=True)) * EXP2_FACTOR)
                weights = raised * (1.0 / jnp.sum(raised, axis=0, keepdims=True))
                grad_weights = lax.dot_general(v, g_h, inner_dims, preferred_element_type=F32)
                inner = jnp.sum(weights * grad_weights, axis=0, keepdims=True)
                grad_logits = (weights * (grad_weights - inner)).astype(BF16)
                dq = lax.dot_general(grad_logits, k, (((0,), (0,)), ((), ())), preferred_element_type=F32)
                dq_ref[:, columns] = (dq * FACTOR).astype(BF16)
                lows.append(weights.astype(BF16))
                grads.append(grad_logits)
                queries.append(q_h)
                gradients.append(g_h)
            dk = jnp.dot(
                jnp.concatenate(grads, axis=1), jnp.concatenate(queries, axis=0), preferred_element_type=F32
            )
            dv = jnp.dot(
                jnp.concatenate(lows, axis=1), jnp.concatenate(gradients, axis=0), preferred_element_type=F32
            )
            total[window, :HEAD_SIZE] = (dk * FACTOR).astype(BF16)
            total[window, HEAD_SIZE:] = dv.astype(BF16)

    send_ref[:, :WIDE] = pick(choose[...], dq_ref[...])
    send_ref[:, WIDE:] = jnp.zeros((ROWS, PAIR), BF16)
    for x in range(RANKS):
        part = total[pl.ds(pl.multiple_of((rank ^ x) * ROWS, ROWS), ROWS), :]
        pieces = pick(pack[x], part)
        stay, turn = ((stay_keep, turn_keep), (stay_send, turn_send))[x & 1]
        stay[x >> 1] = pieces[:HALF]
        turn[x >> 1] = pieces[HALF:]


def backward(mate, metas, merged, g, landed, pairs):
    whole = lambda shape: pl.BlockSpec(shape, lambda h: (0,) * len(shape))
    wide = pl.BlockSpec((ROWS, WIDE), lambda h: (0, h))
    piece = pl.BlockSpec((2, HALF, PAIR), lambda h: (0, 0, h))
    piece_shape = jax.ShapeDtypeStruct((2, HALF, KEY_VALUE_HEADS * PAIR), BF16)
    return pl.pallas_call(
        backward_kernel,
        grid=(KEY_VALUE_HEADS,),
        in_specs=[SMEM] * 5 + [whole((1, META))] * 4
        + [wide, wide, wide, pl.BlockSpec((RANKS * ROWS, PAIR), lambda h: (0, h))],
        out_specs=[wide, pl.BlockSpec((ROWS, BUNDLE), lambda h: (0, h)), piece, piece, piece, piece],
        out_shape=[
            jax.ShapeDtypeStruct((ROWS, KEY_VALUE_HEADS * WIDE), BF16),
            jax.ShapeDtypeStruct((ROWS, KEY_VALUE_HEADS * BUNDLE), BF16),
            piece_shape,
            piece_shape,
            piece_shape,
            piece_shape,
        ],
        scratch_shapes=[
            pltpu.VMEM((ROWS, ROWS), BF16),
            pltpu.VMEM((ROWS, ROWS), BF16),
            pltpu.VMEM((RANKS, ROWS, ROWS), BF16),
            pltpu.VMEM((RANKS * ROWS, ROWS), F32),
            pltpu.VMEM((RANKS * ROWS, PAIR), BF16),
        ],
        compiler_params=PARAMS,
        cost_estimate=pl.CostEstimate(flops=8 * 10**9, bytes_accessed=10**7, transcendentals=4 * 10**6),
        name="backward",
    )(mate, *metas, *[meta.reshape(1, META) for meta in metas], merged, g, landed, pairs)


def returning_kernel(mate_ref, send_ref, own_ref, near_ref, far_ref, out_ref):
    total = own_ref[0].astype(F32) + near_ref[0].astype(F32) + far_ref[...].astype(F32)
    choose = onehot(sent_turn(scalars(mate_ref, 0, ROUNDS)) == lanes(HALF))
    out_ref[...] = pick(choose, total.astype(BF16))


def returning(mate, send, own, near, far):
    first = pl.BlockSpec((1, HALF, PAIR), lambda h: (0, 0, h))
    return pl.pallas_call(
        returning_kernel,
        grid=(KEY_VALUE_HEADS,),
        in_specs=[SMEM, pl.BlockSpec(memory_space=pl.ANY), first, first, pl.BlockSpec((HALF, PAIR), lambda h: (0, h))],
        out_specs=pl.BlockSpec((ROWS, PAIR), lambda h: (0, 3 * h + 2)),
        out_shape=jax.ShapeDtypeStruct(send.shape, BF16),
        input_output_aliases={1: 0},
        compiler_params=PARAMS,
        cost_estimate=pl.CostEstimate(flops=10**8, bytes_accessed=10**6, transcendentals=0),
        name="returning",
    )(mate, send, own, near, far)


def merge_kernel(mate_ref, slot_ref, own_ref, landed_ref, out_ref, bring):
    row = landed_row(scalars(mate_ref, 0, ROUNDS), scalars(slot_ref, 0, ROUNDS))

    @pl.when(pl.program_id(0) == 0)
    def _():
        bring[...] = onehot(row == lanes(ROWS))

    out_ref[...] = jnp.where(row >= 0, pick(bring[...], landed_ref[...]), own_ref[...])


def merge(mate, slot, own, landed):
    wide = pl.BlockSpec((ROWS, WIDE), lambda h: (0, h))
    return pl.pallas_call(
        merge_kernel,
        grid=(KEY_VALUE_HEADS,),
        in_specs=[SMEM, SMEM, wide, wide],
        out_specs=wide,
        out_shape=jax.ShapeDtypeStruct(own.shape, BF16),
        scratch_shapes=[pltpu.VMEM((ROWS, ROWS), BF16)],
        compiler_params=PARAMS,
        cost_estimate=pl.CostEstimate(flops=5 * 10**8, bytes_accessed=3 * 10**6, transcendentals=0),
        name="merge",
    )(mate, slot, own, landed)


def finish_kernel(
    mate_ref, slot_ref, dq_ref, landed_ref, own_ref, near_ref, far_ref, grad_q, grad_k, grad_v, bring, place
):
    row = landed_row(scalars(mate_ref, 0, ROUNDS), scalars(slot_ref, 0, ROUNDS))

    @pl.when(pl.program_id(0) == 0)
    def _():
        bring[...] = onehot(row == lanes(ROWS))
        place[...] = onehot(packed_row(scalars(slot_ref, 0, ROUNDS), 0) == lanes(HALF))

    total = own_ref[0].astype(F32) + near_ref[0].astype(F32) + far_ref[...].astype(F32)
    came = pick(bring[...], landed_ref[...])
    grad_q[...] = jnp.where(row >= 0, came[:, :WIDE], dq_ref[...])
    pairs = jnp.where(row >= 0, came[:, WIDE:], pick(place[...], total.astype(BF16)))
    grad_k[...] = pairs[:, :HEAD_SIZE]
    grad_v[...] = pairs[:, HEAD_SIZE:]


def finish(mate, slot, dq, landed, own, near, far):
    wide = pl.BlockSpec((ROWS, WIDE), lambda h: (0, h))
    head = pl.BlockSpec((ROWS, HEAD_SIZE), lambda h: (0, h))
    first = pl.BlockSpec((1, HALF, PAIR), lambda h: (0, 0, h))
    narrow = jax.ShapeDtypeStruct((ROWS, KEY_VALUE_HEADS * HEAD_SIZE), BF16)
    return pl.pallas_call(
        finish_kernel,
        grid=(KEY_VALUE_HEADS,),
        in_specs=[
            SMEM, SMEM, wide, pl.BlockSpec((ROWS, BUNDLE), lambda h: (0, h)),
            first, first, pl.BlockSpec((HALF, PAIR), lambda h: (0, h)),
        ],
        out_specs=[wide, head, head],
        out_shape=[jax.ShapeDtypeStruct(dq.shape, BF16), narrow, narrow],
        scratch_shapes=[pltpu.VMEM((ROWS, ROWS), BF16), pltpu.VMEM((ROWS, HALF), BF16)],
        compiler_params=PARAMS,
        cost_estimate=pl.CostEstimate(flops=8 * 10**8, bytes_accessed=5 * 10**6, transcendentals=0),
        name="finish",
    )(mate, slot, dq, landed, own, near, far)


def exchange(rows):
    blocks = rows.reshape(GROUPS, BLOCK, rows.shape[-1])
    return lax.all_to_all(blocks, "dp", split_axis=0, concat_axis=0, tiled=True).reshape(rows.shape)


def across(array):
    return lax.ppermute(array, "sp", [(i, i ^ 2) for i in range(RANKS)])


def beside(array):
    return lax.ppermute(array, "sp", [(i, i ^ 1) for i in range(RANKS)])


def spread(array):
    far = across(array)
    near = beside(jnp.stack([array, far]))
    return array, far, near


def collect(keep, send):
    near = beside(send)
    partial = (keep[1].astype(F32) + near[1].astype(F32)).astype(BF16)
    return keep, near, across(partial)


def body(queries, keys, values, cotangent, doc_ids, partners, swap_slots):
    q, k, v, g = queries[0], keys[0], values[0], cotangent[0]
    mate = partners.reshape(ROUNDS)
    slot = swap_slots.reshape(ROUNDS)
    rank = lax.axis_index("sp").astype(jnp.int32).reshape(1)
    meta = jnp.concatenate(
        [doc_ids.reshape(ROWS), slot, rank, jnp.zeros((META - ROWS - ROUNDS - 1,), jnp.int32)]
    )

    first, second, stay = outgoing(mate, slot, q, k, v, g)
    landed = exchange(first)
    meta_own, meta_far, meta_near = spread(meta)
    metas = (meta_own, meta_near[0], meta_far, meta_near[1])
    stays = spread(stay)
    landed, second = lax.optimization_barrier((landed, second))
    landed_g = exchange(second)
    turns = spread(traded_pairs(mate, landed))
    out, send, merged, pairs = forward(mate, metas, q, landed, stays, turns)
    landed_g, send = lax.optimization_barrier((landed_g, send))
    landed_out = exchange(send)
    dq, send, turn_keep, turn_send, stay_keep, stay_send = backward(mate, metas, merged, g, landed_g, pairs)
    send = returning(mate, send, *collect(turn_keep, turn_send))
    landed_out, send = lax.optimization_barrier((landed_out, send))
    landed = exchange(send)
    attended = merge(mate, slot, out, landed_out)
    grad_q, grad_k, grad_v = finish(mate, slot, dq, landed, *collect(stay_keep, stay_send))
    return attended[None], grad_q[None], grad_k[None], grad_v[None]


def solution(mesh):
    rows = P("dp", "sp", None)
    return jax.shard_map(
        body,
        mesh=mesh,
        in_specs=(rows, rows, rows, rows, P("dp", "sp"), P(None, "dp"), rows),
        out_specs=(rows, rows, rows, rows),
        check_vma=False,
    )
```

profile of v0, /device:TPU:1, one launch (start us, length us, event | category | flops | bytes accessed | tf_op | source)
XLA Modules:
  0.0 180.6 jit_solution(3979768389860794191)
XLA Ops:
  0.6 4.8 %outgoing.1 = (bf16[256,3072]{1,0:T(8,128)(2,1)}, bf16[256,2048]{1,0:T(8,128)(2,1)}, bf16[128,1024]{1,0:T(8,128)(2,1)}) custom-call(s32[16]{0:T(128)} %bitcast.41, s32[16]{0:T(128)} %bitcast.48, bf16[256,2048]{1,0:T(8,128)(2,1)} %bitcast.53, bf16[256,512]{1,0:T(8,128)(2,1)} %bitcast.58, bf16[256,512]{1,0:T(8,128)(2,1)} %bitcast.59, bf16[256,2048]{1,0:T(8,128)(2,1)} %bitcast.55), custom_call_target="tpu_custom_call" | custom-call | flops 1000000000 | bytes 5000000 | tf_op jit(solution)/shard_map/outgoing/pallas_call | solution.py:112
  5.4 9.4 %all-to-all-start = ((bf16[32,8,3072]{2,1,0:T(8,128)(2,1)}), bf16[32,8,3072]{2,1,0:T(8,128)(2,1)S(1)}, u32[]{:S(2)}, u32[]{:S(2)}) async-start(bf16[32,8,3072]{2,1,0:T(8,128)(2,1)} %bitcast.33), calls=%async_computation | async-start | bytes 3145728 | tf_op jit(solution)/shard_map/all_to_all | solution.py:459
  14.8 3.4 %collective-permute-start.2 = (bf16[128,1024]{1,0:T(8,128)(2,1)S(1)}, bf16[128,1024]{1,0:T(8,128)(2,1)S(1)}, u32[]{:S(2)}, u32[]{:S(2)}) collective-permute-start(bf16[128,1024]{1,0:T(8,128)(2,1)S(1)} %copy-done.11), channel_id=1, source_target_pairs={{0,2},{1,3},{2,0},{3,1},{4,6},{5,7},{6,4},{7,5},{8,10},{9,11},{10,... | collective-permute-start | bytes 786440 | tf_op jit(solution)/shard_map/ppermute | solution.py:463
  18.2 18.9 %all-to-all-done = bf16[32,8,3072]{2,1,0:T(8,128)(2,1)S(1)} async-done(((bf16[32,8,3072]{2,1,0:T(8,128)(2,1)}), bf16[32,8,3072]{2,1,0:T(8,128)(2,1)S(1)}, u32[]{:S(2)}, u32[]{:S(2)}) %all-to-all-start) | async-done | bytes 1572896 | tf_op jit(solution)/shard_map/all_to_all | solution.py:459
  37.1 1.1 copy-done
  38.3 3.6 %traded_pairs.1.turn_own = bf16[128,1024]{1,0:T(8,128)(2,1)} custom-call(s32[16]{0:T(128)} %bitcast.42, bf16[256,3072]{1,0:T(8,128)(2,1)} %bitcast.28), custom_call_target="tpu_custom_call" | custom-call | flops 100000000 | bytes 800000 | tf_op jit(solution)/shard_map/traded_pairs/pallas_call | solution.py:149
  41.8 3.3 %collective-permute-start.4 = (bf16[128,1024]{1,0:T(8,128)(2,1)}, bf16[128,1024]{1,0:T(8,128)(2,1)S(1)}, u32[]{:S(2)}, u32[]{:S(2)}) collective-permute-start(bf16[128,1024]{1,0:T(8,128)(2,1)} %traded_pairs.1.turn_own), channel_id=1, source_target_pairs={{0,2},{1,3},{2,0},{3,1},{4,6},{5,7},{6,4},{7,5},{8,10},{9,11},{10,... | collective-permute-start | bytes 786440 | tf_op jit(solution)/shard_map/ppermute | solution.py:463
  45.1 0.0 collective-permute-done.2.stay_far
  45.1 0.1 pad_maximum_fusion
  45.2 2.6 %collective-permute-start.3 = (bf16[2,128,1024]{2,1,0:T(8,128)(2,1)S(1)}, bf16[2,128,1024]{2,1,0:T(8,128)(2,1)}, u32[]{:S(2)}, u32[]{:S(2)}) collective-permute-start(bf16[2,128,1024]{2,1,0:T(8,128)(2,1)S(1)} %pad_maximum_fusion), channel_id=1, source_target_pairs={{0,1},{1,0},{2,3},{3,2},{4,5},{5,4},{6,7},{7,6},{8,9},{9,8},{10,11... | collective-permute-start | bytes 1572872 | tf_op jit(solution)/shard_map/ppermute | solution.py:467
  47.8 4.1 %all-to-all-start.1 = ((bf16[32,8,2048]{2,1,0:T(8,128)(2,1)}), bf16[32,8,2048]{2,1,0:T(8,128)(2,1)S(1)}, u32[]{:S(2)}, u32[]{:S(2)}) async-start(bf16[32,8,2048]{2,1,0:T(8,128)(2,1)} %bitcast.14), calls=%async_computation.1 | async-start | bytes 2097152 | tf_op jit(solution)/shard_map/all_to_all | solution.py:459
  51.9 0.0 collective-permute-done.4.turn_far
  51.9 0.1 pad_maximum_fusion.1
  51.9 0.8 collective-permute-start.5
  52.8 0.1 pad_add_fusion.1.meta_own
  52.8 3.0 %collective-permute-start = (s32[384]{0:T(512)S(1)}, s32[384]{0:T(512)S(1)}, u32[]{:S(2)}, u32[]{:S(2)}) collective-permute-start(s32[384]{0:T(512)S(1)} %pad_add_fusion.1.meta_own), channel_id=1, source_target_pairs={{0,2},{1,3},{2,0},{3,1},{4,6},{5,7},{6,4},{7,5},{8,10},{9,11},{10,... | collective-permute-start | bytes 4616 | tf_op jit(solution)/shard_map/ppermute | solution.py:463
  55.8 1.2 collective-permute-done.meta_far
  57.0 1.4 collective-permute-start.1
  58.4 0.8 collective-permute-done.1
  59.2 1.2 slice_reduce_fusion
  60.4 0.0 collective-permute-done.3.stay_near
  60.4 0.0 collective-permute-done.5.turn_near
  60.5 14.9 %forward.1 = (bf16[256,2048]{1,0:T(8,128)(2,1)}, bf16[256,2048]{1,0:T(8,128)(2,1)}, bf16[256,2048]{1,0:T(8,128)(2,1)}, bf16[1024,1024]{1,0:T(8,128)(2,1)}) custom-call(s32[16]{0:T(128)} %bitcast.43, s32[384]{0:T(512)} %copy-done.14, s32[384]{0:T(512)} %get-tuple-element.49.meta_near, s32[384]{0:T(512)} %copy-done.18, s32[384]{0:T(512)} %get-tuple-element.48.meta_both, ...), custom_call_target="tpu_custom_call" | custom-call | flops 4000000000 | bytes 10000000 | tf_op jit(solution)/shard_map/forward/pallas_call | solution.py:237
  75.4 0.0 all-to-all-done.1
  75.4 0.0 copy-start.7
  75.4 1.0 copy-done.7
  76.4 18.2 %backward.1 = (bf16[256,2048]{1,0:T(8,128)(2,1)}, bf16[256,3072]{1,0:T(8,128)(2,1)}, bf16[2,128,1024]{2,1,0:T(8,128)(2,1)}, bf16[2,128,1024]{2,1,0:T(8,128)(2,1)...) custom-call(s32[16]{0:T(128)} %bitcast.44, s32[384]{0:T(512)} %copy-done.14, ...), custom_call_target="tpu_custom_call" | custom-call | flops 8000000000 | bytes 10000000 | tf_op jit(solution)/shard_map/backward/pallas_call | solution.py:345
  94.6 0.1 collective-permute-start.6
  94.7 13.4 %all-to-all-start.2 = ((bf16[32,8,2048]{2,1,0:T(8,128)(2,1)}), bf16[32,8,2048]{2,1,0:T(8,128)(2,1)S(1)}, u32[]{:S(2)}, u32[]{:S(2)}) async-start(bf16[32,8,2048]{2,1,0:T(8,128)(2,1)} %bitcast.35), calls=%async_computation.2 | async-start | bytes 2097152 | tf_op jit(solution)/shard_map/all_to_all | solution.py:459
  108.1 0.0 copy-start.6
  108.1 0.1 fusion
  108.2 11.1 %collective-permute-start.7 = (bf16[128,1024]{1,0:T(8,128)(2,1)S(1)}, bf16[128,1024]{1,0:T(8,128)(2,1)S(1)}, u32[]{:S(2)}, u32[]{:S(2)}) collective-permute-start(bf16[128,1024]{1,0:T(8,128)(2,1)S(1)} %fusion), channel_id=1, source_target_pairs={{0,2},{1,3},{2,0},{3,1},{4,6},{5,7},{6,4},{7,5},{8,10},{9,11},{10,... | collective-permute-start | bytes 786440 | tf_op jit(solution)/shard_map/ppermute | solution.py:463
  119.3 17.1 %collective-permute-done.7.far_ref = bf16[128,1024]{1,0:T(8,128)(2,1)S(1)} collective-permute-done((bf16[128,1024]{1,0:T(8,128)(2,1)S(1)}, bf16[128,1024]{1,0:T(8,128)(2,1)S(1)}, u32[]{:S(2)}, u32[]{:S(2)}) %collective-permute-start.7) | collective-permute-done | bytes 262176 | tf_op jit(solution)/shard_map/ppermute | solution.py:463
  136.4 0.7 copy-done.10
  137.1 3.8 %returning.1 = bf16[256,3072]{1,0:T(8,128)(2,1)} custom-call(s32[16]{0:T(128)} %bitcast.45, bf16[256,3072]{1,0:T(8,128)(2,1)} %get-tuple-element.37.send_ref, bf16[2,128,1024]{2,1,0:T(8,128)(2,1)} %get-tuple-element.38.own_ref, bf16[2,128,1024]{2,1,0:T(8,128)(2,1)} %copy-done.6, bf16[128,1024]{1,0:T(8,128)(2,1)} %copy-done.10), custom_call_target="tpu_custom_call", output_to_operand_aliasing={{}: (1, {})} | custom-call | flops 100000000 | bytes 1000000 | tf_op jit(solution)/shard_map/returning/pallas_call | solution.py:380
  140.9 0.0 all-to-all-done.2
  140.9 1.0 copy-done.2
  141.9 7.9 %all-to-all-start.3 = ((bf16[32,8,3072]{2,1,0:T(8,128)(2,1)}), bf16[32,8,3072]{2,1,0:T(8,128)(2,1)S(1)}, u32[]{:S(2)}, u32[]{:S(2)}) async-start(bf16[32,8,3072]{2,1,0:T(8,128)(2,1)} %bitcast.30), calls=%async_computation.3 | async-start | bytes 3145728 | tf_op jit(solution)/shard_map/all_to_all | solution.py:459
  149.8 0.9 collective-permute-start.8
  150.6 1.7 collective-permute-done.8.near_ref
  152.4 0.1 fusion.1
  152.4 0.1 collective-permute-start.9
  152.5 4.4 %merge.1 = bf16[256,2048]{1,0:T(8,128)(2,1)} custom-call(s32[16]{0:T(128)} %bitcast.46, s32[16]{0:T(128)} %bitcast.49, bf16[256,2048]{1,0:T(8,128)(2,1)} %get-tuple-element.30.own_ref, bf16[256,2048]{1,0:T(8,128)(2,1)} %bitcast.32), custom_call_target="tpu_custom_call" | custom-call | flops 500000000 | bytes 3000000 | tf_op jit(solution)/shard_map/merge/pallas_call | solution.py:405
  156.9 17.4 %collective-permute-done.9.far_ref = bf16[128,1024]{1,0:T(8,128)(2,1)S(1)} collective-permute-done((bf16[128,1024]{1,0:T(8,128)(2,1)S(1)}, bf16[128,1024]{1,0:T(8,128)(2,1)S(1)}, u32[]{:S(2)}, u32[]{:S(2)}) %collective-permute-start.9) | collective-permute-done | bytes 262176 | tf_op jit(solution)/shard_map/ppermute | solution.py:463
  174.3 0.0 all-to-all-done.3
  174.3 0.7 copy-done.9
  175.0 0.6 copy-done.1
  175.6 5.0 %finish.1 = (bf16[256,2048]{1,0:T(8,128)(2,1)}, bf16[256,512]{1,0:T(8,128)(2,1)}, bf16[256,512]{1,0:T(8,128)(2,1)}) custom-call(s32[16]{0:T(128)} %bitcast.47, s32[16]{0:T(128)} %bitcast.50, bf16[256,2048]{1,0:T(8,128)(2,1)} %get-tuple-element.41.dq_ref, bf16[256,3072]{1,0:T(8,128)(2,1)} %bitcast.31, bf16[2,128,1024]{2,1,0:T(8,128)(2,1)} %get-tuple-element.43.own_ref, ...), custom_call_target="tpu_custom_call" | custom-call | flops 800000000 | bytes 5000000 | tf_op jit(solution)/shard_map/finish/pallas_call | solution.py:441
  (37 shorter events, 0.1 us)
Async XLA Ops:
  5.4 9.4 %copy-start.11 = (bf16[128,1024]{1,0:T(8,128)(2,1)S(1)}, bf16[128,1024]{1,0:T(8,128)(2,1)}, u32[]{:S(2)}) copy-start(bf16[128,1024]{1,0:T(8,128)(2,1)} %get-tuple-element.29.stay_own) | copy-start | bytes 786436
  5.4 31.7 %all-to-all-start = ((bf16[32,8,3072]{2,1,0:T(8,128)(2,1)}), bf16[32,8,3072]{2,1,0:T(8,128)(2,1)S(1)}, u32[]{:S(2)}, u32[]{:S(2)}) async-start(bf16[32,8,3072]{2,1,0:T(8,128)(2,1)} %bitcast.33), calls=%async_computation | async-start | bytes 3145728 | tf_op jit(solution)/shard_map/all_to_all | solution.py:459
  14.8 30.3 %collective-permute-start.2 = (bf16[128,1024]{1,0:T(8,128)(2,1)S(1)}, bf16[128,1024]{1,0:T(8,128)(2,1)S(1)}, u32[]{:S(2)}, u32[]{:S(2)}) collective-permute-start(bf16[128,1024]{1,0:T(8,128)(2,1)S(1)} %copy-done.11), channel_id=1, source_target_pairs={{0,2},{1,3},{2,0},{3,1},{4,6},{5,7},{6,4},{7,5},{8,10},{9,11},{10,... | collective-permute-start | bytes 786440 | tf_op jit(solution)/shard_map/ppermute | solution.py:463
  37.1 1.1 copy-start
  41.8 10.0 %collective-permute-start.4 = (bf16[128,1024]{1,0:T(8,128)(2,1)}, bf16[128,1024]{1,0:T(8,128)(2,1)S(1)}, u32[]{:S(2)}, u32[]{:S(2)}) collective-permute-start(bf16[128,1024]{1,0:T(8,128)(2,1)} %traded_pairs.1.turn_own), channel_id=1, source_target_pairs={{0,2},{1,3},{2,0},{3,1},{4,6},{5,7},{6,4},{7,5},{8,10},{9,11},{10,... | collective-permute-start | bytes 786440 | tf_op jit(solution)/shard_map/ppermute | solution.py:463
  45.1 2.6 %copy-start.12 = (bf16[128,1024]{1,0:T(8,128)(2,1)}, bf16[128,1024]{1,0:T(8,128)(2,1)S(1)}, u32[]{:S(2)}) copy-start(bf16[128,1024]{1,0:T(8,128)(2,1)S(1)} %collective-permute-done.2.stay_far) | copy-start | bytes 786436
  45.1 6.7 %copy-start.8 = (bf16[128,1024]{1,0:T(8,128)(2,1)S(1)}, bf16[128,1024]{1,0:T(8,128)(2,1)}, u32[]{:S(2)}) copy-start(bf16[128,1024]{1,0:T(8,128)(2,1)} %traded_pairs.1.turn_own) | copy-start | bytes 786436
  45.2 15.2 %collective-permute-start.3 = (bf16[2,128,1024]{2,1,0:T(8,128)(2,1)S(1)}, bf16[2,128,1024]{2,1,0:T(8,128)(2,1)}, u32[]{:S(2)}, u32[]{:S(2)}) collective-permute-start(bf16[2,128,1024]{2,1,0:T(8,128)(2,1)S(1)} %pad_maximum_fusion), channel_id=1, source_target_pairs={{0,1},{1,0},{2,3},{3,2},{4,5},{5,4},{6,7},{7,6},{8,9},{9,8},{10,11... | collective-permute-start | bytes 1572872 | tf_op jit(solution)/shard_map/ppermute | solution.py:467
  47.8 5.0 %copy-start.17 = (s32[1,1,16]{2,1,0:T(1,128)S(1)}, s32[1,1,16]{2,1,0:T(1,128)}, u32[]{:S(2)}) copy-start(s32[1,1,16]{2,1,0:T(1,128)} %param.13) | copy-start | bytes 196
  47.8 5.0 %copy-start.19 = (s32[1,256]{1,0:T(1,128)S(1)}, s32[1,256]{1,0:T(1,128)}, u32[]{:S(2)}) copy-start(s32[1,256]{1,0:T(1,128)} %param.11) | copy-start | bytes 3076
  47.8 27.6 %all-to-all-start.1 = ((bf16[32,8,2048]{2,1,0:T(8,128)(2,1)}), bf16[32,8,2048]{2,1,0:T(8,128)(2,1)S(1)}, u32[]{:S(2)}, u32[]{:S(2)}) async-start(bf16[32,8,2048]{2,1,0:T(8,128)(2,1)} %bitcast.14), calls=%async_computation.1 | async-start | bytes 2097152 | tf_op jit(solution)/shard_map/all_to_all | solution.py:459
  51.9 8.6 %copy-start.13 = (bf16[128,1024]{1,0:T(8,128)(2,1)}, bf16[128,1024]{1,0:T(8,128)(2,1)S(1)}, u32[]{:S(2)}) copy-start(bf16[128,1024]{1,0:T(8,128)(2,1)S(1)} %collective-permute-done.4.turn_far) | copy-start | bytes 786436
  51.9 8.5 %collective-permute-start.5 = (bf16[2,128,1024]{2,1,0:T(8,128)(2,1)S(1)}, bf16[2,128,1024]{2,1,0:T(8,128)(2,1)}, u32[]{:S(2)}, u32[]{:S(2)}) collective-permute-start(bf16[2,128,1024]{2,1,0:T(8,128)(2,1)S(1)} %pad_maximum_fusion.1), channel_id=1, source_target_pairs={{0,1},{1,0},{2,3},{3,2},{4,5},{5,4},{6,7},{7,6},{8,9},{9,8},{10,11... | collective-permute-start | bytes 1572872 | tf_op jit(solution)/shard_map/ppermute | solution.py:467
  52.8 7.6 %copy-start.14 = (s32[384]{0:T(512)}, s32[384]{0:T(512)S(1)}, u32[]{:S(2)}) copy-start(s32[384]{0:T(512)S(1)} %pad_add_fusion.1.meta_own) | copy-start | bytes 4612
  52.8 4.2 %collective-permute-start = (s32[384]{0:T(512)S(1)}, s32[384]{0:T(512)S(1)}, u32[]{:S(2)}, u32[]{:S(2)}) collective-permute-start(s32[384]{0:T(512)S(1)} %pad_add_fusion.1.meta_own), channel_id=1, source_target_pairs={{0,2},{1,3},{2,0},{3,1},{4,6},{5,7},{6,4},{7,5},{8,10},{9,11},{10,... | collective-permute-start | bytes 4616 | tf_op jit(solution)/shard_map/ppermute | solution.py:463
  55.8 4.6 %copy-start.15 = (s32[1,384]{1,0:T(1,128)}, s32[1,384]{1,0:T(1,128)S(1)}, u32[]{:S(2)}) copy-start(s32[1,384]{1,0:T(1,128)S(1)} %stack.27.ids_own) | copy-start | bytes 4612
  57.0 3.5 %copy-start.18 = (s32[384]{0:T(512)}, s32[384]{0:T(512)S(1)}, u32[]{:S(2)}) copy-start(s32[384]{0:T(512)S(1)} %collective-permute-done.meta_far) | copy-start | bytes 4612
  57.0 3.5 %copy-start.16 = (s32[1,384]{1,0:T(1,128)}, s32[1,384]{1,0:T(1,128)S(1)}, u32[]{:S(2)}) copy-start(s32[1,384]{1,0:T(1,128)S(1)} %stack.28.ids_far) | copy-start | bytes 4612
  57.0 2.2 %collective-permute-start.1 = (s32[2,384]{1,0:T(2,128)S(1)}, s32[2,384]{1,0:T(2,128)S(1)}, u32[]{:S(2)}, u32[]{:S(2)}) collective-permute-start(s32[2,384]{1,0:T(2,128)S(1)} %pad_add_fusion), channel_id=1, source_target_pairs={{0,1},{1,0},{2,3},{3,2},{4,5},{5,4},{6,7},{7,6},{8,9},{9,8},{10,11... | collective-permute-start | bytes 9224 | tf_op jit(solution)/shard_map/ppermute | solution.py:467
  75.4 1.0 copy-start.7
  94.6 13.5 %copy-start.4 = (bf16[2,128,1024]{2,1,0:T(8,128)(2,1)S(1)}, bf16[2,128,1024]{2,1,0:T(8,128)(2,1)}, u32[]{:S(2)}) copy-start(bf16[2,128,1024]{2,1,0:T(8,128)(2,1)} %get-tuple-element.38.own_ref) | copy-start | bytes 1572868
  94.6 13.5 %collective-permute-start.6 = (bf16[2,128,1024]{2,1,0:T(8,128)(2,1)}, bf16[2,128,1024]{2,1,0:T(8,128)(2,1)S(1)}, u32[]{:S(2)}, u32[]{:S(2)}) collective-permute-start(bf16[2,128,1024]{2,1,0:T(8,128)(2,1)} %get-tuple-element.39), channel_id=1, source_target_pairs={{0,1},{1,0},{2,3},{3,2},{4,5},{5,4},{6,7},{7,6},{8,9},{9,8},{10,11... | collective-permute-start | bytes 1572872 | tf_op jit(solution)/shard_map/ppermute | solution.py:467
  94.7 46.2 %all-to-all-start.2 = ((bf16[32,8,2048]{2,1,0:T(8,128)(2,1)}), bf16[32,8,2048]{2,1,0:T(8,128)(2,1)S(1)}, u32[]{:S(2)}, u32[]{:S(2)}) async-start(bf16[32,8,2048]{2,1,0:T(8,128)(2,1)} %bitcast.35), calls=%async_computation.2 | async-start | bytes 2097152 | tf_op jit(solution)/shard_map/all_to_all | solution.py:459
  108.1 28.3 %copy-start.6 = (bf16[2,128,1024]{2,1,0:T(8,128)(2,1)}, bf16[2,128,1024]{2,1,0:T(8,128)(2,1)S(1)}, u32[]{:S(2)}) copy-start(bf16[2,128,1024]{2,1,0:T(8,128)(2,1)S(1)} %collective-permute-done.6.near_ref) | copy-start | bytes 1572868
  108.2 28.2 %collective-permute-start.7 = (bf16[128,1024]{1,0:T(8,128)(2,1)S(1)}, bf16[128,1024]{1,0:T(8,128)(2,1)S(1)}, u32[]{:S(2)}, u32[]{:S(2)}) collective-permute-start(bf16[128,1024]{1,0:T(8,128)(2,1)S(1)} %fusion), channel_id=1, source_target_pairs={{0,2},{1,3},{2,0},{3,1},{4,6},{5,7},{6,4},{7,5},{8,10},{9,11},{10,... | collective-permute-start | bytes 786440 | tf_op jit(solution)/shard_map/ppermute | solution.py:463
  136.4 0.7 copy-start.10
  140.9 1.0 copy-start.2
  140.9 11.5 %copy-start.3 = (bf16[2,128,1024]{2,1,0:T(8,128)(2,1)S(1)}, bf16[2,128,1024]{2,1,0:T(8,128)(2,1)}, u32[]{:S(2)}) copy-start(bf16[2,128,1024]{2,1,0:T(8,128)(2,1)} %get-tuple-element.43.own_ref) | copy-start | bytes 1572868
  141.9 32.4 %all-to-all-start.3 = ((bf16[32,8,3072]{2,1,0:T(8,128)(2,1)}), bf16[32,8,3072]{2,1,0:T(8,128)(2,1)S(1)}, u32[]{:S(2)}, u32[]{:S(2)}) async-start(bf16[32,8,3072]{2,1,0:T(8,128)(2,1)} %bitcast.30), calls=%async_computation.3 | async-start | bytes 3145728 | tf_op jit(solution)/shard_map/all_to_all | solution.py:459
  149.8 2.6 %collective-permute-start.8 = (bf16[2,128,1024]{2,1,0:T(8,128)(2,1)}, bf16[2,128,1024]{2,1,0:T(8,128)(2,1)S(1)}, u32[]{:S(2)}, u32[]{:S(2)}) collective-permute-start(bf16[2,128,1024]{2,1,0:T(8,128)(2,1)} %get-tuple-element.44), channel_id=1, source_target_pairs={{0,1},{1,0},{2,3},{3,2},{4,5},{5,4},{6,7},{7,6},{8,9},{9,8},{10,11... | collective-permute-start | bytes 1572872 | tf_op jit(solution)/shard_map/ppermute | solution.py:467
  152.4 4.6 %copy-start.5 = (bf16[2,128,1024]{2,1,0:T(8,128)(2,1)}, bf16[2,128,1024]{2,1,0:T(8,128)(2,1)S(1)}, u32[]{:S(2)}) copy-start(bf16[2,128,1024]{2,1,0:T(8,128)(2,1)S(1)} %collective-permute-done.8.near_ref) | copy-start | bytes 1572868
  152.4 21.9 %collective-permute-start.9 = (bf16[128,1024]{1,0:T(8,128)(2,1)S(1)}, bf16[128,1024]{1,0:T(8,128)(2,1)S(1)}, u32[]{:S(2)}, u32[]{:S(2)}) collective-permute-start(bf16[128,1024]{1,0:T(8,128)(2,1)S(1)} %fusion.1), channel_id=1, source_target_pairs={{0,2},{1,3},{2,0},{3,1},{4,6},{5,7},{6,4},{7,5},{8,10},{9,11},{10,... | collective-permute-start | bytes 786440 | tf_op jit(solution)/shard_map/ppermute | solution.py:463
  174.3 0.7 copy-start.9
  174.3 1.3 copy-start.1
where the time goes:
time: 183 us; the launch traced here: 181 us
  starting transfers between devices  61.3 us (33%)
  waiting for transfers between devices  57.2 us (31%)
  Pallas kernels  54.6 us (30%)
  local copies, waits for them, and re-layouts  6.28 us (3%)
    ppermute x5, waiting for transfers between devices, across(): return lax.ppermute(array, 'sp', [(i, i ^ 2) for i in range(RANKS)])  35.7 us
    all_to_all x4, starting transfers between devices, exchange(): lax.all_to_all(blocks, 'dp', split_axis=0, concat_axis=0, tiled=True)  34.7 us
    ppermute x5, starting transfers between devices, across(): return lax.ppermute(array, 'sp', [(i, i ^ 2) for i in range(RANKS)])  20.9 us
    all_to_all x4, waiting for transfers between devices, exchange(): lax.all_to_all(blocks, 'dp', split_axis=0, concat_axis=0, tiled=True)  18.9 us
    pallas_call x1, Pallas kernels, backward(): pl.pallas_call(backward_kernel, grid=(KEY_VALUE_HEADS,), in_specs=[SMEM]...  18.2 us
    pallas_call x1, Pallas kernels, forward(): pl.pallas_call(forward_kernel, grid=(KEY_VALUE_HEADS,), in_specs=[SMEM] *...  14.9 us
    ppermute x5, starting transfers between devices, beside(): return lax.ppermute(array, 'sp', [(i, i ^ 1) for i in range(RANKS)])  5.71 us
    unnamed x40, local copies, waits for them, and re-layouts  5.07 us
  transfers between devices with their start and end apart: 14, of which 6 were waited for; matrix products, arithmetic and copies ran while one was open for 1% of the time, Pallas kernels for 15%

commit v1 on v0

v1 whole, which is shorter than its diff:
```python
import jax
import jax.numpy as jnp
from jax import lax
from jax.experimental import pallas as pl
from jax.experimental.pallas import tpu as pltpu
from jax.sharding import PartitionSpec as P

KEY_VALUE_HEADS = 4
SHARED = 4
HEAD_SIZE = 128
BLOCK = 8
ROUNDS = 16
ROWS = 256
HALF = ROUNDS * BLOCK
GROUPS = 32
RANKS = 4
WIDE = SHARED * HEAD_SIZE
PAIR = 2 * HEAD_SIZE
BUNDLE = WIDE + PAIR
CARGO = 2 * WIDE + PAIR
META = 384
KEYS = 128
EARLIER = (RANKS - 1) * ROWS // KEYS
FACTOR = HEAD_SIZE ** (-0.5)
EXP2_FACTOR = FACTOR * 1.4426950408889634
MASKED = -1e30
BF16 = jnp.bfloat16
F32 = jnp.float32

SMEM = pl.BlockSpec(memory_space=pltpu.SMEM)
VMEM = pl.BlockSpec(memory_space=pltpu.VMEM)
HBM = pl.BlockSpec(memory_space=pl.ANY)
PARAMS = pltpu.CompilerParams(vmem_limit_bytes=24 * 1024 * 1024)


def in_hbm(array):
    return pltpu.with_memory_space_constraint(array, pltpu.HBM)


def in_vmem(array):
    return pltpu.with_memory_space_constraint(array, pltpu.VMEM)


def iota(shape, axis):
    return lax.broadcasted_iota(jnp.int32, shape, axis)


def onehot(hit):
    return jnp.where(hit, 1.0, 0.0).astype(BF16)


def pick(matrix, rows):
    return jnp.dot(matrix, rows, preferred_element_type=F32).astype(BF16)


def part(h, first, width, whole):
    return pl.ds(pl.multiple_of(h * whole + first, HEAD_SIZE), width)


def lanes(width):
    return iota((1, width), 1)


def matching(value, keys, results):
    found = jnp.full_like(value, -1)
    for key, result in zip(keys, results):
        found = jnp.where(value == key, result, found)
    return found


def rows_at(block, place):
    return jnp.where(block >= 0, block * BLOCK + (place & 7), -1)


def placing(target, count):
    return onehot(target == iota((count, target.shape[1]), 0))


def choose_sent(mate, slot):
    place = lanes(ROWS)
    return placing(rows_at(matching(place >> 3, slot, mate), place), ROWS)


def choose_landed(mate, slot):
    place = lanes(ROWS)
    return placing(rows_at(matching(place >> 3, mate, slot), place), ROWS)


def choose_turns(mate):
    place = lanes(ROWS)
    return placing(rows_at(matching(place >> 3, mate, range(ROUNDS)), place), HALF)


def choose_sent_turns(mate):
    place = lanes(HALF)
    return placing(rows_at(matching(place >> 3, range(ROUNDS), mate), place), ROWS)


def packed_row(slot):
    place = lanes(ROWS)
    block = place >> 3
    turn = matching(block, slot, range(ROUNDS))
    lower = jnp.zeros_like(place)
    for t in range(ROUNDS):
        lower = lower + jnp.where(block > slot[t], 1, 0)
    return jnp.where(turn >= 0, HALF + turn * BLOCK, (block - lower) * BLOCK) + (place & 7)


def packing(slot, count=ROWS):
    return placing(packed_row(slot), count)


def unpacking(slot):
    hit = jnp.where(packed_row(slot) == iota((ROWS, ROWS), 0), 1.0, 0.0)
    return hit.T.astype(BF16)


def share_landed(matrix):
    return jnp.broadcast_to(jnp.sum(matrix.astype(F32), axis=1, keepdims=True), (ROWS, HEAD_SIZE))


def replaced(came, landed, own):
    mask = jnp.concatenate([came] * (own.shape[1] // HEAD_SIZE), axis=1)
    return jnp.where(mask > 0.5, landed, own.astype(F32)).astype(BF16)


def scalars(ref, first, count):
    return [ref[first + t] for t in range(count)]


def outgoing_kernel(mate_ref, slot_ref, q_ref, k_ref, v_ref, g_ref, send_ref, stay_ref, choose, keep):
    @pl.when(pl.program_id(0) == 0)
    def _():
        mate, slot = scalars(mate_ref, 0, ROUNDS), scalars(slot_ref, 0, ROUNDS)
        choose[...] = choose_sent(mate, slot)
        keep[...] = packing(slot, HALF)

    pairs = jnp.concatenate([k_ref[...], v_ref[...]], axis=1)
    send_ref[...] = pick(choose[...], jnp.concatenate([q_ref[...], pairs, g_ref[...]], axis=1))
    stay_ref[...] = pick(keep[...], pairs)


def outgoing(mate, slot, q, k, v, g):
    return pl.pallas_call(
        outgoing_kernel,
        grid=(KEY_VALUE_HEADS,),
        in_specs=[
            SMEM,
            SMEM,
            pl.BlockSpec((ROWS, WIDE), lambda h: (0, h)),
            pl.BlockSpec((ROWS, HEAD_SIZE), lambda h: (0, h)),
            pl.BlockSpec((ROWS, HEAD_SIZE), lambda h: (0, h)),
            pl.BlockSpec((ROWS, WIDE), lambda h: (0, h)),
        ],
        out_specs=[
            pl.BlockSpec((ROWS, CARGO), lambda h: (0, h)),
            pl.BlockSpec((HALF, PAIR), lambda h: (0, h)),
        ],
        out_shape=[
            pltpu.HBM((ROWS, KEY_VALUE_HEADS * CARGO), BF16),
            pltpu.VMEM((HALF, KEY_VALUE_HEADS * PAIR), BF16),
        ],
        scratch_shapes=[pltpu.VMEM((ROWS, ROWS), BF16), pltpu.VMEM((HALF, ROWS), BF16)],
        compiler_params=PARAMS,
        cost_estimate=pl.CostEstimate(flops=10**9, bytes_accessed=5 * 10**6, transcendentals=0),
        name="outgoing",
    )(mate, slot, in_hbm(q), in_hbm(k), in_hbm(v), in_hbm(g))


def traded_pairs_kernel(mate_ref, landed_ref, out_ref):
    choose = choose_turns(scalars(mate_ref, 0, ROUNDS))
    for h in range(KEY_VALUE_HEADS):
        out_ref[:, part(h, 0, PAIR, PAIR)] = pick(choose, landed_ref[:, part(h, WIDE, PAIR, CARGO)])


def traded_pairs(mate, landed):
    return pl.pallas_call(
        traded_pairs_kernel,
        in_specs=[SMEM, VMEM],
        out_specs=VMEM,
        out_shape=pltpu.VMEM((HALF, KEY_VALUE_HEADS * PAIR), BF16),
        compiler_params=PARAMS,
        cost_estimate=pl.CostEstimate(flops=10**8, bytes_accessed=8 * 10**5, transcendentals=0),
        name="traded_pairs",
    )(mate, in_vmem(landed))


def to_column(row):
    here = iota((ROWS, ROWS), 0) == iota((ROWS, ROWS), 1)
    return jnp.sum(jnp.where(here, row, 0.0), axis=1, keepdims=True)


def earlier_blocks(metas, rank):
    first = metas[0][0]
    count = jnp.int32(0)
    for x in (1, 2, 3):
        for last in range(KEYS - 1, ROWS, KEYS):
            count = count + jnp.where(((rank ^ x) < rank) & (metas[x][last] == first), 1, 0)
    return count


def fill_mask(mask, metas_ids, rank):
    ids = [piece[:, :ROWS].astype(F32) for piece in metas_ids]
    for x in range(RANKS):
        allowed = to_column(ids[x]) == ids[0]
        if x == 0:
            allowed = allowed & (iota((ROWS, 1), 0) <= lanes(ROWS))
        mask[pl.ds(pl.multiple_of((rank ^ x) * ROWS, ROWS), ROWS), :] = jnp.where(allowed, 0.0, MASKED)


INNER = (((1,), (1,)), ((), ()))


def forward_kernel(
    mate_ref, meta_own, meta_near, meta_far, meta_both, ids_own, ids_near, ids_far, ids_both,
    q_hbm, g_hbm, landed_ref, stay_own, stay_near, stay_far, stay_both, turn_own, turn_near, turn_far, turn_both,
    out_hbm, send_hbm, q_kept, g_kept, pairs_kept, stats_hbm,
    out_ref, send_ref, q_ref, g_ref, pairs_ref, stats_ref, bring, place, mask, came, q_arrived, g_arrived, left,
):
    q_copy = pltpu.make_async_copy(q_hbm, q_ref, q_arrived)
    g_copy = pltpu.make_async_copy(g_hbm, g_ref, g_arrived)
    q_copy.start()
    g_copy.start()
    metas = (meta_own, meta_near, meta_far, meta_both)
    rank = metas[0][ROWS + ROUNDS]
    count = earlier_blocks(metas, rank)
    mate, slot = scalars(mate_ref, 0, ROUNDS), scalars(metas[0], ROWS, ROUNDS)
    choose = choose_sent(mate, slot)
    bring[...] = choose_landed(mate, slot)
    came[...] = share_landed(bring[...])
    fill_mask(mask, (ids_own, ids_near, ids_far, ids_both), rank)
    stay = (stay_own, stay_near, stay_far, stay_both)
    turn = (turn_own, turn_near, turn_far, turn_both)
    for x in range(RANKS):
        other = rank ^ x

        @pl.when((other <= rank) & ((rank - other - 1) * ROWS < count * KEYS))
        def _(x=x, other=other):
            rows = jnp.concatenate([stay[x][...], turn[x][...]], axis=0)
            place[...] = unpacking(scalars(metas[x], ROWS, ROUNDS))
            pairs_ref[pl.ds(pl.multiple_of(other * ROWS, ROWS), ROWS), :] = pick(place[...], rows)

    q_copy.wait()
    g_copy.wait()

    def leave(h, turn, source, target, whole):
        columns = part(h, 0, whole, whole)
        return pltpu.make_async_copy(source.at[:, columns], target.at[:, columns], left.at[turn, h])

    def leave_early(h):
        return [leave(h, 0, q_ref, q_kept, WIDE), leave(h, 1, g_ref, g_kept, WIDE), leave(h, 2, pairs_ref, pairs_kept, PAIR)]

    def leave_late(h):
        return [leave(h, 3, out_ref, out_hbm, WIDE), leave(h, 4, send_ref, send_hbm, WIDE)]

    def head(h, carry):
        wide = part(h, 0, WIDE, WIDE)
        came_q = jnp.dot(bring[...], landed_ref[:, part(h, 0, WIDE, CARGO)], preferred_element_type=F32)
        came_g = jnp.dot(bring[...], landed_ref[:, part(h, BUNDLE, WIDE, CARGO)], preferred_element_type=F32)
        q_ref[:, wide] = replaced(came[...], came_q, q_ref[:, wide])
        g_ref[:, wide] = replaced(came[...], came_g, g_ref[:, wide])
        for copy in leave_early(h):
            copy.start()

        for n in range(EARLIER + 1):

            @pl.when(count == n)
            def _(n=n):
                window = pl.ds(pl.multiple_of(rank * ROWS - n * KEYS, KEYS), n * KEYS + ROWS)
                k = pairs_ref[window, part(h, 0, HEAD_SIZE, PAIR)]
                v_turned = pairs_ref[window, part(h, HEAD_SIZE, HEAD_SIZE, PAIR)].T
                shifts, inners = [], []
                for i in range(SHARED):
                    columns = part(h, i * HEAD_SIZE, HEAD_SIZE, WIDE)
                    logits = lax.dot_general(k, q_ref[:, columns], INNER, preferred_element_type=F32) + mask[window, :]
                    top = jnp.max(logits, axis=0, keepdims=True)
                    raised = jnp.exp2((logits - top) * EXP2_FACTOR)
                    total = jnp.sum(raised, axis=0, keepdims=True)
                    out = jnp.dot(v_turned, raised.astype(BF16), preferred_element_type=F32) * (1.0 / total)
                    inners.append(jnp.sum(out * g_ref[:, columns].T.astype(F32), axis=0, keepdims=True))
                    shifts.append(top * EXP2_FACTOR + jnp.log2(total))
                    out_ref[:, columns] = out.astype(BF16).T
                stats_ref[pl.ds(pl.multiple_of(h * 2 * SHARED, 2 * SHARED), 2 * SHARED), :] = jnp.concatenate(
                    shifts + inners, axis=0
                )

        send_ref[:, wide] = pick(choose, out_ref[:, wide])
        for copy in leave_late(h):
            copy.start()
        return carry

    lax.fori_loop(0, KEY_VALUE_HEADS, head, 0)
    stats_copy = pltpu.make_async_copy(stats_ref, stats_hbm, q_arrived)
    stats_copy.start()
    for h in range(KEY_VALUE_HEADS):
        for copy in leave_early(h) + leave_late(h):
            copy.wait()
    stats_copy.wait()


def forward(mate, metas, q, g, landed, stays, turns):
    wide = (ROWS, KEY_VALUE_HEADS * WIDE)
    return pl.pallas_call(
        forward_kernel,
        in_specs=[SMEM] * 5 + [VMEM] * 4 + [HBM] * 2 + [VMEM] * (1 + 2 * RANKS),
        out_specs=[HBM] * 6,
        out_shape=[
            pltpu.HBM(wide, BF16),
            pltpu.HBM(wide, BF16),
            pltpu.HBM(wide, BF16),
            pltpu.HBM(wide, BF16),
            pltpu.HBM((RANKS * ROWS, KEY_VALUE_HEADS * PAIR), BF16),
            pltpu.HBM((KEY_VALUE_HEADS * 2 * SHARED, ROWS), F32),
        ],
        scratch_shapes=[
            pltpu.VMEM(wide, BF16),
            pltpu.VMEM(wide, BF16),
            pltpu.VMEM(wide, BF16),
            pltpu.VMEM(wide, BF16),
            pltpu.VMEM((RANKS * ROWS, KEY_VALUE_HEADS * PAIR), BF16),
            pltpu.VMEM((KEY_VALUE_HEADS * 2 * SHARED, ROWS), F32),
            pltpu.VMEM((ROWS, ROWS), BF16),
            pltpu.VMEM((ROWS, ROWS), BF16),
            pltpu.VMEM((RANKS * ROWS, ROWS), F32),
            pltpu.VMEM((ROWS, HEAD_SIZE), F32),
            pltpu.SemaphoreType.DMA,
            pltpu.SemaphoreType.DMA,
            pltpu.SemaphoreType.DMA((5, KEY_VALUE_HEADS)),
        ],
        compiler_params=PARAMS,
        cost_estimate=pl.CostEstimate(flops=4 * 10**9, bytes_accessed=10**7, transcendentals=4 * 10**6),
        name="forward",
    )(
        mate, *metas, *[in_vmem(meta.reshape(1, META)) for meta in metas],
        in_hbm(q), in_hbm(g), in_vmem(landed), *[in_vmem(x) for x in (*stays, *turns)],
    )


def backward_kernel(
    mate_ref, meta_own, meta_near, meta_far, meta_both, ids_own, ids_near, ids_far, ids_both,
    q_hbm, g_hbm, pairs_hbm, stats_hbm,
    dq_hbm, send_ref, turn_keep, turn_send, keep_hbm, send_hbm,
    q_ref, g_ref, pairs_ref, stats_ref, dq_ref, stay_keep, stay_send, mask, total, arrived, stats_arrived, left, stay_left,
):
    def arrive(h, turn, source, target, whole):
        columns = part(h, 0, whole, whole)
        return pltpu.make_async_copy(source.at[:, columns], target.at[:, columns], arrived.at[turn, h])

    def arrivals(h):
        return [arrive(h, 0, pairs_hbm, pairs_ref, PAIR), arrive(h, 1, q_hbm, q_ref, WIDE), arrive(h, 2, g_hbm, g_ref, WIDE)]

    stats_copy = pltpu.make_async_copy(stats_hbm, stats_ref, stats_arrived)
    stats_copy.start()
    for h in range(KEY_VALUE_HEADS):
        for copy in arrivals(h):
            copy.start()
    metas = (meta_own, meta_near, meta_far, meta_both)
    rank = metas[0][ROWS + ROUNDS]
    count = earlier_blocks(metas, rank)
    choose = choose_sent(scalars(mate_ref, 0, ROUNDS), scalars(metas[0], ROWS, ROUNDS))
    fill_mask(mask, (ids_own, ids_near, ids_far, ids_both), rank)
    total[...] = jnp.zeros_like(total)

    def leave(h):
        columns = part(h, 0, WIDE, WIDE)
        return pltpu.make_async_copy(dq_ref.at[:, columns], dq_hbm.at[:, columns], left.at[h])

    stats_copy.wait()

    def head(h, carry):
        for copy in arrivals(h):
            copy.wait()

        for n in range(EARLIER + 1):

            @pl.when(count == n)
            def _(n=n):
                window = pl.ds(pl.multiple_of(rank * ROWS - n * KEYS, KEYS), n * KEYS + ROWS)
                k_columns = part(h, 0, HEAD_SIZE, PAIR)
                v_columns = part(h, HEAD_SIZE, HEAD_SIZE, PAIR)
                k = pairs_ref[window, k_columns]
                v = pairs_ref[window, v_columns]
                k_turned = k.T
                stats = stats_ref[pl.ds(pl.multiple_of(h * 2 * SHARED, 2 * SHARED), 2 * SHARED), :]
                lows, grads, queries, gradients = [], [], [], []
                for i in range(SHARED):
                    columns = part(h, i * HEAD_SIZE, HEAD_SIZE, WIDE)
                    q, g = q_ref[:, columns], g_ref[:, columns]
                    logits = lax.dot_general(k, q, INNER, preferred_element_type=F32)
                    weights = jnp.exp2(logits * EXP2_FACTOR - stats[i : i + 1, :] + mask[window, :])
                    grad_weights = lax.dot_general(v, g, INNER, preferred_element_type=F32)
                    inner = stats[SHARED + i : SHARED + i + 1, :]
                    grad_logits = (weights * (grad_weights - inner)).astype(BF16)
                    dq = jnp.dot(k_turned, grad_logits, preferred_element_type=F32) * FACTOR
                    dq_ref[:, columns] = dq.astype(BF16).T
                    lows.append(weights.astype(BF16))
                    grads.append(grad_logits)
                    queries.append(q)
                    gradients.append(g)
                dk = jnp.dot(
                    jnp.concatenate(grads, axis=1), jnp.concatenate(queries, axis=0), preferred_element_type=F32
                )
                dv = jnp.dot(
                    jnp.concatenate(lows, axis=1), jnp.concatenate(gradients, axis=0), preferred_element_type=F32
                )
                total[window, k_columns] = (dk * FACTOR).astype(BF16)
                total[window, v_columns] = dv.astype(BF16)

        leave(h).start()
        wide = part(h, 0, WIDE, WIDE)
        send_ref[:, wide] = pick(choose, dq_ref[:, wide])
        return carry

    lax.fori_loop(0, KEY_VALUE_HEADS, head, 0)
    for x in range(RANKS):
        rows = total[pl.ds(pl.multiple_of((rank ^ x) * ROWS, ROWS), ROWS), :]
        pieces = pick(packing(scalars(metas[x], ROWS, ROUNDS)), rows)
        stay, turn = ((stay_keep, turn_keep), (stay_send, turn_send))[x & 1]
        stay[x >> 1] = pieces[:HALF]
        turn[x >> 1] = pieces[HALF:]
    leaving = [
        pltpu.make_async_copy(stay_keep, keep_hbm, stay_left.at[0]),
        pltpu.make_async_copy(stay_send, send_hbm, stay_left.at[1]),
    ]
    for copy in leaving:
        copy.start()
    for copy in leaving + [leave(h) for h in range(KEY_VALUE_HEADS)]:
        copy.wait()


def backward(mate, metas, q, g, pairs, stats):
    wide = (ROWS, KEY_VALUE_HEADS * WIDE)
    piece = (2, HALF, KEY_VALUE_HEADS * PAIR)
    return pl.pallas_call(
        backward_kernel,
        in_specs=[SMEM] * 5 + [VMEM] * 4 + [HBM] * 4,
        out_specs=[HBM, VMEM, VMEM, VMEM, HBM, HBM],
        out_shape=[
            pltpu.HBM(wide, BF16),
            pltpu.VMEM(wide, BF16),
            pltpu.VMEM(piece, BF16),
            pltpu.VMEM(piece, BF16),
            pltpu.HBM(piece, BF16),
            pltpu.HBM(piece, BF16),
        ],
        scratch_shapes=[
            pltpu.VMEM(wide, BF16),
            pltpu.VMEM(wide, BF16),
            pltpu.VMEM(pairs.shape, BF16),
            pltpu.VMEM(stats.shape, F32),
            pltpu.VMEM(wide, BF16),
            pltpu.VMEM(piece, BF16),
            pltpu.VMEM(piece, BF16),
            pltpu.VMEM((RANKS * ROWS, ROWS), F32),
            pltpu.VMEM(pairs.shape, BF16),
            pltpu.SemaphoreType.DMA((3, KEY_VALUE_HEADS)),
            pltpu.SemaphoreType.DMA,
            pltpu.SemaphoreType.DMA((KEY_VALUE_HEADS,)),
            pltpu.SemaphoreType.DMA((2,)),
        ],
        compiler_params=PARAMS,
        cost_estimate=pl.CostEstimate(flops=8 * 10**9, bytes_accessed=10**7, transcendentals=4 * 10**6),
        name="backward",
    )(
        mate, *metas, *[in_vmem(meta.reshape(1, META)) for meta in metas],
        in_hbm(q), in_hbm(g), in_hbm(pairs), in_hbm(stats),
    )


def returning_kernel(mate_ref, dq_ref, own_ref, near_ref, far_ref, send_ref):
    choose = choose_sent_turns(scalars(mate_ref, 0, ROUNDS))
    for h in range(KEY_VALUE_HEADS):
        columns = part(h, 0, PAIR, PAIR)
        total = (
            own_ref[0, :, columns].astype(F32) + near_ref[0, :, columns].astype(F32) + far_ref[:, columns].astype(F32)
        )
        send_ref[:, part(h, 0, WIDE, BUNDLE)] = dq_ref[:, part(h, 0, WIDE, WIDE)]
        send_ref[:, part(h, WIDE, PAIR, BUNDLE)] = pick(choose, total.astype(BF16))


def returning(mate, dq, own, near, far):
    return pl.pallas_call(
        returning_kernel,
        in_specs=[SMEM] + [VMEM] * 4,
        out_specs=VMEM,
        out_shape=pltpu.VMEM((ROWS, KEY_VALUE_HEADS * BUNDLE), BF16),
        compiler_params=PARAMS,
        cost_estimate=pl.CostEstimate(flops=10**8, bytes_accessed=10**6, transcendentals=0),
        name="returning",
    )(mate, in_vmem(dq), in_vmem(own), in_vmem(near), in_vmem(far))


def merge_kernel(mate_ref, slot_ref, own_ref, landed_ref, out_ref, bring, came):
    @pl.when(pl.program_id(0) == 0)
    def _():
        bring[...] = choose_landed(scalars(mate_ref, 0, ROUNDS), scalars(slot_ref, 0, ROUNDS))
        came[...] = share_landed(bring[...])

    landed = jnp.dot(bring[...], landed_ref[...], preferred_element_type=F32)
    out_ref[...] = replaced(came[...], landed, own_ref[...])


def merge(mate, slot, own, landed):
    wide = pl.BlockSpec((ROWS, WIDE), lambda h: (0, h))
    return pl.pallas_call(
        merge_kernel,
        grid=(KEY_VALUE_HEADS,),
        in_specs=[SMEM, SMEM, wide, wide],
        out_specs=wide,
        out_shape=pltpu.HBM(own.shape, BF16),
        scratch_shapes=[pltpu.VMEM((ROWS, ROWS), BF16), pltpu.VMEM((ROWS, HEAD_SIZE), F32)],
        compiler_params=PARAMS,
        cost_estimate=pl.CostEstimate(flops=5 * 10**8, bytes_accessed=3 * 10**6, transcendentals=0),
        name="merge",
    )(mate, slot, in_hbm(own), in_vmem(landed))


def finish_kernel(
    mate_ref, slot_ref, dq_hbm, landed_ref, own_hbm, near_ref, far_ref,
    grad_q, grad_k, grad_v,
    dq_ref, own_ref, k_ref, v_ref, arrived, left,
):
    own_arriving = pltpu.make_async_copy(own_hbm, own_ref, arrived.at[1])
    own_arriving.start()
    arriving = pltpu.make_async_copy(dq_hbm, dq_ref, arrived.at[0])
    arriving.start()
    mate, slot = scalars(mate_ref, 0, ROUNDS), scalars(slot_ref, 0, ROUNDS)
    bring = choose_landed(mate, slot)
    came = share_landed(bring)
    place = unpacking(slot)[:, :HALF]
    own_arriving.wait()
    for h in range(KEY_VALUE_HEADS):
        columns = part(h, 0, PAIR, PAIR)
        total = (
            own_ref[0, :, columns].astype(F32) + near_ref[0, :, columns].astype(F32) + far_ref[:, columns].astype(F32)
        )
        landed = jnp.dot(bring, landed_ref[:, part(h, WIDE, PAIR, BUNDLE)], preferred_element_type=F32)
        pairs = (jnp.dot(place, total.astype(BF16), preferred_element_type=F32) + landed).astype(BF16)
        k_ref[:, part(h, 0, HEAD_SIZE, HEAD_SIZE)] = pairs[:, :HEAD_SIZE]
        v_ref[:, part(h, 0, HEAD_SIZE, HEAD_SIZE)] = pairs[:, HEAD_SIZE:]
    leaving = [
        pltpu.make_async_copy(k_ref, grad_k, left.at[0]),
        pltpu.make_async_copy(v_ref, grad_v, left.at[1]),
    ]
    for copy in leaving:
        copy.start()
    arriving.wait()
    for h in range(KEY_VALUE_HEADS):
        columns = part(h, 0, WIDE, WIDE)
        landed = jnp.dot(bring, landed_ref[:, part(h, 0, WIDE, BUNDLE)], preferred_element_type=F32)
        dq_ref[:, columns] = replaced(came, landed, dq_ref[:, columns])
        copy = pltpu.make_async_copy(dq_ref.at[:, columns], grad_q.at[:, columns], left.at[2 + h])
        copy.start()
        leaving.append(copy)
    for copy in leaving:
        copy.wait()


def finish(mate, slot, dq, landed, own, near, far):
    narrow = (ROWS, KEY_VALUE_HEADS * HEAD_SIZE)
    return pl.pallas_call(
        finish_kernel,
        in_specs=[SMEM, SMEM, HBM, VMEM, HBM, VMEM, VMEM],
        out_specs=[HBM] * 3,
        out_shape=[pltpu.HBM(dq.shape, BF16), pltpu.HBM(narrow, BF16), pltpu.HBM(narrow, BF16)],
        scratch_shapes=[
            pltpu.VMEM(dq.shape, BF16),
            pltpu.VMEM(own.shape, BF16),
            pltpu.VMEM(narrow, BF16),
            pltpu.VMEM(narrow, BF16),
            pltpu.SemaphoreType.DMA((2,)),
            pltpu.SemaphoreType.DMA((2 + KEY_VALUE_HEADS,)),
        ],
        compiler_params=PARAMS,
        cost_estimate=pl.CostEstimate(flops=8 * 10**8, bytes_accessed=5 * 10**6, transcendentals=0),
        name="finish",
    )(mate, slot, in_hbm(dq), in_vmem(landed), in_hbm(own), in_vmem(near), in_vmem(far))


def exchange(rows):
    blocks = rows.reshape(GROUPS, BLOCK, rows.shape[-1])
    return lax.all_to_all(blocks, "dp", split_axis=0, concat_axis=0, tiled=True).reshape(rows.shape)


def across(array):
    return lax.ppermute(array, "sp", [(i, i ^ 2) for i in range(RANKS)])


def beside(array):
    return lax.ppermute(array, "sp", [(i, i ^ 1) for i in range(RANKS)])


def spread(array):
    far = across(array)
    return array, beside(array), far, beside(far)


def collect(keep, send):
    near = beside(send)
    partial = (keep[1].astype(F32) + near[1].astype(F32)).astype(BF16)
    return keep, near, across(partial)


def body(queries, keys, values, cotangent, doc_ids, partners, swap_slots):
    q, k, v, g = queries[0], keys[0], values[0], cotangent[0]
    mate = in_hbm(partners.reshape(ROUNDS))
    slots = swap_slots.reshape(ROUNDS)
    slot = in_hbm(slots)
    rank = lax.axis_index("sp").astype(jnp.int32).reshape(1)
    meta = jnp.concatenate(
        [doc_ids.reshape(ROWS), slots, rank, jnp.zeros((META - ROWS - ROUNDS - 1,), jnp.int32)]
    )

    metas = meta, beside(meta), across(meta), lax.ppermute(meta, "sp", [(i, i ^ 3) for i in range(RANKS)])
    send, stay = outgoing(mate, slot, q, k, v, g)
    send, metas = lax.optimization_barrier((send, metas))
    landed = exchange(send)
    stays = spread(stay)
    landed, stays = lax.optimization_barrier((landed, stays))
    turns = spread(traded_pairs(mate, landed))
    out, send, *kept = forward(mate, metas, q, g, landed, stays, turns)
    landed_out = exchange(send)
    dq, send, turn_keep, turn_send, stay_keep, stay_send = backward(mate, metas, *kept)
    landed_out, turn_send = lax.optimization_barrier((landed_out, turn_send))
    send = returning(mate, send, *collect(turn_keep, turn_send))
    landed = exchange(send)
    attended = merge(mate, slot, out, landed_out)
    grad_q, grad_k, grad_v = finish(mate, slot, dq, landed, *collect(stay_keep, stay_send))
    return attended[None], grad_q[None], grad_k[None], grad_v[None]


def solution(mesh):
    rows = P("dp", "sp", None)
    return jax.shard_map(
        body,
        mesh=mesh,
        in_specs=(rows, rows, rows, rows, P("dp", "sp"), P(None, "dp"), rows),
        out_specs=(rows, rows, rows, rows),
        check_vma=False,
    )
```

time: 183 us -> 159 us (0.87); the launches traced: 181 us -> 159 us
  starting transfers between devices: 61.3 us -> 38.8 us
  waiting for transfers between devices: 57.2 us -> 75.2 us
  Pallas kernels: 54.6 us -> 41.8 us
  local copies, waits for them, and re-layouts: 6.28 us -> 0.72 us
    ppermute x5, waiting for transfers between devices: 35.7 us -> 65.2 us  [across(): return lax.ppermute(array, 'sp', [(i, i ^ 2) for i in range(RANKS)])]
    all_to_all x4 -> x3, starting transfers between devices: 34.7 us -> 18.9 us  [exchange(): lax.all_to_all(blocks, 'dp', split_axis=0, concat_axis=0, tiled=True)]
    all_to_all x4 -> x3, waiting for transfers between devices: 18.9 us -> 4.27 us  [exchange(): lax.all_to_all(blocks, 'dp', split_axis=0, concat_axis=0, tiled=True)]
    pallas_call x5, Pallas kernels: 45.4 us -> 33 us  [the longest x1 13.4 us: backward(): pl.pallas_call(backward_kernel, in_specs=[SMEM] * 5 + [VMEM] * 4 + [HBM]...]
    ppermute x5, starting transfers between devices: 20.9 us -> 8.95 us  [across(): return lax.ppermute(array, 'sp', [(i, i ^ 2) for i in range(RANKS)])]
    ppermute x0 -> x1, starting transfers between devices: none -> 5 us  [body(): lax.ppermute(meta, 'sp', [(i, i ^ 3) for i in range(RANKS)])]
    unnamed x40 -> x4, local copies, waits for them, and re-layouts: 5.07 us -> 0.71 us
    ppermute x5 -> x7, waiting for transfers between devices: 2.58 us -> 5.69 us  [beside(): return lax.ppermute(array, 'sp', [(i, i ^ 1) for i in range(RANKS)])]
  transfers between devices with their start and end apart: 14 -> 16, of which waited for: 6 -> 9; matrix products, arithmetic and copies ran while one was open for 1% -> 1% of each run, Pallas kernels for 15% -> 14%
where the time goes in v1:
time: 159 us
  waiting for transfers between devices  75.2 us (47%)
  Pallas kernels  41.8 us (26%)
  starting transfers between devices  38.8 us (24%)
  other arithmetic  1.86 us (1%)
    ppermute x5, waiting for transfers between devices, across(): return lax.ppermute(array, 'sp', [(i, i ^ 2) for i in range(RANKS)])  65.2 us
    all_to_all x3, starting transfers between devices, exchange(): lax.all_to_all(blocks, 'dp', split_axis=0, concat_axis=0, tiled=True)  18.9 us
    pallas_call x1, Pallas kernels, backward(): pl.pallas_call(backward_kernel, in_specs=[SMEM] * 5 + [VMEM] * 4 + [HBM]...  13.4 us
    pallas_call x1, Pallas kernels, forward(): pl.pallas_call(forward_kernel, in_specs=[SMEM] * 5 + [VMEM] * 4 + [HBM] *...  13 us
    ppermute x5, starting transfers between devices, across(): return lax.ppermute(array, 'sp', [(i, i ^ 2) for i in range(RANKS)])  8.95 us
    ppermute x7, starting transfers between devices, beside(): return lax.ppermute(array, 'sp', [(i, i ^ 1) for i in range(RANKS)])  6.04 us
    ppermute x7, waiting for transfers between devices, beside(): return lax.ppermute(array, 'sp', [(i, i ^ 1) for i in range(RANKS)])  5.69 us
    ppermute x1, starting transfers between devices, body(): lax.ppermute(meta, 'sp', [(i, i ^ 3) for i in range(RANKS)])  5 us
  transfers between devices with their start and end apart: 16, of which 9 were waited for; matrix products, arithmetic and copies ran while one was open for 1% of the time, Pallas kernels for 14%

profile of v1, /device:TPU:1, one launch (start us, length us, event | category | flops | bytes accessed | tf_op | source)
XLA Modules:
  0.0 159.3 jit_solution(9589005347097061420)
XLA Ops:
  0.6 0.8 pad_add_fusion.meta_own
  1.4 5.0 %collective-permute-start.2 = (s32[384]{0:T(512)S(1)}, s32[384]{0:T(512)S(1)}, u32[]{:S(2)}, u32[]{:S(2)}) collective-permute-start(s32[384]{0:T(512)S(1)} %pad_add_fusion.meta_own), channel_id=1, source_target_pairs={{0,3},{1,2},{2,1},{3,0},{4,7},{5,6},{6,5},{7,4},{8,11},{9,10},{10,... | collective-permute-start | bytes 4616 | tf_op jit(solution)/shard_map/ppermute | solution.py:614
  6.4 0.0 collective-permute-start.1
  6.4 0.5 collective-permute-start
  6.9 4.9 %outgoing.1 = (bf16[256,5120]{1,0:T(8,128)(2,1)}, bf16[128,1024]{1,0:T(8,128)(2,1)S(1)}) custom-call(s32[16]{0:T(128)} %bitcast.29, s32[16]{0:T(128)} %bitcast.37, bf16[256,2048]{1,0:T(8,128)(2,1)} %bitcast.41, bf16[256,512]{1,0:T(8,128)(2,1)} %bitcast.46, bf16[256,512]{1,0:T(8,128)(2,1)} %bitcast.47, bf16[256,2048]{1,0:T(8,128)(2,1)} %bitcast.43), custom_call_target="tpu_custom_call" | custom-call | flops 1000000000 | bytes 5000000 | tf_op jit(solution)/shard_map/outgoing/pallas_call | solution.py:144
  11.8 0.0 collective-permute-done.2.meta_both
  11.8 0.0 collective-permute-done.1.meta_far
  11.8 0.0 collective-permute-done.meta_near
  11.8 7.5 %all-to-all-start = ((bf16[32,8,5120]{2,1,0:T(8,128)(2,1)}), bf16[32,8,5120]{2,1,0:T(8,128)(2,1)S(1)}, u32[]{:S(2)}, u32[]{:S(2)}) async-start(bf16[32,8,5120]{2,1,0:T(8,128)(2,1)} %bitcast.26), calls=%async_computation | async-start | bytes 5242880 | tf_op jit(solution)/shard_map/all_to_all | solution.py:582
  19.3 3.3 %collective-permute-start.4 = (bf16[128,1024]{1,0:T(8,128)(2,1)S(1)}, bf16[128,1024]{1,0:T(8,128)(2,1)S(1)}, u32[]{:S(2)}, u32[]{:S(2)}) collective-permute-start(bf16[128,1024]{1,0:T(8,128)(2,1)S(1)} %get-tuple-element.41.stay_own), channel_id=1, source_target_pairs={{0,2},{1,3},{2,0},{3,1},{4,6},{5,7},{6,4},{7,5},{8,10},{9,11},{10,... | collective-permute-start | bytes 786440 | tf_op jit(solution)/shard_map/ppermute | solution.py:586
  22.6 1.0 collective-permute-start.3
  23.6 33.1 %collective-permute-done.4.stay_far = bf16[128,1024]{1,0:T(8,128)(2,1)S(1)} collective-permute-done((bf16[128,1024]{1,0:T(8,128)(2,1)S(1)}, bf16[128,1024]{1,0:T(8,128)(2,1)S(1)}, u32[]{:S(2)}, u32[]{:S(2)}) %collective-permute-start.4) | collective-permute-done | bytes 262176 | tf_op jit(solution)/shard_map/ppermute | solution.py:586
  56.6 1.2 collective-permute-start.5
  57.9 0.0 collective-permute-done.3.stay_near
  57.9 1.2 collective-permute-done.5.stay_both
  59.0 0.0 copy-start
  59.0 0.7 copy-done
  59.7 0.0 all-to-all-done
  59.7 0.0 copy-start.1
  59.7 1.0 traded_pairs.1.turn_own
  60.8 0.4 collective-permute-start.7
  61.2 0.7 collective-permute-start.6
  61.8 8.1 %collective-permute-done.7.turn_far = bf16[128,1024]{1,0:T(8,128)(2,1)S(1)} collective-permute-done((bf16[128,1024]{1,0:T(8,128)(2,1)S(1)}, bf16[128,1024]{1,0:T(8,128)(2,1)S(1)}, u32[]{:S(2)}, u32[]{:S(2)}) %collective-permute-start.7) | collective-permute-done | bytes 262176 | tf_op jit(solution)/shard_map/ppermute | solution.py:586
  69.9 1.2 collective-permute-start.8
  71.1 0.0 collective-permute-done.6.turn_near
  71.1 1.1 collective-permute-done.8.turn_both
  72.2 0.0 copy-done.1
  72.2 13.0 %forward.1 = (bf16[256,2048]{1,0:T(8,128)(2,1)}, bf16[256,2048]{1,0:T(8,128)(2,1)}, bf16[256,2048]{1,0:T(8,128)(2,1)}, bf16[256,2048]{1,0:T(8,128)(2,1)}, bf16[1024,1024]{1,0:T(8,128)(2,1)}, /*index=5*/f32[32,256]{1,0:T(8,128)}) custom-call(s32[16]{0:T(128)} %bitcast.31, s32[384]{0:T(512)S(1)} %pad_add_fusion.meta_own, ...), custom_call_target="tpu_custom_call" | custom-call | flops 4000000000 | bytes 10000000 | tf_op jit(solution)/shard_map/forward/pallas_call | solution.py:303
  85.2 6.9 %all-to-all-start.1 = ((bf16[32,8,2048]{2,1,0:T(8,128)(2,1)}), bf16[32,8,2048]{2,1,0:T(8,128)(2,1)S(1)}, u32[]{:S(2)}, u32[]{:S(2)}) async-start(bf16[32,8,2048]{2,1,0:T(8,128)(2,1)} %bitcast.27), calls=%async_computation.1 | async-start | bytes 2097152 | tf_op jit(solution)/shard_map/all_to_all | solution.py:582
  92.1 13.4 %backward.1 = (bf16[256,2048]{1,0:T(8,128)(2,1)}, bf16[256,2048]{1,0:T(8,128)(2,1)S(1)}, bf16[2,128,1024]{2,1,0:T(8,128)(2,1)S(1)}, bf16[2,128,1024]{2,1,0:T(8,1...) custom-call(s32[16]{0:T(128)} %bitcast.32, s32[384]{0:T(512)S(1)} %pad_add_fusion.meta_own, ...), custom_call_target="tpu_custom_call" | custom-call | flops 8000000000 | bytes 10000000 | tf_op jit(solution)/shard_map/backward/pallas_call | solution.py:434
  105.5 4.3 %all-to-all-done.1 = bf16[32,8,2048]{2,1,0:T(8,128)(2,1)S(1)} async-done(((bf16[32,8,2048]{2,1,0:T(8,128)(2,1)}), bf16[32,8,2048]{2,1,0:T(8,128)(2,1)S(1)}, u32[]{:S(2)}, u32[]{:S(2)}) %all-to-all-start.1) | async-done | bytes 1048608 | tf_op jit(solution)/shard_map/all_to_all | solution.py:582
  109.8 0.3 collective-permute-start.9
  110.1 1.6 %collective-permute-done.9.near_ref = bf16[2,128,1024]{2,1,0:T(8,128)(2,1)S(1)} collective-permute-done((bf16[2,128,1024]{2,1,0:T(8,128)(2,1)S(1)}, bf16[2,128,1024]{2,1,0:T(8,128)(2,1)S(1)}, u32[]{:S(2)}, u32[]{:S(2)}) %collective-permute-start.9) | collective-permute-done | bytes 524320 | tf_op jit(solution)/shard_map/ppermute | solution.py:590
  111.7 0.1 fusion
  111.8 1.6 %collective-permute-start.10 = (bf16[128,1024]{1,0:T(8,128)(2,1)S(1)}, bf16[128,1024]{1,0:T(8,128)(2,1)S(1)}, u32[]{:S(2)}, u32[]{:S(2)}) collective-permute-start(bf16[128,1024]{1,0:T(8,128)(2,1)S(1)} %fusion), channel_id=1, source_target_pairs={{0,2},{1,3},{2,0},{3,1},{4,6},{5,7},{6,4},{7,5},{8,10},{9,11},{10,... | collective-permute-start | bytes 786440 | tf_op jit(solution)/shard_map/ppermute | solution.py:586
  113.4 7.6 %collective-permute-done.10.far_ref = bf16[128,1024]{1,0:T(8,128)(2,1)S(1)} collective-permute-done((bf16[128,1024]{1,0:T(8,128)(2,1)S(1)}, bf16[128,1024]{1,0:T(8,128)(2,1)S(1)}, u32[]{:S(2)}, u32[]{:S(2)}) %collective-permute-start.10) | collective-permute-done | bytes 262176 | tf_op jit(solution)/shard_map/ppermute | solution.py:586
  121.0 2.2 %returning.1 = bf16[256,3072]{1,0:T(8,128)(2,1)} custom-call(s32[16]{0:T(128)} %bitcast.33, bf16[256,2048]{1,0:T(8,128)(2,1)S(1)} %get-tuple-element.54.dq_ref, bf16[2,128,1024]{2,1,0:T(8,128)(2,1)S(1)} %get-tuple-element.55.own_ref, bf16[2,128,1024]{2,1,0:T(8,128)(2,1)S(1)} %collective-permute-done.9.near_ref, ...), custom_call_target="tpu_custom_call" | custom-call | flops 100000000 | bytes 1000000 | tf_op jit(solution)/shard_map/returning/pallas_call | solution.py:482
  123.2 4.4 %all-to-all-start.2 = ((bf16[32,8,3072]{2,1,0:T(8,128)(2,1)}), bf16[32,8,3072]{2,1,0:T(8,128)(2,1)S(1)}, u32[]{:S(2)}, u32[]{:S(2)}) async-start(bf16[32,8,3072]{2,1,0:T(8,128)(2,1)} %bitcast.14), calls=%async_computation.2 | async-start | bytes 3145728 | tf_op jit(solution)/shard_map/all_to_all | solution.py:582
  127.6 1.2 collective-permute-start.11
  128.8 1.7 %collective-permute-done.11.near_ref = bf16[2,128,1024]{2,1,0:T(8,128)(2,1)S(1)} collective-permute-done((bf16[2,128,1024]{2,1,0:T(8,128)(2,1)}, bf16[2,128,1024]{2,1,0:T(8,128)(2,1)S(1)}, u32[]{:S(2)}, u32[]{:S(2)}) %collective-permute-start.11) | collective-permute-done | bytes 524320 | tf_op jit(solution)/shard_map/ppermute | solution.py:590
  130.6 1.0 fusion.1
  131.6 3.6 %collective-permute-start.12 = (bf16[128,1024]{1,0:T(8,128)(2,1)S(1)}, bf16[128,1024]{1,0:T(8,128)(2,1)S(1)}, u32[]{:S(2)}, u32[]{:S(2)}) collective-permute-start(bf16[128,1024]{1,0:T(8,128)(2,1)S(1)} %fusion.1), channel_id=1, source_target_pairs={{0,2},{1,3},{2,0},{3,1},{4,6},{5,7},{6,4},{7,5},{8,10},{9,11},{10,... | collective-permute-start | bytes 786440 | tf_op jit(solution)/shard_map/ppermute | solution.py:586
  135.3 3.9 %merge.1 = bf16[256,2048]{1,0:T(8,128)(2,1)} custom-call(s32[16]{0:T(128)} %bitcast.34, s32[16]{0:T(128)} %bitcast.38, bf16[256,2048]{1,0:T(8,128)(2,1)} %get-tuple-element.45.own_ref, bf16[256,2048]{1,0:T(8,128)(2,1)S(1)} %bitcast.25), custom_call_target="tpu_custom_call" | custom-call | flops 500000000 | bytes 3000000 | tf_op jit(solution)/shard_map/merge/pallas_call | solution.py:505
  139.2 16.5 %collective-permute-done.12.far_ref = bf16[128,1024]{1,0:T(8,128)(2,1)S(1)} collective-permute-done((bf16[128,1024]{1,0:T(8,128)(2,1)S(1)}, bf16[128,1024]{1,0:T(8,128)(2,1)S(1)}, u32[]{:S(2)}, u32[]{:S(2)}) %collective-permute-start.12) | collective-permute-done | bytes 262176 | tf_op jit(solution)/shard_map/ppermute | solution.py:586
  155.7 0.0 all-to-all-done.2
  155.7 3.4 %finish.1 = (bf16[256,2048]{1,0:T(8,128)(2,1)}, bf16[256,512]{1,0:T(8,128)(2,1)}, bf16[256,512]{1,0:T(8,128)(2,1)}) custom-call(s32[16]{0:T(128)} %bitcast.35, s32[16]{0:T(128)} %bitcast.39, bf16[256,2048]{1,0:T(8,128)(2,1)} %get-tuple-element.53.dq_hbm, bf16[256,3072]{1,0:T(8,128)(2,1)S(1)} %bitcast.24, bf16[2,128,1024]{2,1,0:T(8,128)(2,1)} %get-tuple-element.57.own_hbm, ...), custom_call_target="tpu_custom_call" | custom-call | flops 800000000 | bytes 5000000 | tf_op jit(solution)/shard_map/finish/pallas_call | solution.py:561
  (5 shorter events, 0.0 us)
Async XLA Ops:
  1.4 10.4 %collective-permute-start.2 = (s32[384]{0:T(512)S(1)}, s32[384]{0:T(512)S(1)}, u32[]{:S(2)}, u32[]{:S(2)}) collective-permute-start(s32[384]{0:T(512)S(1)} %pad_add_fusion.meta_own), channel_id=1, source_target_pairs={{0,3},{1,2},{2,1},{3,0},{4,7},{5,6},{6,5},{7,4},{8,11},{9,10},{10,... | collective-permute-start | bytes 4616 | tf_op jit(solution)/shard_map/ppermute | solution.py:614
  6.4 5.4 %collective-permute-start.1 = (s32[384]{0:T(512)S(1)}, s32[384]{0:T(512)S(1)}, u32[]{:S(2)}, u32[]{:S(2)}) collective-permute-start(s32[384]{0:T(512)S(1)} %pad_add_fusion.meta_own), channel_id=1, source_target_pairs={{0,2},{1,3},{2,0},{3,1},{4,6},{5,7},{6,4},{7,5},{8,10},{9,11},{10,... | collective-permute-start | bytes 4616 | tf_op jit(solution)/shard_map/ppermute | solution.py:586
  6.4 5.4 %collective-permute-start = (s32[384]{0:T(512)S(1)}, s32[384]{0:T(512)S(1)}, u32[]{:S(2)}, u32[]{:S(2)}) collective-permute-start(s32[384]{0:T(512)S(1)} %pad_add_fusion.meta_own), channel_id=1, source_target_pairs={{0,1},{1,0},{2,3},{3,2},{4,5},{5,4},{6,7},{7,6},{8,9},{9,8},{10,11... | collective-permute-start | bytes 4616 | tf_op jit(solution)/shard_map/ppermute | solution.py:590
  11.8 47.9 %all-to-all-start = ((bf16[32,8,5120]{2,1,0:T(8,128)(2,1)}), bf16[32,8,5120]{2,1,0:T(8,128)(2,1)S(1)}, u32[]{:S(2)}, u32[]{:S(2)}) async-start(bf16[32,8,5120]{2,1,0:T(8,128)(2,1)} %bitcast.26), calls=%async_computation | async-start | bytes 5242880 | tf_op jit(solution)/shard_map/all_to_all | solution.py:582
  19.3 37.3 %collective-permute-start.4 = (bf16[128,1024]{1,0:T(8,128)(2,1)S(1)}, bf16[128,1024]{1,0:T(8,128)(2,1)S(1)}, u32[]{:S(2)}, u32[]{:S(2)}) collective-permute-start(bf16[128,1024]{1,0:T(8,128)(2,1)S(1)} %get-tuple-element.41.stay_own), channel_id=1, source_target_pairs={{0,2},{1,3},{2,0},{3,1},{4,6},{5,7},{6,4},{7,5},{8,10},{9,11},{10,... | collective-permute-start | bytes 786440 | tf_op jit(solution)/shard_map/ppermute | solution.py:586
  22.6 35.3 %collective-permute-start.3 = (bf16[128,1024]{1,0:T(8,128)(2,1)S(1)}, bf16[128,1024]{1,0:T(8,128)(2,1)S(1)}, u32[]{:S(2)}, u32[]{:S(2)}) collective-permute-start(bf16[128,1024]{1,0:T(8,128)(2,1)S(1)} %get-tuple-element.41.stay_own), channel_id=1, source_target_pairs={{0,1},{1,0},{2,3},{3,2},{4,5},{5,4},{6,7},{7,6},{8,9},{9,8},{10,11... | collective-permute-start | bytes 786440 | tf_op jit(solution)/shard_map/ppermute | solution.py:590
  56.6 2.4 %collective-permute-start.5 = (bf16[128,1024]{1,0:T(8,128)(2,1)S(1)}, bf16[128,1024]{1,0:T(8,128)(2,1)S(1)}, u32[]{:S(2)}, u32[]{:S(2)}) collective-permute-start(bf16[128,1024]{1,0:T(8,128)(2,1)S(1)} %collective-permute-done.4.stay_far), channel_id=1, source_target_pairs={{0,1},{1,0},{2,3},{3,2},{4,5},{5,4},{6,7},{7,6},{8,9},{9,8},{10,11... | collective-permute-start | bytes 786440 | tf_op jit(solution)/shard_map/ppermute | solution.py:590
  59.0 0.7 copy-start
  59.7 12.5 %copy-start.1 = (bf16[128,1024]{1,0:T(8,128)(2,1)S(1)}, bf16[128,1024]{1,0:T(8,128)(2,1)}, u32[]{:S(2)}) copy-start(bf16[128,1024]{1,0:T(8,128)(2,1)} %copy-done) | copy-start | bytes 786436
  60.8 9.1 %collective-permute-start.7 = (bf16[128,1024]{1,0:T(8,128)(2,1)S(1)}, bf16[128,1024]{1,0:T(8,128)(2,1)S(1)}, u32[]{:S(2)}, u32[]{:S(2)}) collective-permute-start(bf16[128,1024]{1,0:T(8,128)(2,1)S(1)} %traded_pairs.1.turn_own), channel_id=1, source_target_pairs={{0,2},{1,3},{2,0},{3,1},{4,6},{5,7},{6,4},{7,5},{8,10},{9,11},{10,... | collective-permute-start | bytes 786440 | tf_op jit(solution)/shard_map/ppermute | solution.py:586
  61.2 9.9 %collective-permute-start.6 = (bf16[128,1024]{1,0:T(8,128)(2,1)S(1)}, bf16[128,1024]{1,0:T(8,128)(2,1)S(1)}, u32[]{:S(2)}, u32[]{:S(2)}) collective-permute-start(bf16[128,1024]{1,0:T(8,128)(2,1)S(1)} %traded_pairs.1.turn_own), channel_id=1, source_target_pairs={{0,1},{1,0},{2,3},{3,2},{4,5},{5,4},{6,7},{7,6},{8,9},{9,8},{10,11... | collective-permute-start | bytes 786440 | tf_op jit(solution)/shard_map/ppermute | solution.py:590
  69.9 2.4 %collective-permute-start.8 = (bf16[128,1024]{1,0:T(8,128)(2,1)S(1)}, bf16[128,1024]{1,0:T(8,128)(2,1)S(1)}, u32[]{:S(2)}, u32[]{:S(2)}) collective-permute-start(bf16[128,1024]{1,0:T(8,128)(2,1)S(1)} %collective-permute-done.7.turn_far), channel_id=1, source_target_pairs={{0,1},{1,0},{2,3},{3,2},{4,5},{5,4},{6,7},{7,6},{8,9},{9,8},{10,11... | collective-permute-start | bytes 786440 | tf_op jit(solution)/shard_map/ppermute | solution.py:590
  85.2 24.6 %all-to-all-start.1 = ((bf16[32,8,2048]{2,1,0:T(8,128)(2,1)}), bf16[32,8,2048]{2,1,0:T(8,128)(2,1)S(1)}, u32[]{:S(2)}, u32[]{:S(2)}) async-start(bf16[32,8,2048]{2,1,0:T(8,128)(2,1)} %bitcast.27), calls=%async_computation.1 | async-start | bytes 2097152 | tf_op jit(solution)/shard_map/all_to_all | solution.py:582
  109.8 1.9 %collective-permute-start.9 = (bf16[2,128,1024]{2,1,0:T(8,128)(2,1)S(1)}, bf16[2,128,1024]{2,1,0:T(8,128)(2,1)S(1)}, u32[]{:S(2)}, u32[]{:S(2)}) collective-permute-start(bf16[2,128,1024]{2,1,0:T(8,128)(2,1)S(1)} %get-tuple-element.56), channel_id=1, source_target_pairs={{0,1},{1,0},{2,3},{3,2},{4,5},{5,4},{6,7},{7,6},{8,9},{9,8},{10,11... | collective-permute-start | bytes 1572872 | tf_op jit(solution)/shard_map/ppermute | solution.py:590
  111.8 9.2 %collective-permute-start.10 = (bf16[128,1024]{1,0:T(8,128)(2,1)S(1)}, bf16[128,1024]{1,0:T(8,128)(2,1)S(1)}, u32[]{:S(2)}, u32[]{:S(2)}) collective-permute-start(bf16[128,1024]{1,0:T(8,128)(2,1)S(1)} %fusion), channel_id=1, source_target_pairs={{0,2},{1,3},{2,0},{3,1},{4,6},{5,7},{6,4},{7,5},{8,10},{9,11},{10,... | collective-permute-start | bytes 786440 | tf_op jit(solution)/shard_map/ppermute | solution.py:586
  123.2 32.5 %all-to-all-start.2 = ((bf16[32,8,3072]{2,1,0:T(8,128)(2,1)}), bf16[32,8,3072]{2,1,0:T(8,128)(2,1)S(1)}, u32[]{:S(2)}, u32[]{:S(2)}) async-start(bf16[32,8,3072]{2,1,0:T(8,128)(2,1)} %bitcast.14), calls=%async_computation.2 | async-start | bytes 3145728 | tf_op jit(solution)/shard_map/all_to_all | solution.py:582
  127.6 3.0 %collective-permute-start.11 = (bf16[2,128,1024]{2,1,0:T(8,128)(2,1)}, bf16[2,128,1024]{2,1,0:T(8,128)(2,1)S(1)}, u32[]{:S(2)}, u32[]{:S(2)}) collective-permute-start(bf16[2,128,1024]{2,1,0:T(8,128)(2,1)} %get-tuple-element.58), channel_id=1, source_target_pairs={{0,1},{1,0},{2,3},{3,2},{4,5},{5,4},{6,7},{7,6},{8,9},{9,8},{10,11... | collective-permute-start | bytes 1572872 | tf_op jit(solution)/shard_map/ppermute | solution.py:590
  131.6 24.1 %collective-permute-start.12 = (bf16[128,1024]{1,0:T(8,128)(2,1)S(1)}, bf16[128,1024]{1,0:T(8,128)(2,1)S(1)}, u32[]{:S(2)}, u32[]{:S(2)}) collective-permute-start(bf16[128,1024]{1,0:T(8,128)(2,1)S(1)} %fusion.1), channel_id=1, source_target_pairs={{0,2},{1,3},{2,0},{3,1},{4,6},{5,7},{6,4},{7,5},{8,10},{9,11},{10,... | collective-permute-start | bytes 786440 | tf_op jit(solution)/shard_map/ppermute | solution.py:586

commit v2 on v1

--- a/solution.py
+++ b/solution.py
@@ -30,7 +30,7 @@
 SMEM = pl.BlockSpec(memory_space=pltpu.SMEM)
 VMEM = pl.BlockSpec(memory_space=pltpu.VMEM)
 HBM = pl.BlockSpec(memory_space=pl.ANY)
-PARAMS = pltpu.CompilerParams(vmem_limit_bytes=24 * 1024 * 1024)
+PARAMS = pltpu.CompilerParams(vmem_limit_bytes=28 * 1024 * 1024)
 
 
 def in_hbm(array):
@@ -128,39 +128,50 @@
     return [ref[first + t] for t in range(count)]
 
 
-def outgoing_kernel(mate_ref, slot_ref, q_ref, k_ref, v_ref, g_ref, send_ref, stay_ref, choose, keep):
+def staying_kernel(slot_ref, k_hbm, v_hbm, stay_ref, k_ref, v_ref, arrived):
+    copies = [pltpu.make_async_copy(k_hbm, k_ref, arrived.at[0]), pltpu.make_async_copy(v_hbm, v_ref, arrived.at[1])]
+    for copy in copies:
+        copy.start()
+    keep = packing(scalars(slot_ref, 0, ROUNDS), HALF)
+    for copy in copies:
+        copy.wait()
+    for h in range(KEY_VALUE_HEADS):
+        head = part(h, 0, HEAD_SIZE, HEAD_SIZE)
+        stay_ref[:, part(h, 0, PAIR, PAIR)] = pick(keep, jnp.concatenate([k_ref[:, head], v_ref[:, head]], axis=1))
+
+
+def staying(slot, k, v):
+    return pl.pallas_call(
+        staying_kernel,
+        in_specs=[SMEM, HBM, HBM],
+        out_specs=VMEM,
+        out_shape=pltpu.VMEM((HALF, KEY_VALUE_HEADS * PAIR), BF16),
+        scratch_shapes=[pltpu.VMEM(k.shape, BF16), pltpu.VMEM(v.shape, BF16), pltpu.SemaphoreType.DMA((2,))],
+        compiler_params=PARAMS,
+        cost_estimate=pl.CostEstimate(flops=10**8, bytes_accessed=10**6, transcendentals=0),
+        name="staying",
+    )(slot, in_hbm(k), in_hbm(v))
+
+
+def outgoing_kernel(mate_ref, slot_ref, q_ref, k_ref, v_ref, g_ref, send_ref, choose):
     @pl.when(pl.program_id(0) == 0)
     def _():
-        mate, slot = scalars(mate_ref, 0, ROUNDS), scalars(slot_ref, 0, ROUNDS)
-        choose[...] = choose_sent(mate, slot)
-        keep[...] = packing(slot, HALF)
-
-    pairs = jnp.concatenate([k_ref[...], v_ref[...]], axis=1)
-    send_ref[...] = pick(choose[...], jnp.concatenate([q_ref[...], pairs, g_ref[...]], axis=1))
-    stay_ref[...] = pick(keep[...], pairs)
+        choose[...] = choose_sent(scalars(mate_ref, 0, ROUNDS), scalars(slot_ref, 0, ROUNDS))
+
+    rows = jnp.concatenate([q_ref[...], k_ref[...], v_ref[...], g_ref[...]], axis=1)
+    send_ref[...] = pick(choose[...], rows)
 
 
 def outgoing(mate, slot, q, k, v, g):
+    wide = pl.BlockSpec((ROWS, WIDE), lambda h: (0, h))
+    head = pl.BlockSpec((ROWS, HEAD_SIZE), lambda h: (0, h))
     return pl.pallas_call(
         outgoing_kernel,
         grid=(KEY_VALUE_HEADS,),
-        in_specs=[
-            SMEM,
-            SMEM,
-            pl.BlockSpec((ROWS, WIDE), lambda h: (0, h)),
-            pl.BlockSpec((ROWS, HEAD_SIZE), lambda h: (0, h)),
-            pl.BlockSpec((ROWS, HEAD_SIZE), lambda h: (0, h)),
-            pl.BlockSpec((ROWS, WIDE), lambda h: (0, h)),
-        ],
-        out_specs=[
-            pl.BlockSpec((ROWS, CARGO), lambda h: (0, h)),
-            pl.BlockSpec((HALF, PAIR), lambda h: (0, h)),
-        ],
-        out_shape=[
-            pltpu.HBM((ROWS, KEY_VALUE_HEADS * CARGO), BF16),
-            pltpu.VMEM((HALF, KEY_VALUE_HEADS * PAIR), BF16),
-        ],
-        scratch_shapes=[pltpu.VMEM((ROWS, ROWS), BF16), pltpu.VMEM((HALF, ROWS), BF16)],
+        in_specs=[SMEM, SMEM, wide, head, head, wide],
+        out_specs=pl.BlockSpec((ROWS, CARGO), lambda h: (0, h)),
+        out_shape=pltpu.HBM((ROWS, KEY_VALUE_HEADS * CARGO), BF16),
+        scratch_shapes=[pltpu.VMEM((ROWS, ROWS), BF16)],
         compiler_params=PARAMS,
         cost_estimate=pl.CostEstimate(flops=10**9, bytes_accessed=5 * 10**6, transcendentals=0),
         name="outgoing",
@@ -269,20 +280,20 @@
                 window = pl.ds(pl.multiple_of(rank * ROWS - n * KEYS, KEYS), n * KEYS + ROWS)
                 k = pairs_ref[window, part(h, 0, HEAD_SIZE, PAIR)]
                 v_turned = pairs_ref[window, part(h, HEAD_SIZE, HEAD_SIZE, PAIR)].T
-                shifts, inners = [], []
-                for i in range(SHARED):
-                    columns = part(h, i * HEAD_SIZE, HEAD_SIZE, WIDE)
-                    logits = lax.dot_general(k, q_ref[:, columns], INNER, preferred_element_type=F32) + mask[window, :]
-                    top = jnp.max(logits, axis=0, keepdims=True)
-                    raised = jnp.exp2((logits - top) * EXP2_FACTOR)
-                    total = jnp.sum(raised, axis=0, keepdims=True)
-                    out = jnp.dot(v_turned, raised.astype(BF16), preferred_element_type=F32) * (1.0 / total)
-                    inners.append(jnp.sum(out * g_ref[:, columns].T.astype(F32), axis=0, keepdims=True))
-                    shifts.append(top * EXP2_FACTOR + jnp.log2(total))
-                    out_ref[:, columns] = out.astype(BF16).T
-                stats_ref[pl.ds(pl.multiple_of(h * 2 * SHARED, 2 * SHARED), 2 * SHARED), :] = jnp.concatenate(
-                    shifts + inners, axis=0
-                )
+                heads = [part(h, i * HEAD_SIZE, HEAD_SIZE, WIDE) for i in range(SHARED)]
+                q = jnp.concatenate([q_ref[:, columns] for columns in heads], axis=0)
+                g_turned = jnp.concatenate([g_ref[:, columns].T for columns in heads], axis=1)
+                logits = lax.dot_general(k, q, INNER, preferred_element_type=F32)
+                logits = logits + jnp.concatenate([mask[window, :]] * SHARED, axis=1)
+                top = jnp.max(logits, axis=0, keepdims=True)
+                raised = jnp.exp2((logits - top) * EXP2_FACTOR)
+                total = jnp.sum(raised, axis=0, keepdims=True)
+                out = jnp.dot(v_turned, raised.astype(BF16), preferred_element_type=F32) * (1.0 / total)
+                inner = jnp.sum(out * g_turned.astype(F32), axis=0, keepdims=True)
+                out = out.astype(BF16)
+                for i, columns in enumerate(heads):
+                    out_ref[:, columns] = out[:, i * ROWS : (i + 1) * ROWS].T
+                stats_ref[h] = jnp.concatenate([top * EXP2_FACTOR + jnp.log2(total), inner], axis=0)
 
         send_ref[:, wide] = pick(choose, out_ref[:, wide])
         for copy in leave_late(h):
@@ -310,7 +321,7 @@
             pltpu.HBM(wide, BF16),
             pltpu.HBM(wide, BF16),
             pltpu.HBM((RANKS * ROWS, KEY_VALUE_HEADS * PAIR), BF16),
-            pltpu.HBM((KEY_VALUE_HEADS * 2 * SHARED, ROWS), F32),
+            pltpu.HBM((KEY_VALUE_HEADS, 2, SHARED * ROWS), F32),
         ],
         scratch_shapes=[
             pltpu.VMEM(wide, BF16),
@@ -318,7 +329,7 @@
             pltpu.VMEM(wide, BF16),
             pltpu.VMEM(wide, BF16),
             pltpu.VMEM((RANKS * ROWS, KEY_VALUE_HEADS * PAIR), BF16),
-            pltpu.VMEM((KEY_VALUE_HEADS * 2 * SHARED, ROWS), F32),
+            pltpu.VMEM((KEY_VALUE_HEADS, 2, SHARED * ROWS), F32),
             pltpu.VMEM((ROWS, ROWS), BF16),
             pltpu.VMEM((ROWS, ROWS), BF16),
             pltpu.VMEM((RANKS * ROWS, ROWS), F32),
@@ -381,28 +392,20 @@
                 k = pairs_ref[window, k_columns]
                 v = pairs_ref[window, v_columns]
                 k_turned = k.T
-                stats = stats_ref[pl.ds(pl.multiple_of(h * 2 * SHARED, 2 * SHARED), 2 * SHARED), :]
-                lows, grads, queries, gradients = [], [], [], []
-                for i in range(SHARED):
-                    columns = part(h, i * HEAD_SIZE, HEAD_SIZE, WIDE)
-                    q, g = q_ref[:, columns], g_ref[:, columns]
-                    logits = lax.dot_general(k, q, INNER, preferred_element_type=F32)
-                    weights = jnp.exp2(logits * EXP2_FACTOR - stats[i : i + 1, :] + mask[window, :])
-                    grad_weights = lax.dot_general(v, g, INNER, preferred_element_type=F32)
-                    inner = stats[SHARED + i : SHARED + i + 1, :]
-                    grad_logits = (weights * (grad_weights - inner)).astype(BF16)
-                    dq = jnp.dot(k_turned, grad_logits, preferred_element_type=F32) * FACTOR
-                    dq_ref[:, columns] = dq.astype(BF16).T
-                    lows.append(weights.astype(BF16))
-                    grads.append(grad_logits)
-                    queries.append(q)
-                    gradients.append(g)
-                dk = jnp.dot(
-                    jnp.concatenate(grads, axis=1), jnp.concatenate(queries, axis=0), preferred_element_type=F32
-                )
-                dv = jnp.dot(
-                    jnp.concatenate(lows, axis=1), jnp.concatenate(gradients, axis=0), preferred_element_type=F32
-                )
+                heads = [part(h, i * HEAD_SIZE, HEAD_SIZE, WIDE) for i in range(SHARED)]
+                q = jnp.concatenate([q_ref[:, columns] for columns in heads], axis=0)
+                g = jnp.concatenate([g_ref[:, columns] for columns in heads], axis=0)
+                stats = stats_ref[h]
+                logits = lax.dot_general(k, q, INNER, preferred_element_type=F32)
+                allowed = jnp.concatenate([mask[window, :]] * SHARED, axis=1)
+                weights = jnp.exp2(logits * EXP2_FACTOR - stats[0:1] + allowed)
+                grad_weights = lax.dot_general(v, g, INNER, preferred_element_type=F32)
+                grad_logits = (weights * (grad_weights - stats[1:2])).astype(BF16)
+                dq = (jnp.dot(k_turned, grad_logits, preferred_element_type=F32) * FACTOR).astype(BF16)
+                for i, columns in enumerate(heads):
+                    dq_ref[:, columns] = dq[:, i * ROWS : (i + 1) * ROWS].T
+                dk = jnp.dot(grad_logits, q, preferred_element_type=F32)
+                dv = jnp.dot(weights.astype(BF16), g, preferred_element_type=F32)
                 total[window, k_columns] = (dk * FACTOR).astype(BF16)
                 total[window, v_columns] = dv.astype(BF16)
 
@@ -595,10 +598,8 @@
     return array, beside(array), far, beside(far)
 
 
-def collect(keep, send):
-    near = beside(send)
-    partial = (keep[1].astype(F32) + near[1].astype(F32)).astype(BF16)
-    return keep, near, across(partial)
+def partial_sum(keep, near):
+    return (keep[1].astype(F32) + near[1].astype(F32)).astype(BF16)
 
 
 def body(queries, keys, values, cotangent, doc_ids, partners, swap_slots):
@@ -611,21 +612,28 @@
         [doc_ids.reshape(ROWS), slots, rank, jnp.zeros((META - ROWS - ROUNDS - 1,), jnp.int32)]
     )
 
+    stay = staying(slot, k, v)
+    stay_far = across(stay)
+    send = outgoing(mate, slot, q, k, v, g)
+    send, stay_far = lax.optimization_barrier((send, stay_far))
+    landed = exchange(send)
+    stays = stay, beside(stay), stay_far, beside(stay_far)
     metas = meta, beside(meta), across(meta), lax.ppermute(meta, "sp", [(i, i ^ 3) for i in range(RANKS)])
-    send, stay = outgoing(mate, slot, q, k, v, g)
-    send, metas = lax.optimization_barrier((send, metas))
-    landed = exchange(send)
-    stays = spread(stay)
-    landed, stays = lax.optimization_barrier((landed, stays))
+    landed, stays, metas = lax.optimization_barrier((landed, stays, metas))
     turns = spread(traded_pairs(mate, landed))
     out, send, *kept = forward(mate, metas, q, g, landed, stays, turns)
     landed_out = exchange(send)
     dq, send, turn_keep, turn_send, stay_keep, stay_send = backward(mate, metas, *kept)
     landed_out, turn_send = lax.optimization_barrier((landed_out, turn_send))
-    send = returning(mate, send, *collect(turn_keep, turn_send))
+    turn_near = beside(turn_send)
+    turn_far = across(partial_sum(turn_keep, turn_near))
+    stay_near = beside(stay_send)
+    stay_far = across(partial_sum(stay_keep, stay_near))
+    send = returning(mate, send, turn_keep, turn_near, turn_far)
+    send, stay_far = lax.optimization_barrier((send, stay_far))
     landed = exchange(send)
     attended = merge(mate, slot, out, landed_out)
-    grad_q, grad_k, grad_v = finish(mate, slot, dq, landed, *collect(stay_keep, stay_send))
+    grad_q, grad_k, grad_v = finish(mate, slot, dq, landed, stay_keep, stay_near, stay_far)
     return attended[None], grad_q[None], grad_k[None], grad_v[None]
 
 

time: 159 us -> 151 us (0.950)
  waiting for transfers between devices: 75.2 us -> 64.6 us
  starting transfers between devices: 38.8 us -> 44.5 us
  Pallas kernels: 41.8 us -> 38.5 us
    ppermute x5, waiting for transfers between devices: 65.2 us -> 9.47 us  [across(): return lax.ppermute(array, 'sp', [(i, i ^ 2) for i in range(RANKS)])]
    all_to_all x3, waiting for transfers between devices: 4.27 us -> 41.4 us  [exchange(): lax.all_to_all(blocks, 'dp', split_axis=0, concat_axis=0, tiled=True)]
    ppermute x1, waiting for transfers between devices: 0.01 us -> 10.9 us  [body(): lax.ppermute(meta, 'sp', [(i, i ^ 3) for i in range(RANKS)])]
    ppermute x7, starting transfers between devices: 6.04 us -> 11.7 us  [beside(): return lax.ppermute(array, 'sp', [(i, i ^ 1) for i in range(RANKS)])]
    ppermute x5, starting transfers between devices: 8.95 us -> 13.5 us  [across(): return lax.ppermute(array, 'sp', [(i, i ^ 2) for i in range(RANKS)])]
    pallas_call x1, Pallas kernels: 13 us -> 9.66 us  [forward(): pl.pallas_call(forward_kernel, in_specs=[SMEM] * 5 + [VMEM] * 4 + [HBM] *...]
    all_to_all x3, starting transfers between devices: 18.9 us -> 15.7 us  [exchange(): lax.all_to_all(blocks, 'dp', split_axis=0, concat_axis=0, tiled=True)]
    ppermute x7, waiting for transfers between devices: 5.69 us -> 2.89 us  [beside(): return lax.ppermute(array, 'sp', [(i, i ^ 1) for i in range(RANKS)])]
  transfers between devices with their start and end apart: 16 -> 16, of which waited for: 9 -> 9; matrix products, arithmetic and copies ran while one was open for 1% -> 1% of each run, Pallas kernels for 14% -> 15%
where the time goes in v2:
time: 151 us; the launch traced here: 150 us
  waiting for transfers between devices  64.6 us (43%)
  starting transfers between devices  44.5 us (29%)
  Pallas kernels  38.5 us (25%)
    all_to_all x3, waiting for transfers between devices, exchange(): lax.all_to_all(blocks, 'dp', split_axis=0, concat_axis=0, tiled=True)  41.4 us
    all_to_all x3, starting transfers between devices, exchange(): lax.all_to_all(blocks, 'dp', split_axis=0, concat_axis=0, tiled=True)  15.7 us
    ppermute x5, starting transfers between devices, across(): return lax.ppermute(array, 'sp', [(i, i ^ 2) for i in range(RANKS)])  13.5 us
    ppermute x7, starting transfers between devices, beside(): return lax.ppermute(array, 'sp', [(i, i ^ 1) for i in range(RANKS)])  11.7 us
    pallas_call x1, Pallas kernels, backward(): pl.pallas_call(backward_kernel, in_specs=[SMEM] * 5 + [VMEM] * 4 + [HBM]...  11.6 us
    ppermute x1, waiting for transfers between devices, body(): lax.ppermute(meta, 'sp', [(i, i ^ 3) for i in range(RANKS)])  10.9 us
    pallas_call x1, Pallas kernels, forward(): pl.pallas_call(forward_kernel, in_specs=[SMEM] * 5 + [VMEM] * 4 + [HBM] *...  9.66 us
    ppermute x5, waiting for transfers between devices, across(): return lax.ppermute(array, 'sp', [(i, i ^ 2) for i in range(RANKS)])  9.47 us
  transfers between devices with their start and end apart: 16, of which 9 were waited for; matrix products, arithmetic and copies ran while one was open for 1% of the time, Pallas kernels for 15%

profile of v2, /device:TPU:1, one launch (start us, length us, event | category | flops | bytes accessed | tf_op | source)
XLA Modules:
  0.0 149.8 jit_solution(15716863023846846069)
XLA Ops:
  0.6 1.9 %staying.1.stay_own = bf16[128,1024]{1,0:T(8,128)(2,1)S(1)} custom-call(s32[16]{0:T(128)} %bitcast.44, bf16[256,512]{1,0:T(8,128)(2,1)} %bitcast.29, bf16[256,512]{1,0:T(8,128)(2,1)} %bitcast.31), custom_call_target="tpu_custom_call" | custom-call | flops 100000000 | bytes 1000000 | tf_op jit(solution)/shard_map/staying/pallas_call | solution.py:144
  2.6 4.5 %collective-permute-start = (bf16[128,1024]{1,0:T(8,128)(2,1)S(1)}, bf16[128,1024]{1,0:T(8,128)(2,1)S(1)}, u32[]{:S(2)}, u32[]{:S(2)}) collective-permute-start(bf16[128,1024]{1,0:T(8,128)(2,1)S(1)} %staying.1.stay_own), channel_id=1, source_target_pairs={{0,2},{1,3},{2,0},{3,1},{4,6},{5,7},{6,4},{7,5},{8,10},{9,11},{10,... | collective-permute-start | bytes 786440 | tf_op jit(solution)/shard_map/ppermute | solution.py:589
  7.1 4.8 %outgoing.1 = bf16[256,5120]{1,0:T(8,128)(2,1)} custom-call(s32[16]{0:T(128)} %bitcast.37, s32[16]{0:T(128)} %bitcast.45, bf16[256,2048]{1,0:T(8,128)(2,1)} %bitcast.33, bf16[256,512]{1,0:T(8,128)(2,1)} %bitcast.30, bf16[256,512]{1,0:T(8,128)(2,1)} %bitcast.32, bf16[256,2048]{1,0:T(8,128)(2,1)} %bitcast.35), custom_call_target="tpu_custom_call" | custom-call | flops 1000000000 | bytes 5000000 | tf_op jit(solution)/shard_map/outgoing/pallas_call | solution.py:168
  11.9 1.3 collective-permute-done.stay_far
  13.1 0.0 copy-start
  13.1 0.0 copy-start.1
  13.1 7.6 %all-to-all-start = ((bf16[32,8,5120]{2,1,0:T(8,128)(2,1)}), bf16[32,8,5120]{2,1,0:T(8,128)(2,1)S(1)}, u32[]{:S(2)}, u32[]{:S(2)}) async-start(bf16[32,8,5120]{2,1,0:T(8,128)(2,1)} %bitcast.26), calls=%async_computation | async-start | bytes 5242880 | tf_op jit(solution)/shard_map/all_to_all | solution.py:585
  20.7 1.9 %collective-permute-start.1 = (bf16[128,1024]{1,0:T(8,128)(2,1)S(1)}, bf16[128,1024]{1,0:T(8,128)(2,1)S(1)}, u32[]{:S(2)}, u32[]{:S(2)}) collective-permute-start(bf16[128,1024]{1,0:T(8,128)(2,1)S(1)} %staying.1.stay_own), channel_id=1, source_target_pairs={{0,1},{1,0},{2,3},{3,2},{4,5},{5,4},{6,7},{7,6},{8,9},{9,8},{10,11... | collective-permute-start | bytes 786440 | tf_op jit(solution)/shard_map/ppermute | solution.py:593
  22.6 0.1 collective-permute-start.2
  22.7 0.0 copy-done
  22.7 0.0 copy-done.1
  22.7 0.1 pad_add_fusion.meta_own
  22.8 3.6 %collective-permute-start.5 = (s32[384]{0:T(512)S(1)}, s32[384]{0:T(512)S(1)}, u32[]{:S(2)}, u32[]{:S(2)}) collective-permute-start(s32[384]{0:T(512)S(1)} %pad_add_fusion.meta_own), channel_id=1, source_target_pairs={{0,3},{1,2},{2,1},{3,0},{4,7},{5,6},{6,5},{7,4},{8,11},{9,10},{10,... | collective-permute-start | bytes 4616 | tf_op jit(solution)/shard_map/ppermute | solution.py:621
  26.4 0.0 collective-permute-start.4
  26.4 0.5 collective-permute-start.3
  26.9 10.9 %collective-permute-done.5.meta_both = s32[384]{0:T(512)S(1)} collective-permute-done((s32[384]{0:T(512)S(1)}, s32[384]{0:T(512)S(1)}, u32[]{:S(2)}, u32[]{:S(2)}) %collective-permute-start.5) | collective-permute-done | bytes 1568 | tf_op jit(solution)/shard_map/ppermute | solution.py:621
  37.8 0.0 collective-permute-done.4.meta_far
  37.8 0.0 collective-permute-done.3.meta_near
  37.8 0.0 collective-permute-done.1.stay_near
  37.8 0.0 collective-permute-done.2.stay_both
  37.8 16.5 %all-to-all-done = bf16[32,8,5120]{2,1,0:T(8,128)(2,1)S(1)} async-done(((bf16[32,8,5120]{2,1,0:T(8,128)(2,1)}), bf16[32,8,5120]{2,1,0:T(8,128)(2,1)S(1)}, u32[]{:S(2)}, u32[]{:S(2)}) %all-to-all-start) | async-done | bytes 2621472 | tf_op jit(solution)/shard_map/all_to_all | solution.py:585
  54.3 0.9 traded_pairs.1.turn_own
  55.2 3.4 %collective-permute-start.7 = (bf16[128,1024]{1,0:T(8,128)(2,1)S(1)}, bf16[128,1024]{1,0:T(8,128)(2,1)S(1)}, u32[]{:S(2)}, u32[]{:S(2)}) collective-permute-start(bf16[128,1024]{1,0:T(8,128)(2,1)S(1)} %traded_pairs.1.turn_own), channel_id=1, source_target_pairs={{0,2},{1,3},{2,0},{3,1},{4,6},{5,7},{6,4},{7,5},{8,10},{9,11},{10,... | collective-permute-start | bytes 786440 | tf_op jit(solution)/shard_map/ppermute | solution.py:589
  58.6 4.2 %collective-permute-start.6 = (bf16[128,1024]{1,0:T(8,128)(2,1)S(1)}, bf16[128,1024]{1,0:T(8,128)(2,1)S(1)}, u32[]{:S(2)}, u32[]{:S(2)}) collective-permute-start(bf16[128,1024]{1,0:T(8,128)(2,1)S(1)} %traded_pairs.1.turn_own), channel_id=1, source_target_pairs={{0,1},{1,0},{2,3},{3,2},{4,5},{5,4},{6,7},{7,6},{8,9},{9,8},{10,11... | collective-permute-start | bytes 786440 | tf_op jit(solution)/shard_map/ppermute | solution.py:593
  62.8 0.0 collective-permute-done.7.turn_far
  62.8 4.3 %collective-permute-start.8 = (bf16[128,1024]{1,0:T(8,128)(2,1)S(1)}, bf16[128,1024]{1,0:T(8,128)(2,1)S(1)}, u32[]{:S(2)}, u32[]{:S(2)}) collective-permute-start(bf16[128,1024]{1,0:T(8,128)(2,1)S(1)} %collective-permute-done.7.turn_far), channel_id=1, source_target_pairs={{0,1},{1,0},{2,3},{3,2},{4,5},{5,4},{6,7},{7,6},{8,9},{9,8},{10,11... | collective-permute-start | bytes 786440 | tf_op jit(solution)/shard_map/ppermute | solution.py:593
  67.1 0.0 collective-permute-done.6.turn_near
  67.1 1.1 collective-permute-done.8.turn_both
  68.3 9.7 %forward.1 = (bf16[256,2048]{1,0:T(8,128)(2,1)}, bf16[256,2048]{1,0:T(8,128)(2,1)}, bf16[256,2048]{1,0:T(8,128)(2,1)}, bf16[256,2048]{1,0:T(8,128)(2,1)}, bf16[1...) custom-call(s32[16]{0:T(128)} %bitcast.39, s32[384]{0:T(512)S(1)} %pad_add_fusion.meta_own, ...), custom_call_target="tpu_custom_call" | custom-call | flops 4000000000 | bytes 10000000 | tf_op jit(solution)/shard_map/forward/pallas_call | solution.py:314
  78.0 4.1 %all-to-all-start.1 = ((bf16[32,8,2048]{2,1,0:T(8,128)(2,1)}), bf16[32,8,2048]{2,1,0:T(8,128)(2,1)S(1)}, u32[]{:S(2)}, u32[]{:S(2)}) async-start(bf16[32,8,2048]{2,1,0:T(8,128)(2,1)} %bitcast.27), calls=%async_computation.1 | async-start | bytes 2097152 | tf_op jit(solution)/shard_map/all_to_all | solution.py:585
  82.1 11.6 %backward.1 = (bf16[256,2048]{1,0:T(8,128)(2,1)}, bf16[256,2048]{1,0:T(8,128)(2,1)S(1)}, bf16[2,128,1024]{2,1,0:T(8,128)(2,1)S(1)}, bf16[2,128,1024]{2,1,0:T(8,1...) custom-call(s32[16]{0:T(128)} %bitcast.40, s32[384]{0:T(512)S(1)} %pad_add_fusion.meta_own, ...), custom_call_target="tpu_custom_call" | custom-call | flops 8000000000 | bytes 10000000 | tf_op jit(solution)/shard_map/backward/pallas_call | solution.py:437
  93.7 6.5 %all-to-all-done.1 = bf16[32,8,2048]{2,1,0:T(8,128)(2,1)S(1)} async-done(((bf16[32,8,2048]{2,1,0:T(8,128)(2,1)}), bf16[32,8,2048]{2,1,0:T(8,128)(2,1)S(1)}, u32[]{:S(2)}, u32[]{:S(2)}) %all-to-all-start.1) | async-done | bytes 1048608 | tf_op jit(solution)/shard_map/all_to_all | solution.py:585
  100.2 0.7 collective-permute-start.9
  100.9 0.0 collective-permute-start.11
  100.9 1.7 %collective-permute-done.9.near_ref = bf16[2,128,1024]{2,1,0:T(8,128)(2,1)S(1)} collective-permute-done((bf16[2,128,1024]{2,1,0:T(8,128)(2,1)}, bf16[2,128,1024]{2,1,0:T(8,128)(2,1)S(1)}, u32[]{:S(2)}, u32[]{:S(2)}) %collective-permute-start.9) | collective-permute-done | bytes 524320 | tf_op jit(solution)/shard_map/ppermute | solution.py:593
  102.7 0.1 fusion
  102.7 4.9 %collective-permute-start.10 = (bf16[128,1024]{1,0:T(8,128)(2,1)S(1)}, bf16[128,1024]{1,0:T(8,128)(2,1)S(1)}, u32[]{:S(2)}, u32[]{:S(2)}) collective-permute-start(bf16[128,1024]{1,0:T(8,128)(2,1)S(1)} %fusion), channel_id=1, source_target_pairs={{0,2},{1,3},{2,0},{3,1},{4,6},{5,7},{6,4},{7,5},{8,10},{9,11},{10,... | collective-permute-start | bytes 786440 | tf_op jit(solution)/shard_map/ppermute | solution.py:589
  107.7 0.0 collective-permute-done.11.near_ref
  107.7 1.0 fusion.1
  108.7 0.7 collective-permute-start.12
  109.4 4.8 %collective-permute-done.10.far_ref = bf16[128,1024]{1,0:T(8,128)(2,1)S(1)} collective-permute-done((bf16[128,1024]{1,0:T(8,128)(2,1)S(1)}, bf16[128,1024]{1,0:T(8,128)(2,1)S(1)}, u32[]{:S(2)}, u32[]{:S(2)}) %collective-permute-start.10) | collective-permute-done | bytes 262176 | tf_op jit(solution)/shard_map/ppermute | solution.py:589
  114.1 2.2 %returning.1 = bf16[256,3072]{1,0:T(8,128)(2,1)} custom-call(s32[16]{0:T(128)} %bitcast.41, bf16[256,2048]{1,0:T(8,128)(2,1)S(1)} %get-tuple-element.54.dq_ref, bf16[2,128,1024]{2,1,0:T(8,128)(2,1)S(1)} %get-tuple-element.55.own_ref, bf16[2,128,1024]{2,1,0:T(8,128)(2,1)S(1)} %collective-permute-done.9.near_ref, ...), custom_call_target="tpu_custom_call" | custom-call | flops 100000000 | bytes 1000000 | tf_op jit(solution)/shard_map/returning/pallas_call | solution.py:485
  116.3 3.4 %collective-permute-done.12.far_ref = bf16[128,1024]{1,0:T(8,128)(2,1)S(1)} collective-permute-done((bf16[128,1024]{1,0:T(8,128)(2,1)S(1)}, bf16[128,1024]{1,0:T(8,128)(2,1)S(1)}, u32[]{:S(2)}, u32[]{:S(2)}) %collective-permute-start.12) | collective-permute-done | bytes 262176 | tf_op jit(solution)/shard_map/ppermute | solution.py:589
  119.8 4.0 %all-to-all-start.2 = ((bf16[32,8,3072]{2,1,0:T(8,128)(2,1)}), bf16[32,8,3072]{2,1,0:T(8,128)(2,1)S(1)}, u32[]{:S(2)}, u32[]{:S(2)}) async-start(bf16[32,8,3072]{2,1,0:T(8,128)(2,1)} %bitcast.15), calls=%async_computation.2 | async-start | bytes 3145728 | tf_op jit(solution)/shard_map/all_to_all | solution.py:585
  123.7 4.0 %merge.1 = bf16[256,2048]{1,0:T(8,128)(2,1)} custom-call(s32[16]{0:T(128)} %bitcast.42, s32[16]{0:T(128)} %bitcast.46, bf16[256,2048]{1,0:T(8,128)(2,1)} %get-tuple-element.45.own_ref, bf16[256,2048]{1,0:T(8,128)(2,1)S(1)} %bitcast.25), custom_call_target="tpu_custom_call" | custom-call | flops 500000000 | bytes 3000000 | tf_op jit(solution)/shard_map/merge/pallas_call | solution.py:508
  127.7 18.4 %all-to-all-done.2 = bf16[32,8,3072]{2,1,0:T(8,128)(2,1)S(1)} async-done(((bf16[32,8,3072]{2,1,0:T(8,128)(2,1)}), bf16[32,8,3072]{2,1,0:T(8,128)(2,1)S(1)}, u32[]{:S(2)}, u32[]{:S(2)}) %all-to-all-start.2) | async-done | bytes 1572896 | tf_op jit(solution)/shard_map/all_to_all | solution.py:585
  146.1 3.5 %finish.1 = (bf16[256,2048]{1,0:T(8,128)(2,1)}, bf16[256,512]{1,0:T(8,128)(2,1)}, bf16[256,512]{1,0:T(8,128)(2,1)}) custom-call(s32[16]{0:T(128)} %bitcast.43, s32[16]{0:T(128)} %bitcast.47, bf16[256,2048]{1,0:T(8,128)(2,1)} %get-tuple-element.53.dq_hbm, bf16[256,3072]{1,0:T(8,128)(2,1)S(1)} %bitcast.24, bf16[2,128,1024]{2,1,0:T(8,128)(2,1)} %get-tuple-element.57.own_hbm, ...), custom_call_target="tpu_custom_call" | custom-call | flops 800000000 | bytes 5000000 | tf_op jit(solution)/shard_map/finish/pallas_call | solution.py:564
  (5 shorter events, 0.0 us)
Async XLA Ops:
  2.6 10.5 %collective-permute-start = (bf16[128,1024]{1,0:T(8,128)(2,1)S(1)}, bf16[128,1024]{1,0:T(8,128)(2,1)S(1)}, u32[]{:S(2)}, u32[]{:S(2)}) collective-permute-start(bf16[128,1024]{1,0:T(8,128)(2,1)S(1)} %staying.1.stay_own), channel_id=1, source_target_pairs={{0,2},{1,3},{2,0},{3,1},{4,6},{5,7},{6,4},{7,5},{8,10},{9,11},{10,... | collective-permute-start | bytes 786440 | tf_op jit(solution)/shard_map/ppermute | solution.py:589
  13.1 9.6 %copy-start = (s32[1,1,16]{2,1,0:T(1,128)S(1)}, s32[1,1,16]{2,1,0:T(1,128)}, u32[]{:S(2)}) copy-start(s32[1,1,16]{2,1,0:T(1,128)} %param.13) | copy-start | bytes 196
  13.1 9.6 %copy-start.1 = (s32[1,256]{1,0:T(1,128)S(1)}, s32[1,256]{1,0:T(1,128)}, u32[]{:S(2)}) copy-start(s32[1,256]{1,0:T(1,128)} %param.11) | copy-start | bytes 3076
  13.1 41.2 %all-to-all-start = ((bf16[32,8,5120]{2,1,0:T(8,128)(2,1)}), bf16[32,8,5120]{2,1,0:T(8,128)(2,1)S(1)}, u32[]{:S(2)}, u32[]{:S(2)}) async-start(bf16[32,8,5120]{2,1,0:T(8,128)(2,1)} %bitcast.26), calls=%async_computation | async-start | bytes 5242880 | tf_op jit(solution)/shard_map/all_to_all | solution.py:585
  20.7 17.1 %collective-permute-start.1 = (bf16[128,1024]{1,0:T(8,128)(2,1)S(1)}, bf16[128,1024]{1,0:T(8,128)(2,1)S(1)}, u32[]{:S(2)}, u32[]{:S(2)}) collective-permute-start(bf16[128,1024]{1,0:T(8,128)(2,1)S(1)} %staying.1.stay_own), channel_id=1, source_target_pairs={{0,1},{1,0},{2,3},{3,2},{4,5},{5,4},{6,7},{7,6},{8,9},{9,8},{10,11... | collective-permute-start | bytes 786440 | tf_op jit(solution)/shard_map/ppermute | solution.py:593
  22.6 15.2 %collective-permute-start.2 = (bf16[128,1024]{1,0:T(8,128)(2,1)S(1)}, bf16[128,1024]{1,0:T(8,128)(2,1)}, u32[]{:S(2)}, u32[]{:S(2)}) collective-permute-start(bf16[128,1024]{1,0:T(8,128)(2,1)S(1)} %collective-permute-done.stay_far), channel_id=1, source_target_pairs={{0,1},{1,0},{2,3},{3,2},{4,5},{5,4},{6,7},{7,6},{8,9},{9,8},{10,11... | collective-permute-start | bytes 786440 | tf_op jit(solution)/shard_map/ppermute | solution.py:593
  22.8 15.0 %collective-permute-start.5 = (s32[384]{0:T(512)S(1)}, s32[384]{0:T(512)S(1)}, u32[]{:S(2)}, u32[]{:S(2)}) collective-permute-start(s32[384]{0:T(512)S(1)} %pad_add_fusion.meta_own), channel_id=1, source_target_pairs={{0,3},{1,2},{2,1},{3,0},{4,7},{5,6},{6,5},{7,4},{8,11},{9,10},{10,... | collective-permute-start | bytes 4616 | tf_op jit(solution)/shard_map/ppermute | solution.py:621
  26.4 11.3 %collective-permute-start.4 = (s32[384]{0:T(512)S(1)}, s32[384]{0:T(512)S(1)}, u32[]{:S(2)}, u32[]{:S(2)}) collective-permute-start(s32[384]{0:T(512)S(1)} %pad_add_fusion.meta_own), channel_id=1, source_target_pairs={{0,2},{1,3},{2,0},{3,1},{4,6},{5,7},{6,4},{7,5},{8,10},{9,11},{10,... | collective-permute-start | bytes 4616 | tf_op jit(solution)/shard_map/ppermute | solution.py:589
  26.4 11.3 %collective-permute-start.3 = (s32[384]{0:T(512)S(1)}, s32[384]{0:T(512)S(1)}, u32[]{:S(2)}, u32[]{:S(2)}) collective-permute-start(s32[384]{0:T(512)S(1)} %pad_add_fusion.meta_own), channel_id=1, source_target_pairs={{0,1},{1,0},{2,3},{3,2},{4,5},{5,4},{6,7},{7,6},{8,9},{9,8},{10,11... | collective-permute-start | bytes 4616 | tf_op jit(solution)/shard_map/ppermute | solution.py:593
  55.2 7.5 %collective-permute-start.7 = (bf16[128,1024]{1,0:T(8,128)(2,1)S(1)}, bf16[128,1024]{1,0:T(8,128)(2,1)S(1)}, u32[]{:S(2)}, u32[]{:S(2)}) collective-permute-start(bf16[128,1024]{1,0:T(8,128)(2,1)S(1)} %traded_pairs.1.turn_own), channel_id=1, source_target_pairs={{0,2},{1,3},{2,0},{3,1},{4,6},{5,7},{6,4},{7,5},{8,10},{9,11},{10,... | collective-permute-start | bytes 786440 | tf_op jit(solution)/shard_map/ppermute | solution.py:589
  58.6 8.5 %collective-permute-start.6 = (bf16[128,1024]{1,0:T(8,128)(2,1)S(1)}, bf16[128,1024]{1,0:T(8,128)(2,1)S(1)}, u32[]{:S(2)}, u32[]{:S(2)}) collective-permute-start(bf16[128,1024]{1,0:T(8,128)(2,1)S(1)} %traded_pairs.1.turn_own), channel_id=1, source_target_pairs={{0,1},{1,0},{2,3},{3,2},{4,5},{5,4},{6,7},{7,6},{8,9},{9,8},{10,11... | collective-permute-start | bytes 786440 | tf_op jit(solution)/shard_map/ppermute | solution.py:593
  62.8 5.5 %collective-permute-start.8 = (bf16[128,1024]{1,0:T(8,128)(2,1)S(1)}, bf16[128,1024]{1,0:T(8,128)(2,1)S(1)}, u32[]{:S(2)}, u32[]{:S(2)}) collective-permute-start(bf16[128,1024]{1,0:T(8,128)(2,1)S(1)} %collective-permute-done.7.turn_far), channel_id=1, source_target_pairs={{0,1},{1,0},{2,3},{3,2},{4,5},{5,4},{6,7},{7,6},{8,9},{9,8},{10,11... | collective-permute-start | bytes 786440 | tf_op jit(solution)/shard_map/ppermute | solution.py:593
  78.0 22.2 %all-to-all-start.1 = ((bf16[32,8,2048]{2,1,0:T(8,128)(2,1)}), bf16[32,8,2048]{2,1,0:T(8,128)(2,1)S(1)}, u32[]{:S(2)}, u32[]{:S(2)}) async-start(bf16[32,8,2048]{2,1,0:T(8,128)(2,1)} %bitcast.27), calls=%async_computation.1 | async-start | bytes 2097152 | tf_op jit(solution)/shard_map/all_to_all | solution.py:585
  100.2 2.5 %collective-permute-start.9 = (bf16[2,128,1024]{2,1,0:T(8,128)(2,1)}, bf16[2,128,1024]{2,1,0:T(8,128)(2,1)S(1)}, u32[]{:S(2)}, u32[]{:S(2)}) collective-permute-start(bf16[2,128,1024]{2,1,0:T(8,128)(2,1)} %get-tuple-element.56), channel_id=1, source_target_pairs={{0,1},{1,0},{2,3},{3,2},{4,5},{5,4},{6,7},{7,6},{8,9},{9,8},{10,11... | collective-permute-start | bytes 1572872 | tf_op jit(solution)/shard_map/ppermute | solution.py:593
  100.9 6.8 %collective-permute-start.11 = (bf16[2,128,1024]{2,1,0:T(8,128)(2,1)}, bf16[2,128,1024]{2,1,0:T(8,128)(2,1)S(1)}, u32[]{:S(2)}, u32[]{:S(2)}) collective-permute-start(bf16[2,128,1024]{2,1,0:T(8,128)(2,1)} %get-tuple-element.58), channel_id=1, source_target_pairs={{0,1},{1,0},{2,3},{3,2},{4,5},{5,4},{6,7},{7,6},{8,9},{9,8},{10,11... | collective-permute-start | bytes 1572872 | tf_op jit(solution)/shard_map/ppermute | solution.py:593
  102.7 11.4 %collective-permute-start.10 = (bf16[128,1024]{1,0:T(8,128)(2,1)S(1)}, bf16[128,1024]{1,0:T(8,128)(2,1)S(1)}, u32[]{:S(2)}, u32[]{:S(2)}) collective-permute-start(bf16[128,1024]{1,0:T(8,128)(2,1)S(1)} %fusion), channel_id=1, source_target_pairs={{0,2},{1,3},{2,0},{3,1},{4,6},{5,7},{6,4},{7,5},{8,10},{9,11},{10,... | collective-permute-start | bytes 786440 | tf_op jit(solution)/shard_map/ppermute | solution.py:589
  108.7 11.1 %collective-permute-start.12 = (bf16[128,1024]{1,0:T(8,128)(2,1)S(1)}, bf16[128,1024]{1,0:T(8,128)(2,1)S(1)}, u32[]{:S(2)}, u32[]{:S(2)}) collective-permute-start(bf16[128,1024]{1,0:T(8,128)(2,1)S(1)} %fusion.1), channel_id=1, source_target_pairs={{0,2},{1,3},{2,0},{3,1},{4,6},{5,7},{6,4},{7,5},{8,10},{9,11},{10,... | collective-permute-start | bytes 786440 | tf_op jit(solution)/shard_map/ppermute | solution.py:589
  119.8 26.3 %all-to-all-start.2 = ((bf16[32,8,3072]{2,1,0:T(8,128)(2,1)}), bf16[32,8,3072]{2,1,0:T(8,128)(2,1)S(1)}, u32[]{:S(2)}, u32[]{:S(2)}) async-start(bf16[32,8,3072]{2,1,0:T(8,128)(2,1)} %bitcast.15), calls=%async_computation.2 | async-start | bytes 3145728 | tf_op jit(solution)/shard_map/all_to_all | solution.py:585

commit v3 on v2

--- a/solution.py
+++ b/solution.py
@@ -20,6 +20,7 @@
 CARGO = 2 * WIDE + PAIR
 META = 384
 KEYS = 128
+TOGETHER = 2
 EARLIER = (RANKS - 1) * ROWS // KEYS
 FACTOR = HEAD_SIZE ** (-0.5)
 EXP2_FACTOR = FACTOR * 1.4426950408889634
@@ -201,11 +202,11 @@
     return jnp.sum(jnp.where(here, row, 0.0), axis=1, keepdims=True)
 
 
-def earlier_blocks(metas, rank):
+def earlier_blocks(metas, rank, keys):
     first = metas[0][0]
     count = jnp.int32(0)
     for x in (1, 2, 3):
-        for last in range(KEYS - 1, ROWS, KEYS):
+        for last in range(keys - 1, ROWS, keys):
             count = count + jnp.where(((rank ^ x) < rank) & (metas[x][last] == first), 1, 0)
     return count
 
@@ -234,7 +235,7 @@
     g_copy.start()
     metas = (meta_own, meta_near, meta_far, meta_both)
     rank = metas[0][ROWS + ROUNDS]
-    count = earlier_blocks(metas, rank)
+    count = earlier_blocks(metas, rank, ROWS)
     mate, slot = scalars(mate_ref, 0, ROUNDS), scalars(metas[0], ROWS, ROUNDS)
     choose = choose_sent(mate, slot)
     bring[...] = choose_landed(mate, slot)
@@ -245,7 +246,7 @@
     for x in range(RANKS):
         other = rank ^ x
 
-        @pl.when((other <= rank) & ((rank - other - 1) * ROWS < count * KEYS))
+        @pl.when((other <= rank) & (rank - other <= count))
         def _(x=x, other=other):
             rows = jnp.concatenate([stay[x][...], turn[x][...]], axis=0)
             place[...] = unpacking(scalars(metas[x], ROWS, ROUNDS))
@@ -264,7 +265,7 @@
     def leave_late(h):
         return [leave(h, 3, out_ref, out_hbm, WIDE), leave(h, 4, send_ref, send_hbm, WIDE)]
 
-    def head(h, carry):
+    def merged(h):
         wide = part(h, 0, WIDE, WIDE)
         came_q = jnp.dot(bring[...], landed_ref[:, part(h, 0, WIDE, CARGO)], preferred_element_type=F32)
         came_g = jnp.dot(bring[...], landed_ref[:, part(h, BUNDLE, WIDE, CARGO)], preferred_element_type=F32)
@@ -273,34 +274,47 @@
         for copy in leave_early(h):
             copy.start()
 
-        for n in range(EARLIER + 1):
-
-            @pl.when(count == n)
-            def _(n=n):
-                window = pl.ds(pl.multiple_of(rank * ROWS - n * KEYS, KEYS), n * KEYS + ROWS)
-                k = pairs_ref[window, part(h, 0, HEAD_SIZE, PAIR)]
-                v_turned = pairs_ref[window, part(h, HEAD_SIZE, HEAD_SIZE, PAIR)].T
-                heads = [part(h, i * HEAD_SIZE, HEAD_SIZE, WIDE) for i in range(SHARED)]
-                q = jnp.concatenate([q_ref[:, columns] for columns in heads], axis=0)
-                g_turned = jnp.concatenate([g_ref[:, columns].T for columns in heads], axis=1)
-                logits = lax.dot_general(k, q, INNER, preferred_element_type=F32)
-                logits = logits + jnp.concatenate([mask[window, :]] * SHARED, axis=1)
-                top = jnp.max(logits, axis=0, keepdims=True)
-                raised = jnp.exp2((logits - top) * EXP2_FACTOR)
-                total = jnp.sum(raised, axis=0, keepdims=True)
-                out = jnp.dot(v_turned, raised.astype(BF16), preferred_element_type=F32) * (1.0 / total)
-                inner = jnp.sum(out * g_turned.astype(F32), axis=0, keepdims=True)
-                out = out.astype(BF16)
-                for i, columns in enumerate(heads):
-                    out_ref[:, columns] = out[:, i * ROWS : (i + 1) * ROWS].T
-                stats_ref[h] = jnp.concatenate([top * EXP2_FACTOR + jnp.log2(total), inner], axis=0)
-
+    def attend(h, n):
+        window = pl.ds(pl.multiple_of(rank * ROWS - n * ROWS, ROWS), n * ROWS + ROWS)
+        k = pairs_ref[window, part(h, 0, HEAD_SIZE, PAIR)]
+        v_turned = pairs_ref[window, part(h, HEAD_SIZE, HEAD_SIZE, PAIR)].T
+        heads = [part(h, i * HEAD_SIZE, HEAD_SIZE, WIDE) for i in range(SHARED)]
+        q = jnp.concatenate([q_ref[:, columns] for columns in heads], axis=0)
+        g_turned = jnp.concatenate([g_ref[:, columns].T for columns in heads], axis=1)
+        logits = lax.dot_general(k, q, INNER, preferred_element_type=F32)
+        logits = logits + jnp.concatenate([mask[window, :]] * SHARED, axis=1)
+        top = jnp.max(logits, axis=0, keepdims=True)
+        raised = jnp.exp2((logits - top) * EXP2_FACTOR)
+        total = jnp.sum(raised, axis=0, keepdims=True)
+        out = jnp.dot(v_turned, raised.astype(BF16), preferred_element_type=F32) * (1.0 / total)
+        inner = jnp.sum(out * g_turned.astype(F32), axis=0, keepdims=True)
+        out = out.astype(BF16)
+        for i, columns in enumerate(heads):
+            out_ref[:, columns] = out[:, i * ROWS : (i + 1) * ROWS].T
+        stats_ref[h] = jnp.concatenate([top * EXP2_FACTOR + jnp.log2(total), inner], axis=0)
+
+    def sent(h):
+        wide = part(h, 0, WIDE, WIDE)
         send_ref[:, wide] = pick(choose, out_ref[:, wide])
         for copy in leave_late(h):
             copy.start()
+
+    def heads_at(step, carry):
+        heads = [step * TOGETHER + i for i in range(TOGETHER)]
+        for h in heads:
+            merged(h)
+        for n in range(RANKS):
+
+            @pl.when(count == n)
+            def _(n=n):
+                for h in heads:
+                    attend(h, n)
+
+        for h in heads:
+            sent(h)
         return carry
 
-    lax.fori_loop(0, KEY_VALUE_HEADS, head, 0)
+    lax.fori_loop(0, KEY_VALUE_HEADS // TOGETHER, heads_at, 0)
     stats_copy = pltpu.make_async_copy(stats_ref, stats_hbm, q_arrived)
     stats_copy.start()
     for h in range(KEY_VALUE_HEADS):
@@ -350,8 +364,8 @@
 def backward_kernel(
     mate_ref, meta_own, meta_near, meta_far, meta_both, ids_own, ids_near, ids_far, ids_both,
     q_hbm, g_hbm, pairs_hbm, stats_hbm,
-    dq_hbm, send_ref, turn_keep, turn_send, keep_hbm, send_hbm,
-    q_ref, g_ref, pairs_ref, stats_ref, dq_ref, stay_keep, stay_send, mask, total, arrived, stats_arrived, left, stay_left,
+    dq_hbm, cargo_hbm, turn_keep, turn_send, keep_hbm, send_hbm,
+    send_ref, q_ref, g_ref, pairs_ref, stats_ref, dq_ref, stay_keep, stay_send, mask, total, arrived, stats_arrived, left, stay_left,
 ):
     def arrive(h, turn, source, target, whole):
         columns = part(h, 0, whole, whole)
@@ -367,14 +381,18 @@
             copy.start()
     metas = (meta_own, meta_near, meta_far, meta_both)
     rank = metas[0][ROWS + ROUNDS]
-    count = earlier_blocks(metas, rank)
+    count = earlier_blocks(metas, rank, KEYS)
     choose = choose_sent(scalars(mate_ref, 0, ROUNDS), scalars(metas[0], ROWS, ROUNDS))
     fill_mask(mask, (ids_own, ids_near, ids_far, ids_both), rank)
     total[...] = jnp.zeros_like(total)
 
     def leave(h):
         columns = part(h, 0, WIDE, WIDE)
-        return pltpu.make_async_copy(dq_ref.at[:, columns], dq_hbm.at[:, columns], left.at[h])
+        cargo = cargo_hbm.at[:, part(h, 0, WIDE, BUNDLE)]
+        return [
+            pltpu.make_async_copy(dq_ref.at[:, columns], dq_hbm.at[:, columns], left.at[0, h]),
+            pltpu.make_async_copy(send_ref.at[:, columns], cargo, left.at[1, h]),
+        ]
 
     stats_copy.wait()
 
@@ -386,13 +404,12 @@
 
             @pl.when(count == n)
             def _(n=n):
-                window = pl.ds(pl.multiple_of(rank * ROWS - n * KEYS, KEYS), n * KEYS + ROWS)
                 k_columns = part(h, 0, HEAD_SIZE, PAIR)
                 v_columns = part(h, HEAD_SIZE, HEAD_SIZE, PAIR)
+                heads = [part(h, i * HEAD_SIZE, HEAD_SIZE, WIDE) for i in range(SHARED)]
+                window = pl.ds(pl.multiple_of(rank * ROWS - n * KEYS, KEYS), n * KEYS + ROWS)
                 k = pairs_ref[window, k_columns]
                 v = pairs_ref[window, v_columns]
-                k_turned = k.T
-                heads = [part(h, i * HEAD_SIZE, HEAD_SIZE, WIDE) for i in range(SHARED)]
                 q = jnp.concatenate([q_ref[:, columns] for columns in heads], axis=0)
                 g = jnp.concatenate([g_ref[:, columns] for columns in heads], axis=0)
                 stats = stats_ref[h]
@@ -401,17 +418,19 @@
                 weights = jnp.exp2(logits * EXP2_FACTOR - stats[0:1] + allowed)
                 grad_weights = lax.dot_general(v, g, INNER, preferred_element_type=F32)
                 grad_logits = (weights * (grad_weights - stats[1:2])).astype(BF16)
-                dq = (jnp.dot(k_turned, grad_logits, preferred_element_type=F32) * FACTOR).astype(BF16)
-                for i, columns in enumerate(heads):
-                    dq_ref[:, columns] = dq[:, i * ROWS : (i + 1) * ROWS].T
                 dk = jnp.dot(grad_logits, q, preferred_element_type=F32)
                 dv = jnp.dot(weights.astype(BF16), g, preferred_element_type=F32)
                 total[window, k_columns] = (dk * FACTOR).astype(BF16)
                 total[window, v_columns] = dv.astype(BF16)
-
-        leave(h).start()
+                dq = jnp.dot(k.T, grad_logits, preferred_element_type=F32)
+                dq = (dq * FACTOR).astype(BF16)
+                for i, columns in enumerate(heads):
+                    dq_ref[:, columns] = dq[:, i * ROWS : (i + 1) * ROWS].T
+
         wide = part(h, 0, WIDE, WIDE)
         send_ref[:, wide] = pick(choose, dq_ref[:, wide])
+        for copy in leave(h):
+            copy.start()
         return carry
 
     lax.fori_loop(0, KEY_VALUE_HEADS, head, 0)
@@ -427,7 +446,9 @@
     ]
     for copy in leaving:
         copy.start()
-    for copy in leaving + [leave(h) for h in range(KEY_VALUE_HEADS)]:
+    for h in range(KEY_VALUE_HEADS):
+        leaving.extend(leave(h))
+    for copy in leaving:
         copy.wait()
 
 
@@ -437,10 +458,10 @@
     return pl.pallas_call(
         backward_kernel,
         in_specs=[SMEM] * 5 + [VMEM] * 4 + [HBM] * 4,
-        out_specs=[HBM, VMEM, VMEM, VMEM, HBM, HBM],
+        out_specs=[HBM, HBM, VMEM, VMEM, HBM, HBM],
         out_shape=[
             pltpu.HBM(wide, BF16),
-            pltpu.VMEM(wide, BF16),
+            pltpu.HBM((ROWS, KEY_VALUE_HEADS * BUNDLE), BF16),
             pltpu.VMEM(piece, BF16),
             pltpu.VMEM(piece, BF16),
             pltpu.HBM(piece, BF16),
@@ -449,6 +470,7 @@
         scratch_shapes=[
             pltpu.VMEM(wide, BF16),
             pltpu.VMEM(wide, BF16),
+            pltpu.VMEM(wide, BF16),
             pltpu.VMEM(pairs.shape, BF16),
             pltpu.VMEM(stats.shape, F32),
             pltpu.VMEM(wide, BF16),
@@ -458,7 +480,7 @@
             pltpu.VMEM(pairs.shape, BF16),
             pltpu.SemaphoreType.DMA((3, KEY_VALUE_HEADS)),
             pltpu.SemaphoreType.DMA,
-            pltpu.SemaphoreType.DMA((KEY_VALUE_HEADS,)),
+            pltpu.SemaphoreType.DMA((2, KEY_VALUE_HEADS)),
             pltpu.SemaphoreType.DMA((2,)),
         ],
         compiler_params=PARAMS,
@@ -470,27 +492,35 @@
     )
 
 
-def returning_kernel(mate_ref, dq_ref, own_ref, near_ref, far_ref, send_ref):
+def returning_kernel(mate_ref, cargo_in, own_ref, near_ref, far_ref, cargo_hbm, pairs_ref, left):
+    del cargo_in
     choose = choose_sent_turns(scalars(mate_ref, 0, ROUNDS))
+    leaving = []
     for h in range(KEY_VALUE_HEADS):
         columns = part(h, 0, PAIR, PAIR)
         total = (
             own_ref[0, :, columns].astype(F32) + near_ref[0, :, columns].astype(F32) + far_ref[:, columns].astype(F32)
         )
-        send_ref[:, part(h, 0, WIDE, BUNDLE)] = dq_ref[:, part(h, 0, WIDE, WIDE)]
-        send_ref[:, part(h, WIDE, PAIR, BUNDLE)] = pick(choose, total.astype(BF16))
-
-
-def returning(mate, dq, own, near, far):
+        pairs_ref[:, columns] = pick(choose, total.astype(BF16))
+        cargo = cargo_hbm.at[:, part(h, WIDE, PAIR, BUNDLE)]
+        leaving.append(pltpu.make_async_copy(pairs_ref.at[:, columns], cargo, left.at[h]))
+        leaving[-1].start()
+    for copy in leaving:
+        copy.wait()
+
+
+def returning(mate, cargo, own, near, far):
     return pl.pallas_call(
         returning_kernel,
-        in_specs=[SMEM] + [VMEM] * 4,
-        out_specs=VMEM,
-        out_shape=pltpu.VMEM((ROWS, KEY_VALUE_HEADS * BUNDLE), BF16),
+        in_specs=[SMEM, HBM] + [VMEM] * 3,
+        out_specs=HBM,
+        out_shape=pltpu.HBM(cargo.shape, BF16),
+        input_output_aliases={1: 0},
+        scratch_shapes=[pltpu.VMEM((ROWS, KEY_VALUE_HEADS * PAIR), BF16), pltpu.SemaphoreType.DMA((KEY_VALUE_HEADS,))],
         compiler_params=PARAMS,
         cost_estimate=pl.CostEstimate(flops=10**8, bytes_accessed=10**6, transcendentals=0),
         name="returning",
-    )(mate, in_vmem(dq), in_vmem(own), in_vmem(near), in_vmem(far))
+    )(mate, in_hbm(cargo), in_vmem(own), in_vmem(near), in_vmem(far))
 
 
 def merge_kernel(mate_ref, slot_ref, own_ref, landed_ref, out_ref, bring, came):
@@ -624,11 +654,10 @@
     out, send, *kept = forward(mate, metas, q, g, landed, stays, turns)
     landed_out = exchange(send)
     dq, send, turn_keep, turn_send, stay_keep, stay_send = backward(mate, metas, *kept)
-    landed_out, turn_send = lax.optimization_barrier((landed_out, turn_send))
-    turn_near = beside(turn_send)
-    turn_far = across(partial_sum(turn_keep, turn_near))
-    stay_near = beside(stay_send)
-    stay_far = across(partial_sum(stay_keep, stay_near))
+    turn_near, stay_near = beside(turn_send), beside(stay_send)
+    partials = partial_sum(turn_keep, turn_near), partial_sum(stay_keep, stay_near)
+    landed_out, partials = lax.optimization_barrier((landed_out, partials))
+    turn_far, stay_far = across(partials[0]), across(partials[1])
     send = returning(mate, send, turn_keep, turn_near, turn_far)
     send, stay_far = lax.optimization_barrier((send, stay_far))
     landed = exchange(send)

time: 151 us -> 150 us (level)
  Pallas kernels: 38.5 us -> 34.1 us
  starting transfers between devices: 44.5 us -> 47.4 us
    all_to_all x3, starting transfers between devices: 15.7 us -> 21.3 us  [exchange(): lax.all_to_all(blocks, 'dp', split_axis=0, concat_axis=0, tiled=True)]
    ppermute x5, starting transfers between devices: 13.5 us -> 10.9 us  [across(): return lax.ppermute(array, 'sp', [(i, i ^ 2) for i in range(RANKS)])]
    all_to_all x3, waiting for transfers between devices: 41.4 us -> 39.2 us  [exchange(): lax.all_to_all(blocks, 'dp', split_axis=0, concat_axis=0, tiled=True)]
    pallas_call x1, Pallas kernels: 11.6 us -> 9.43 us  [backward(): pl.pallas_call(backward_kernel, in_specs=[SMEM] * 5 + [VMEM] * 4 + [HBM]...]
    pallas_call x1, Pallas kernels: 9.66 us -> 7.89 us  [forward(): pl.pallas_call(forward_kernel, in_specs=[SMEM] * 5 + [VMEM] * 4 + [HBM] *...]
  transfers between devices with their start and end apart: 16 -> 16, of which waited for: 9 -> 10; matrix products, arithmetic and copies ran while one was open for 1% -> 1% of each run, Pallas kernels for 15% -> 13%
where the time goes in v3:
time: 150 us; the launch traced here: 148 us
  waiting for transfers between devices  63.4 us (42%)
  starting transfers between devices  47.4 us (32%)
  Pallas kernels  34.1 us (23%)
  other arithmetic  1.86 us (1%)
    all_to_all x3, waiting for transfers between devices, exchange(): lax.all_to_all(blocks, 'dp', split_axis=0, concat_axis=0, tiled=True)  39.2 us
    all_to_all x3, starting transfers between devices, exchange(): lax.all_to_all(blocks, 'dp', split_axis=0, concat_axis=0, tiled=True)  21.3 us
    ppermute x7, starting transfers between devices, beside(): return lax.ppermute(array, 'sp', [(i, i ^ 1) for i in range(RANKS)])  11.6 us
    ppermute x5, starting transfers between devices, across(): return lax.ppermute(array, 'sp', [(i, i ^ 2) for i in range(RANKS)])  10.9 us
    ppermute x1, waiting for transfers between devices, body(): lax.ppermute(meta, 'sp', [(i, i ^ 3) for i in range(RANKS)])  10.9 us
    ppermute x5, waiting for transfers between devices, across(): return lax.ppermute(array, 'sp', [(i, i ^ 2) for i in range(RANKS)])  10.7 us
    pallas_call x1, Pallas kernels, backward(): pl.pallas_call(backward_kernel, in_specs=[SMEM] * 5 + [VMEM] * 4 + [HBM]...  9.43 us
    pallas_call x1, Pallas kernels, forward(): pl.pallas_call(forward_kernel, in_specs=[SMEM] * 5 + [VMEM] * 4 + [HBM] *...  7.89 us
  transfers between devices with their start and end apart: 16, of which 10 were waited for; matrix products, arithmetic and copies ran while one was open for 1% of the time, Pallas kernels for 13%

profile of v3, /device:TPU:1, one launch (start us, length us, event | category | flops | bytes accessed | tf_op | source)
XLA Modules:
  0.0 147.8 jit_solution(15293030092413721821)
XLA Ops:
  0.6 1.9 %staying.1.stay_own = bf16[128,1024]{1,0:T(8,128)(2,1)S(1)} custom-call(s32[16]{0:T(128)} %bitcast.45, bf16[256,512]{1,0:T(8,128)(2,1)} %bitcast.30, bf16[256,512]{1,0:T(8,128)(2,1)} %bitcast.32), custom_call_target="tpu_custom_call" | custom-call | flops 100000000 | bytes 1000000 | tf_op jit(solution)/shard_map/staying/pallas_call | solution.py:145
  2.6 4.5 %collective-permute-start = (bf16[128,1024]{1,0:T(8,128)(2,1)S(1)}, bf16[128,1024]{1,0:T(8,128)(2,1)S(1)}, u32[]{:S(2)}, u32[]{:S(2)}) collective-permute-start(bf16[128,1024]{1,0:T(8,128)(2,1)S(1)} %staying.1.stay_own), channel_id=1, source_target_pairs={{0,2},{1,3},{2,0},{3,1},{4,6},{5,7},{6,4},{7,5},{8,10},{9,11},{10,... | collective-permute-start | bytes 786440 | tf_op jit(solution)/shard_map/ppermute | solution.py:619
  7.1 4.8 %outgoing.1 = bf16[256,5120]{1,0:T(8,128)(2,1)} custom-call(s32[16]{0:T(128)} %bitcast.38, s32[16]{0:T(128)} %bitcast.46, bf16[256,2048]{1,0:T(8,128)(2,1)} %bitcast.34, bf16[256,512]{1,0:T(8,128)(2,1)} %bitcast.31, bf16[256,512]{1,0:T(8,128)(2,1)} %bitcast.33, bf16[256,2048]{1,0:T(8,128)(2,1)} %bitcast.36), custom_call_target="tpu_custom_call" | custom-call | flops 1000000000 | bytes 5000000 | tf_op jit(solution)/shard_map/outgoing/pallas_call | solution.py:169
  11.9 1.3 collective-permute-done.stay_far
  13.1 0.0 copy-start
  13.1 0.0 copy-start.1
  13.1 7.6 %all-to-all-start = ((bf16[32,8,5120]{2,1,0:T(8,128)(2,1)}), bf16[32,8,5120]{2,1,0:T(8,128)(2,1)S(1)}, u32[]{:S(2)}, u32[]{:S(2)}) async-start(bf16[32,8,5120]{2,1,0:T(8,128)(2,1)} %bitcast.26), calls=%async_computation | async-start | bytes 5242880 | tf_op jit(solution)/shard_map/all_to_all | solution.py:615
  20.7 1.9 %collective-permute-start.1 = (bf16[128,1024]{1,0:T(8,128)(2,1)S(1)}, bf16[128,1024]{1,0:T(8,128)(2,1)S(1)}, u32[]{:S(2)}, u32[]{:S(2)}) collective-permute-start(bf16[128,1024]{1,0:T(8,128)(2,1)S(1)} %staying.1.stay_own), channel_id=1, source_target_pairs={{0,1},{1,0},{2,3},{3,2},{4,5},{5,4},{6,7},{7,6},{8,9},{9,8},{10,11... | collective-permute-start | bytes 786440 | tf_op jit(solution)/shard_map/ppermute | solution.py:623
  22.6 0.1 collective-permute-start.2
  22.7 0.0 copy-done
  22.7 0.0 copy-done.1
  22.7 0.1 pad_add_fusion.meta_own
  22.8 3.6 %collective-permute-start.5 = (s32[384]{0:T(512)S(1)}, s32[384]{0:T(512)S(1)}, u32[]{:S(2)}, u32[]{:S(2)}) collective-permute-start(s32[384]{0:T(512)S(1)} %pad_add_fusion.meta_own), channel_id=1, source_target_pairs={{0,3},{1,2},{2,1},{3,0},{4,7},{5,6},{6,5},{7,4},{8,11},{9,10},{10,... | collective-permute-start | bytes 4616 | tf_op jit(solution)/shard_map/ppermute | solution.py:651
  26.4 0.0 collective-permute-start.4
  26.4 0.5 collective-permute-start.3
  26.9 10.9 %collective-permute-done.5.meta_both = s32[384]{0:T(512)S(1)} collective-permute-done((s32[384]{0:T(512)S(1)}, s32[384]{0:T(512)S(1)}, u32[]{:S(2)}, u32[]{:S(2)}) %collective-permute-start.5) | collective-permute-done | bytes 1568 | tf_op jit(solution)/shard_map/ppermute | solution.py:651
  37.8 0.0 collective-permute-done.4.meta_far
  37.8 0.0 collective-permute-done.3.meta_near
  37.8 0.0 collective-permute-done.1.stay_near
  37.8 0.0 collective-permute-done.2.stay_both
  37.8 16.5 %all-to-all-done = bf16[32,8,5120]{2,1,0:T(8,128)(2,1)S(1)} async-done(((bf16[32,8,5120]{2,1,0:T(8,128)(2,1)}), bf16[32,8,5120]{2,1,0:T(8,128)(2,1)S(1)}, u32[]{:S(2)}, u32[]{:S(2)}) %all-to-all-start) | async-done | bytes 2621472 | tf_op jit(solution)/shard_map/all_to_all | solution.py:615
  54.3 0.9 traded_pairs.1.turn_own
  55.2 3.4 %collective-permute-start.7 = (bf16[128,1024]{1,0:T(8,128)(2,1)S(1)}, bf16[128,1024]{1,0:T(8,128)(2,1)S(1)}, u32[]{:S(2)}, u32[]{:S(2)}) collective-permute-start(bf16[128,1024]{1,0:T(8,128)(2,1)S(1)} %traded_pairs.1.turn_own), channel_id=1, source_target_pairs={{0,2},{1,3},{2,0},{3,1},{4,6},{5,7},{6,4},{7,5},{8,10},{9,11},{10,... | collective-permute-start | bytes 786440 | tf_op jit(solution)/shard_map/ppermute | solution.py:619
  58.6 4.2 %collective-permute-start.6 = (bf16[128,1024]{1,0:T(8,128)(2,1)S(1)}, bf16[128,1024]{1,0:T(8,128)(2,1)S(1)}, u32[]{:S(2)}, u32[]{:S(2)}) collective-permute-start(bf16[128,1024]{1,0:T(8,128)(2,1)S(1)} %traded_pairs.1.turn_own), channel_id=1, source_target_pairs={{0,1},{1,0},{2,3},{3,2},{4,5},{5,4},{6,7},{7,6},{8,9},{9,8},{10,11... | collective-permute-start | bytes 786440 | tf_op jit(solution)/shard_map/ppermute | solution.py:623
  62.8 0.0 collective-permute-done.7.turn_far
  62.8 4.3 %collective-permute-start.8 = (bf16[128,1024]{1,0:T(8,128)(2,1)S(1)}, bf16[128,1024]{1,0:T(8,128)(2,1)S(1)}, u32[]{:S(2)}, u32[]{:S(2)}) collective-permute-start(bf16[128,1024]{1,0:T(8,128)(2,1)S(1)} %collective-permute-done.7.turn_far), channel_id=1, source_target_pairs={{0,1},{1,0},{2,3},{3,2},{4,5},{5,4},{6,7},{7,6},{8,9},{9,8},{10,11... | collective-permute-start | bytes 786440 | tf_op jit(solution)/shard_map/ppermute | solution.py:623
  67.1 0.0 collective-permute-done.6.turn_near
  67.1 1.1 collective-permute-done.8.turn_both
  68.3 7.9 %forward.1 = (bf16[256,2048]{1,0:T(8,128)(2,1)}, bf16[256,2048]{1,0:T(8,128)(2,1)}, bf16[256,2048]{1,0:T(8,128)(2,1)}, bf16[256,2048]{1,0:T(8,128)(2,1)}, bf16[1...) custom-call(s32[16]{0:T(128)} %bitcast.40, s32[384]{0:T(512)S(1)} %pad_add_fusion.meta_own, ...), custom_call_target="tpu_custom_call" | custom-call | flops 4000000000 | bytes 10000000 | tf_op jit(solution)/shard_map/forward/pallas_call | solution.py:328
  76.2 5.5 %all-to-all-start.1 = ((bf16[32,8,2048]{2,1,0:T(8,128)(2,1)}), bf16[32,8,2048]{2,1,0:T(8,128)(2,1)S(1)}, u32[]{:S(2)}, u32[]{:S(2)}) async-start(bf16[32,8,2048]{2,1,0:T(8,128)(2,1)} %bitcast.28), calls=%async_computation.1 | async-start | bytes 2097152 | tf_op jit(solution)/shard_map/all_to_all | solution.py:615
  81.7 9.4 %backward.1 = (bf16[256,2048]{1,0:T(8,128)(2,1)}, bf16[256,3072]{1,0:T(8,128)(2,1)}, bf16[2,128,1024]{2,1,0:T(8,128)(2,1)S(1)}, bf16[2,128,1024]{2,1,0:T(8,128)(...) custom-call(s32[16]{0:T(128)} %bitcast.41, s32[384]{0:T(512)S(1)} %pad_add_fusion.meta_own, ...), custom_call_target="tpu_custom_call" | custom-call | flops 8000000000 | bytes 10000000 | tf_op jit(solution)/shard_map/backward/pallas_call | solution.py:458
  91.1 0.1 collective-permute-start.9
  91.2 0.5 collective-permute-start.10
  91.7 1.4 collective-permute-done.9.near_ref
  93.1 0.8 fusion
  93.9 0.2 collective-permute-done.10.near_ref
  94.1 1.0 fusion.1
  95.1 4.5 %all-to-all-done.1 = bf16[32,8,2048]{2,1,0:T(8,128)(2,1)S(1)} async-done(((bf16[32,8,2048]{2,1,0:T(8,128)(2,1)}), bf16[32,8,2048]{2,1,0:T(8,128)(2,1)S(1)}, u32[]{:S(2)}, u32[]{:S(2)}) %all-to-all-start.1) | async-done | bytes 1048608 | tf_op jit(solution)/shard_map/all_to_all | solution.py:615
  99.6 2.4 %collective-permute-start.11 = (bf16[128,1024]{1,0:T(8,128)(2,1)}, bf16[128,1024]{1,0:T(8,128)(2,1)S(1)}, u32[]{:S(2)}, u32[]{:S(2)}) collective-permute-start(bf16[128,1024]{1,0:T(8,128)(2,1)} %fusion), channel_id=1, source_target_pairs={{0,2},{1,3},{2,0},{3,1},{4,6},{5,7},{6,4},{7,5},{8,10},{9,11},{10,... | collective-permute-start | bytes 786440 | tf_op jit(solution)/shard_map/ppermute | solution.py:619
  102.0 0.6 collective-permute-start.12
  102.5 5.6 %collective-permute-done.11.far_ref = bf16[128,1024]{1,0:T(8,128)(2,1)S(1)} collective-permute-done((bf16[128,1024]{1,0:T(8,128)(2,1)}, bf16[128,1024]{1,0:T(8,128)(2,1)S(1)}, u32[]{:S(2)}, u32[]{:S(2)}) %collective-permute-start.11) | collective-permute-done | bytes 262176 | tf_op jit(solution)/shard_map/ppermute | solution.py:619
  108.1 1.8 %returning.1 = bf16[256,3072]{1,0:T(8,128)(2,1)} custom-call(s32[16]{0:T(128)} %bitcast.42, bf16[256,3072]{1,0:T(8,128)(2,1)} %get-tuple-element.58.cargo_in, bf16[2,128,1024]{2,1,0:T(8,128)(2,1)S(1)} %get-tuple-element.52.own_ref, bf16[2,128,1024]{2,1,0:T(8,128)(2,1)S(1)} %collective-permute-done.9.near_ref, ...), custom_call_target="tpu_custom_call", output_to_operand_aliasing={{}: (1, {})} | custom-call | flops 100000000 | bytes 1000000 | tf_op jit(solution)/shard_map/returning/pallas_call | solution.py:513
  109.9 3.8 %collective-permute-done.12.far_ref = bf16[128,1024]{1,0:T(8,128)(2,1)S(1)} collective-permute-done((bf16[128,1024]{1,0:T(8,128)(2,1)S(1)}, bf16[128,1024]{1,0:T(8,128)(2,1)S(1)}, u32[]{:S(2)}, u32[]{:S(2)}) %collective-permute-start.12) | collective-permute-done | bytes 262176 | tf_op jit(solution)/shard_map/ppermute | solution.py:619
  113.7 8.3 %all-to-all-start.2 = ((bf16[32,8,3072]{2,1,0:T(8,128)(2,1)}), bf16[32,8,3072]{2,1,0:T(8,128)(2,1)S(1)}, u32[]{:S(2)}, u32[]{:S(2)}) async-start(bf16[32,8,3072]{2,1,0:T(8,128)(2,1)} %bitcast.27), calls=%async_computation.2 | async-start | bytes 3145728 | tf_op jit(solution)/shard_map/all_to_all | solution.py:615
  122.0 3.9 %merge.1 = bf16[256,2048]{1,0:T(8,128)(2,1)} custom-call(s32[16]{0:T(128)} %bitcast.43, s32[16]{0:T(128)} %bitcast.47, bf16[256,2048]{1,0:T(8,128)(2,1)} %get-tuple-element.46.own_ref, bf16[256,2048]{1,0:T(8,128)(2,1)S(1)} %bitcast.25), custom_call_target="tpu_custom_call" | custom-call | flops 500000000 | bytes 3000000 | tf_op jit(solution)/shard_map/merge/pallas_call | solution.py:538
  125.9 18.2 %all-to-all-done.2 = bf16[32,8,3072]{2,1,0:T(8,128)(2,1)S(1)} async-done(((bf16[32,8,3072]{2,1,0:T(8,128)(2,1)}), bf16[32,8,3072]{2,1,0:T(8,128)(2,1)S(1)}, u32[]{:S(2)}, u32[]{:S(2)}) %all-to-all-start.2) | async-done | bytes 1572896 | tf_op jit(solution)/shard_map/all_to_all | solution.py:615
  144.1 3.4 %finish.1 = (bf16[256,2048]{1,0:T(8,128)(2,1)}, bf16[256,512]{1,0:T(8,128)(2,1)}, bf16[256,512]{1,0:T(8,128)(2,1)}) custom-call(s32[16]{0:T(128)} %bitcast.44, s32[16]{0:T(128)} %bitcast.48, bf16[256,2048]{1,0:T(8,128)(2,1)} %get-tuple-element.57.dq_hbm, bf16[256,3072]{1,0:T(8,128)(2,1)S(1)} %bitcast.24, bf16[2,128,1024]{2,1,0:T(8,128)(2,1)} %get-tuple-element.54.own_hbm, ...), custom_call_target="tpu_custom_call" | custom-call | flops 800000000 | bytes 5000000 | tf_op jit(solution)/shard_map/finish/pallas_call | solution.py:594
  (5 shorter events, 0.0 us)
Async XLA Ops:
  2.6 10.5 %collective-permute-start = (bf16[128,1024]{1,0:T(8,128)(2,1)S(1)}, bf16[128,1024]{1,0:T(8,128)(2,1)S(1)}, u32[]{:S(2)}, u32[]{:S(2)}) collective-permute-start(bf16[128,1024]{1,0:T(8,128)(2,1)S(1)} %staying.1.stay_own), channel_id=1, source_target_pairs={{0,2},{1,3},{2,0},{3,1},{4,6},{5,7},{6,4},{7,5},{8,10},{9,11},{10,... | collective-permute-start | bytes 786440 | tf_op jit(solution)/shard_map/ppermute | solution.py:619
  13.1 9.6 %copy-start = (s32[1,1,16]{2,1,0:T(1,128)S(1)}, s32[1,1,16]{2,1,0:T(1,128)}, u32[]{:S(2)}) copy-start(s32[1,1,16]{2,1,0:T(1,128)} %param.13) | copy-start | bytes 196
  13.1 9.6 %copy-start.1 = (s32[1,256]{1,0:T(1,128)S(1)}, s32[1,256]{1,0:T(1,128)}, u32[]{:S(2)}) copy-start(s32[1,256]{1,0:T(1,128)} %param.11) | copy-start | bytes 3076
  13.1 41.2 %all-to-all-start = ((bf16[32,8,5120]{2,1,0:T(8,128)(2,1)}), bf16[32,8,5120]{2,1,0:T(8,128)(2,1)S(1)}, u32[]{:S(2)}, u32[]{:S(2)}) async-start(bf16[32,8,5120]{2,1,0:T(8,128)(2,1)} %bitcast.26), calls=%async_computation | async-start | bytes 5242880 | tf_op jit(solution)/shard_map/all_to_all | solution.py:615
  20.7 17.1 %collective-permute-start.1 = (bf16[128,1024]{1,0:T(8,128)(2,1)S(1)}, bf16[128,1024]{1,0:T(8,128)(2,1)S(1)}, u32[]{:S(2)}, u32[]{:S(2)}) collective-permute-start(bf16[128,1024]{1,0:T(8,128)(2,1)S(1)} %staying.1.stay_own), channel_id=1, source_target_pairs={{0,1},{1,0},{2,3},{3,2},{4,5},{5,4},{6,7},{7,6},{8,9},{9,8},{10,11... | collective-permute-start | bytes 786440 | tf_op jit(solution)/shard_map/ppermute | solution.py:623
  22.6 15.2 %collective-permute-start.2 = (bf16[128,1024]{1,0:T(8,128)(2,1)S(1)}, bf16[128,1024]{1,0:T(8,128)(2,1)}, u32[]{:S(2)}, u32[]{:S(2)}) collective-permute-start(bf16[128,1024]{1,0:T(8,128)(2,1)S(1)} %collective-permute-done.stay_far), channel_id=1, source_target_pairs={{0,1},{1,0},{2,3},{3,2},{4,5},{5,4},{6,7},{7,6},{8,9},{9,8},{10,11... | collective-permute-start | bytes 786440 | tf_op jit(solution)/shard_map/ppermute | solution.py:623
  22.8 15.0 %collective-permute-start.5 = (s32[384]{0:T(512)S(1)}, s32[384]{0:T(512)S(1)}, u32[]{:S(2)}, u32[]{:S(2)}) collective-permute-start(s32[384]{0:T(512)S(1)} %pad_add_fusion.meta_own), channel_id=1, source_target_pairs={{0,3},{1,2},{2,1},{3,0},{4,7},{5,6},{6,5},{7,4},{8,11},{9,10},{10,... | collective-permute-start | bytes 4616 | tf_op jit(solution)/shard_map/ppermute | solution.py:651
  26.4 11.3 %collective-permute-start.4 = (s32[384]{0:T(512)S(1)}, s32[384]{0:T(512)S(1)}, u32[]{:S(2)}, u32[]{:S(2)}) collective-permute-start(s32[384]{0:T(512)S(1)} %pad_add_fusion.meta_own), channel_id=1, source_target_pairs={{0,2},{1,3},{2,0},{3,1},{4,6},{5,7},{6,4},{7,5},{8,10},{9,11},{10,... | collective-permute-start | bytes 4616 | tf_op jit(solution)/shard_map/ppermute | solution.py:619
  26.4 11.3 %collective-permute-start.3 = (s32[384]{0:T(512)S(1)}, s32[384]{0:T(512)S(1)}, u32[]{:S(2)}, u32[]{:S(2)}) collective-permute-start(s32[384]{0:T(512)S(1)} %pad_add_fusion.meta_own), channel_id=1, source_target_pairs={{0,1},{1,0},{2,3},{3,2},{4,5},{5,4},{6,7},{7,6},{8,9},{9,8},{10,11... | collective-permute-start | bytes 4616 | tf_op jit(solution)/shard_map/ppermute | solution.py:623
  55.2 7.5 %collective-permute-start.7 = (bf16[128,1024]{1,0:T(8,128)(2,1)S(1)}, bf16[128,1024]{1,0:T(8,128)(2,1)S(1)}, u32[]{:S(2)}, u32[]{:S(2)}) collective-permute-start(bf16[128,1024]{1,0:T(8,128)(2,1)S(1)} %traded_pairs.1.turn_own), channel_id=1, source_target_pairs={{0,2},{1,3},{2,0},{3,1},{4,6},{5,7},{6,4},{7,5},{8,10},{9,11},{10,... | collective-permute-start | bytes 786440 | tf_op jit(solution)/shard_map/ppermute | solution.py:619
  58.6 8.5 %collective-permute-start.6 = (bf16[128,1024]{1,0:T(8,128)(2,1)S(1)}, bf16[128,1024]{1,0:T(8,128)(2,1)S(1)}, u32[]{:S(2)}, u32[]{:S(2)}) collective-permute-start(bf16[128,1024]{1,0:T(8,128)(2,1)S(1)} %traded_pairs.1.turn_own), channel_id=1, source_target_pairs={{0,1},{1,0},{2,3},{3,2},{4,5},{5,4},{6,7},{7,6},{8,9},{9,8},{10,11... | collective-permute-start | bytes 786440 | tf_op jit(solution)/shard_map/ppermute | solution.py:623
  62.8 5.5 %collective-permute-start.8 = (bf16[128,1024]{1,0:T(8,128)(2,1)S(1)}, bf16[128,1024]{1,0:T(8,128)(2,1)S(1)}, u32[]{:S(2)}, u32[]{:S(2)}) collective-permute-start(bf16[128,1024]{1,0:T(8,128)(2,1)S(1)} %collective-permute-done.7.turn_far), channel_id=1, source_target_pairs={{0,1},{1,0},{2,3},{3,2},{4,5},{5,4},{6,7},{7,6},{8,9},{9,8},{10,11... | collective-permute-start | bytes 786440 | tf_op jit(solution)/shard_map/ppermute | solution.py:623
  76.2 23.4 %all-to-all-start.1 = ((bf16[32,8,2048]{2,1,0:T(8,128)(2,1)}), bf16[32,8,2048]{2,1,0:T(8,128)(2,1)S(1)}, u32[]{:S(2)}, u32[]{:S(2)}) async-start(bf16[32,8,2048]{2,1,0:T(8,128)(2,1)} %bitcast.28), calls=%async_computation.1 | async-start | bytes 2097152 | tf_op jit(solution)/shard_map/all_to_all | solution.py:615
  91.1 2.0 %collective-permute-start.9 = (bf16[2,128,1024]{2,1,0:T(8,128)(2,1)S(1)}, bf16[2,128,1024]{2,1,0:T(8,128)(2,1)S(1)}, u32[]{:S(2)}, u32[]{:S(2)}) collective-permute-start(bf16[2,128,1024]{2,1,0:T(8,128)(2,1)S(1)} %get-tuple-element.53), channel_id=1, source_target_pairs={{0,1},{1,0},{2,3},{3,2},{4,5},{5,4},{6,7},{7,6},{8,9},{9,8},{10,11... | collective-permute-start | bytes 1572872 | tf_op jit(solution)/shard_map/ppermute | solution.py:623
  91.2 2.9 %collective-permute-start.10 = (bf16[2,128,1024]{2,1,0:T(8,128)(2,1)}, bf16[2,128,1024]{2,1,0:T(8,128)(2,1)S(1)}, u32[]{:S(2)}, u32[]{:S(2)}) collective-permute-start(bf16[2,128,1024]{2,1,0:T(8,128)(2,1)} %get-tuple-element.55), channel_id=1, source_target_pairs={{0,1},{1,0},{2,3},{3,2},{4,5},{5,4},{6,7},{7,6},{8,9},{9,8},{10,11... | collective-permute-start | bytes 1572872 | tf_op jit(solution)/shard_map/ppermute | solution.py:623
  99.6 8.5 %collective-permute-start.11 = (bf16[128,1024]{1,0:T(8,128)(2,1)}, bf16[128,1024]{1,0:T(8,128)(2,1)S(1)}, u32[]{:S(2)}, u32[]{:S(2)}) collective-permute-start(bf16[128,1024]{1,0:T(8,128)(2,1)} %fusion), channel_id=1, source_target_pairs={{0,2},{1,3},{2,0},{3,1},{4,6},{5,7},{6,4},{7,5},{8,10},{9,11},{10,... | collective-permute-start | bytes 786440 | tf_op jit(solution)/shard_map/ppermute | solution.py:619
  102.0 11.8 %collective-permute-start.12 = (bf16[128,1024]{1,0:T(8,128)(2,1)S(1)}, bf16[128,1024]{1,0:T(8,128)(2,1)S(1)}, u32[]{:S(2)}, u32[]{:S(2)}) collective-permute-start(bf16[128,1024]{1,0:T(8,128)(2,1)S(1)} %fusion.1), channel_id=1, source_target_pairs={{0,2},{1,3},{2,0},{3,1},{4,6},{5,7},{6,4},{7,5},{8,10},{9,11},{10,... | collective-permute-start | bytes 786440 | tf_op jit(solution)/shard_map/ppermute | solution.py:619
  113.7 30.4 %all-to-all-start.2 = ((bf16[32,8,3072]{2,1,0:T(8,128)(2,1)}), bf16[32,8,3072]{2,1,0:T(8,128)(2,1)S(1)}, u32[]{:S(2)}, u32[]{:S(2)}) async-start(bf16[32,8,3072]{2,1,0:T(8,128)(2,1)} %bitcast.27), calls=%async_computation.2 | async-start | bytes 3145728 | tf_op jit(solution)/shard_map/all_to_all | solution.py:615

commit v4 on v3

--- a/solution.py
+++ b/solution.py
@@ -211,13 +211,17 @@
     return count
 
 
-def fill_mask(mask, metas_ids, rank):
+def fill_mask(mask, metas_ids, rank, reach):
     ids = [piece[:, :ROWS].astype(F32) for piece in metas_ids]
     for x in range(RANKS):
-        allowed = to_column(ids[x]) == ids[0]
-        if x == 0:
-            allowed = allowed & (iota((ROWS, 1), 0) <= lanes(ROWS))
-        mask[pl.ds(pl.multiple_of((rank ^ x) * ROWS, ROWS), ROWS), :] = jnp.where(allowed, 0.0, MASKED)
+        other = rank ^ x
+
+        @pl.when((other <= rank) & ((rank - other - 1) * ROWS < reach))
+        def _(x=x, other=other):
+            allowed = to_column(ids[x]) == ids[0]
+            if x == 0:
+                allowed = allowed & (iota((ROWS, 1), 0) <= lanes(ROWS))
+            mask[pl.ds(pl.multiple_of(other * ROWS, ROWS), ROWS), :] = jnp.where(allowed, 0.0, MASKED)
 
 
 INNER = (((1,), (1,)), ((), ()))
@@ -240,7 +244,7 @@
     choose = choose_sent(mate, slot)
     bring[...] = choose_landed(mate, slot)
     came[...] = share_landed(bring[...])
-    fill_mask(mask, (ids_own, ids_near, ids_far, ids_both), rank)
+    fill_mask(mask, (ids_own, ids_near, ids_far, ids_both), rank, count * ROWS)
     stay = (stay_own, stay_near, stay_far, stay_both)
     turn = (turn_own, turn_near, turn_far, turn_both)
     for x in range(RANKS):
@@ -383,7 +387,7 @@
     rank = metas[0][ROWS + ROUNDS]
     count = earlier_blocks(metas, rank, KEYS)
     choose = choose_sent(scalars(mate_ref, 0, ROUNDS), scalars(metas[0], ROWS, ROUNDS))
-    fill_mask(mask, (ids_own, ids_near, ids_far, ids_both), rank)
+    fill_mask(mask, (ids_own, ids_near, ids_far, ids_both), rank, count * KEYS)
     total[...] = jnp.zeros_like(total)
 
     def leave(h):
@@ -435,11 +439,22 @@
 
     lax.fori_loop(0, KEY_VALUE_HEADS, head, 0)
     for x in range(RANKS):
-        rows = total[pl.ds(pl.multiple_of((rank ^ x) * ROWS, ROWS), ROWS), :]
-        pieces = pick(packing(scalars(metas[x], ROWS, ROUNDS)), rows)
+        other = rank ^ x
         stay, turn = ((stay_keep, turn_keep), (stay_send, turn_send))[x & 1]
-        stay[x >> 1] = pieces[:HALF]
-        turn[x >> 1] = pieces[HALF:]
+        reached = (other <= rank) & ((rank - other - 1) * ROWS < count * KEYS)
+
+        @pl.when(reached)
+        def _(x=x, other=other, stay=stay, turn=turn):
+            rows = total[pl.ds(pl.multiple_of(other * ROWS, ROWS), ROWS), :]
+            pieces = pick(packing(scalars(metas[x], ROWS, ROUNDS)), rows)
+            stay[x >> 1] = pieces[:HALF]
+            turn[x >> 1] = pieces[HALF:]
+
+        @pl.when(jnp.logical_not(reached))
+        def _(x=x, stay=stay, turn=turn):
+            stay[x >> 1] = jnp.zeros(stay.shape[1:], BF16)
+            turn[x >> 1] = jnp.zeros(turn.shape[1:], BF16)
+
     leaving = [
         pltpu.make_async_copy(stay_keep, keep_hbm, stay_left.at[0]),
         pltpu.make_async_copy(stay_send, send_hbm, stay_left.at[1]),

time: 150 us -> 151 us (level)
  Pallas kernels: 34.1 us -> 38.2 us
  waiting for transfers between devices: 63.4 us -> 60.9 us
    pallas_call x1, Pallas kernels: 9.43 us -> 12.2 us  [backward(): pl.pallas_call(backward_kernel, in_specs=[SMEM] * 5 + [VMEM] * 4 + [HBM]...]
    all_to_all x3, waiting for transfers between devices: 39.2 us -> 36.6 us  [exchange(): lax.all_to_all(blocks, 'dp', split_axis=0, concat_axis=0, tiled=True)]
  transfers between devices with their start and end apart: 16 -> 16, of which waited for: 10 -> 10; matrix products, arithmetic and copies ran while one was open for 1% -> 1% of each run, Pallas kernels for 13% -> 15%
where the time goes in v4:
time: 151 us; the launch traced here: 149 us
  waiting for transfers between devices  60.9 us (40%)
  starting transfers between devices  47.3 us (31%)
  Pallas kernels  38.2 us (25%)
  other arithmetic  1.86 us (1%)
    all_to_all x3, waiting for transfers between devices, exchange(): lax.all_to_all(blocks, 'dp', split_axis=0, concat_axis=0, tiled=True)  36.6 us
    all_to_all x3, starting transfers between devices, exchange(): lax.all_to_all(blocks, 'dp', split_axis=0, concat_axis=0, tiled=True)  21.2 us
    pallas_call x1, Pallas kernels, backward(): pl.pallas_call(backward_kernel, in_specs=[SMEM] * 5 + [VMEM] * 4 + [HBM]...  12.2 us
    ppermute x7, starting transfers between devices, beside(): return lax.ppermute(array, 'sp', [(i, i ^ 1) for i in range(RANKS)])  11.6 us
    ppermute x5, starting transfers between devices, across(): return lax.ppermute(array, 'sp', [(i, i ^ 2) for i in range(RANKS)])  10.9 us
    ppermute x1, waiting for transfers between devices, body(): lax.ppermute(meta, 'sp', [(i, i ^ 3) for i in range(RANKS)])  10.9 us
    ppermute x5, waiting for transfers between devices, across(): return lax.ppermute(array, 'sp', [(i, i ^ 2) for i in range(RANKS)])  10.7 us
    pallas_call x1, Pallas kernels, forward(): pl.pallas_call(forward_kernel, in_specs=[SMEM] * 5 + [VMEM] * 4 + [HBM] *...  9.27 us
  transfers between devices with their start and end apart: 16, of which 10 were waited for; matrix products, arithmetic and copies ran while one was open for 1% of the time, Pallas kernels for 15%

profile of v4, /device:TPU:1, one launch (start us, length us, event | category | flops | bytes accessed | tf_op | source)
XLA Modules:
  0.0 149.2 jit_solution(2401462537008169338)
XLA Ops:
  0.6 1.9 %staying.1.stay_own = bf16[128,1024]{1,0:T(8,128)(2,1)S(1)} custom-call(s32[16]{0:T(128)} %bitcast.45, bf16[256,512]{1,0:T(8,128)(2,1)} %bitcast.30, bf16[256,512]{1,0:T(8,128)(2,1)} %bitcast.32), custom_call_target="tpu_custom_call" | custom-call | flops 100000000 | bytes 1000000 | tf_op jit(solution)/shard_map/staying/pallas_call | solution.py:145
  2.6 4.5 %collective-permute-start = (bf16[128,1024]{1,0:T(8,128)(2,1)S(1)}, bf16[128,1024]{1,0:T(8,128)(2,1)S(1)}, u32[]{:S(2)}, u32[]{:S(2)}) collective-permute-start(bf16[128,1024]{1,0:T(8,128)(2,1)S(1)} %staying.1.stay_own), channel_id=1, source_target_pairs={{0,2},{1,3},{2,0},{3,1},{4,6},{5,7},{6,4},{7,5},{8,10},{9,11},{10,... | collective-permute-start | bytes 786440 | tf_op jit(solution)/shard_map/ppermute | solution.py:634
  7.1 4.8 %outgoing.1 = bf16[256,5120]{1,0:T(8,128)(2,1)} custom-call(s32[16]{0:T(128)} %bitcast.38, s32[16]{0:T(128)} %bitcast.46, bf16[256,2048]{1,0:T(8,128)(2,1)} %bitcast.34, bf16[256,512]{1,0:T(8,128)(2,1)} %bitcast.31, bf16[256,512]{1,0:T(8,128)(2,1)} %bitcast.33, bf16[256,2048]{1,0:T(8,128)(2,1)} %bitcast.36), custom_call_target="tpu_custom_call" | custom-call | flops 1000000000 | bytes 5000000 | tf_op jit(solution)/shard_map/outgoing/pallas_call | solution.py:169
  11.9 1.3 collective-permute-done.stay_far
  13.1 0.0 copy-start
  13.1 0.0 copy-start.1
  13.1 7.6 %all-to-all-start = ((bf16[32,8,5120]{2,1,0:T(8,128)(2,1)}), bf16[32,8,5120]{2,1,0:T(8,128)(2,1)S(1)}, u32[]{:S(2)}, u32[]{:S(2)}) async-start(bf16[32,8,5120]{2,1,0:T(8,128)(2,1)} %bitcast.26), calls=%async_computation | async-start | bytes 5242880 | tf_op jit(solution)/shard_map/all_to_all | solution.py:630
  20.7 1.9 %collective-permute-start.1 = (bf16[128,1024]{1,0:T(8,128)(2,1)S(1)}, bf16[128,1024]{1,0:T(8,128)(2,1)S(1)}, u32[]{:S(2)}, u32[]{:S(2)}) collective-permute-start(bf16[128,1024]{1,0:T(8,128)(2,1)S(1)} %staying.1.stay_own), channel_id=1, source_target_pairs={{0,1},{1,0},{2,3},{3,2},{4,5},{5,4},{6,7},{7,6},{8,9},{9,8},{10,11... | collective-permute-start | bytes 786440 | tf_op jit(solution)/shard_map/ppermute | solution.py:638
  22.6 0.1 collective-permute-start.2
  22.7 0.0 copy-done
  22.7 0.0 copy-done.1
  22.7 0.1 pad_add_fusion.meta_own
  22.8 3.6 %collective-permute-start.5 = (s32[384]{0:T(512)S(1)}, s32[384]{0:T(512)S(1)}, u32[]{:S(2)}, u32[]{:S(2)}) collective-permute-start(s32[384]{0:T(512)S(1)} %pad_add_fusion.meta_own), channel_id=1, source_target_pairs={{0,3},{1,2},{2,1},{3,0},{4,7},{5,6},{6,5},{7,4},{8,11},{9,10},{10,... | collective-permute-start | bytes 4616 | tf_op jit(solution)/shard_map/ppermute | solution.py:666
  26.4 0.0 collective-permute-start.4
  26.4 0.5 collective-permute-start.3
  26.9 10.9 %collective-permute-done.5.meta_both = s32[384]{0:T(512)S(1)} collective-permute-done((s32[384]{0:T(512)S(1)}, s32[384]{0:T(512)S(1)}, u32[]{:S(2)}, u32[]{:S(2)}) %collective-permute-start.5) | collective-permute-done | bytes 1568 | tf_op jit(solution)/shard_map/ppermute | solution.py:666
  37.8 0.0 collective-permute-done.4.meta_far
  37.8 0.0 collective-permute-done.3.meta_near
  37.8 0.0 collective-permute-done.1.stay_near
  37.8 0.0 collective-permute-done.2.stay_both
  37.8 16.5 %all-to-all-done = bf16[32,8,5120]{2,1,0:T(8,128)(2,1)S(1)} async-done(((bf16[32,8,5120]{2,1,0:T(8,128)(2,1)}), bf16[32,8,5120]{2,1,0:T(8,128)(2,1)S(1)}, u32[]{:S(2)}, u32[]{:S(2)}) %all-to-all-start) | async-done | bytes 2621472 | tf_op jit(solution)/shard_map/all_to_all | solution.py:630
  54.3 0.9 traded_pairs.1.turn_own
  55.2 3.4 %collective-permute-start.7 = (bf16[128,1024]{1,0:T(8,128)(2,1)S(1)}, bf16[128,1024]{1,0:T(8,128)(2,1)S(1)}, u32[]{:S(2)}, u32[]{:S(2)}) collective-permute-start(bf16[128,1024]{1,0:T(8,128)(2,1)S(1)} %traded_pairs.1.turn_own), channel_id=1, source_target_pairs={{0,2},{1,3},{2,0},{3,1},{4,6},{5,7},{6,4},{7,5},{8,10},{9,11},{10,... | collective-permute-start | bytes 786440 | tf_op jit(solution)/shard_map/ppermute | solution.py:634
  58.6 4.2 %collective-permute-start.6 = (bf16[128,1024]{1,0:T(8,128)(2,1)S(1)}, bf16[128,1024]{1,0:T(8,128)(2,1)S(1)}, u32[]{:S(2)}, u32[]{:S(2)}) collective-permute-start(bf16[128,1024]{1,0:T(8,128)(2,1)S(1)} %traded_pairs.1.turn_own), channel_id=1, source_target_pairs={{0,1},{1,0},{2,3},{3,2},{4,5},{5,4},{6,7},{7,6},{8,9},{9,8},{10,11... | collective-permute-start | bytes 786440 | tf_op jit(solution)/shard_map/ppermute | solution.py:638
  62.8 0.0 collective-permute-done.7.turn_far
  62.8 4.3 %collective-permute-start.8 = (bf16[128,1024]{1,0:T(8,128)(2,1)S(1)}, bf16[128,1024]{1,0:T(8,128)(2,1)S(1)}, u32[]{:S(2)}, u32[]{:S(2)}) collective-permute-start(bf16[128,1024]{1,0:T(8,128)(2,1)S(1)} %collective-permute-done.7.turn_far), channel_id=1, source_target_pairs={{0,1},{1,0},{2,3},{3,2},{4,5},{5,4},{6,7},{7,6},{8,9},{9,8},{10,11... | collective-permute-start | bytes 786440 | tf_op jit(solution)/shard_map/ppermute | solution.py:638
  67.1 0.0 collective-permute-done.6.turn_near
  67.1 1.1 collective-permute-done.8.turn_both
  68.3 9.3 %forward.1 = (bf16[256,2048]{1,0:T(8,128)(2,1)}, bf16[256,2048]{1,0:T(8,128)(2,1)}, bf16[256,2048]{1,0:T(8,128)(2,1)}, bf16[256,2048]{1,0:T(8,128)(2,1)}, bf16[1...) custom-call(s32[16]{0:T(128)} %bitcast.40, s32[384]{0:T(512)S(1)} %pad_add_fusion.meta_own, ...), custom_call_target="tpu_custom_call" | custom-call | flops 4000000000 | bytes 10000000 | tf_op jit(solution)/shard_map/forward/pallas_call | solution.py:332
  77.6 4.1 %all-to-all-start.1 = ((bf16[32,8,2048]{2,1,0:T(8,128)(2,1)}), bf16[32,8,2048]{2,1,0:T(8,128)(2,1)S(1)}, u32[]{:S(2)}, u32[]{:S(2)}) async-start(bf16[32,8,2048]{2,1,0:T(8,128)(2,1)} %bitcast.28), calls=%async_computation.1 | async-start | bytes 2097152 | tf_op jit(solution)/shard_map/all_to_all | solution.py:630
  81.7 12.2 %backward.1 = (bf16[256,2048]{1,0:T(8,128)(2,1)}, bf16[256,3072]{1,0:T(8,128)(2,1)}, bf16[2,128,1024]{2,1,0:T(8,128)(2,1)S(1)}, bf16[2,128,1024]{2,1,0:T(8,128)(...) custom-call(s32[16]{0:T(128)} %bitcast.41, s32[384]{0:T(512)S(1)} %pad_add_fusion.meta_own, ...), custom_call_target="tpu_custom_call" | custom-call | flops 8000000000 | bytes 10000000 | tf_op jit(solution)/shard_map/backward/pallas_call | solution.py:473
  93.9 0.1 collective-permute-start.9
  94.0 0.5 collective-permute-start.10
  94.4 1.4 collective-permute-done.9.near_ref
  95.8 0.8 fusion
  96.6 0.2 collective-permute-done.10.near_ref
  96.8 1.0 fusion.1
  97.8 1.7 %all-to-all-done.1 = bf16[32,8,2048]{2,1,0:T(8,128)(2,1)S(1)} async-done(((bf16[32,8,2048]{2,1,0:T(8,128)(2,1)}), bf16[32,8,2048]{2,1,0:T(8,128)(2,1)S(1)}, u32[]{:S(2)}, u32[]{:S(2)}) %all-to-all-start.1) | async-done | bytes 1048608 | tf_op jit(solution)/shard_map/all_to_all | solution.py:630
  99.6 2.4 %collective-permute-start.11 = (bf16[128,1024]{1,0:T(8,128)(2,1)}, bf16[128,1024]{1,0:T(8,128)(2,1)S(1)}, u32[]{:S(2)}, u32[]{:S(2)}) collective-permute-start(bf16[128,1024]{1,0:T(8,128)(2,1)} %fusion), channel_id=1, source_target_pairs={{0,2},{1,3},{2,0},{3,1},{4,6},{5,7},{6,4},{7,5},{8,10},{9,11},{10,... | collective-permute-start | bytes 786440 | tf_op jit(solution)/shard_map/ppermute | solution.py:634
  102.0 0.5 collective-permute-start.12
  102.5 5.6 %collective-permute-done.11.far_ref = bf16[128,1024]{1,0:T(8,128)(2,1)S(1)} collective-permute-done((bf16[128,1024]{1,0:T(8,128)(2,1)}, bf16[128,1024]{1,0:T(8,128)(2,1)S(1)}, u32[]{:S(2)}, u32[]{:S(2)}) %collective-permute-start.11) | collective-permute-done | bytes 262176 | tf_op jit(solution)/shard_map/ppermute | solution.py:634
  108.1 1.8 %returning.1 = bf16[256,3072]{1,0:T(8,128)(2,1)} custom-call(s32[16]{0:T(128)} %bitcast.42, bf16[256,3072]{1,0:T(8,128)(2,1)} %get-tuple-element.58.cargo_in, bf16[2,128,1024]{2,1,0:T(8,128)(2,1)S(1)} %get-tuple-element.52.own_ref, bf16[2,128,1024]{2,1,0:T(8,128)(2,1)S(1)} %collective-permute-done.9.near_ref, ...), custom_call_target="tpu_custom_call", output_to_operand_aliasing={{}: (1, {})} | custom-call | flops 100000000 | bytes 1000000 | tf_op jit(solution)/shard_map/returning/pallas_call | solution.py:528
  109.9 3.8 %collective-permute-done.12.far_ref = bf16[128,1024]{1,0:T(8,128)(2,1)S(1)} collective-permute-done((bf16[128,1024]{1,0:T(8,128)(2,1)S(1)}, bf16[128,1024]{1,0:T(8,128)(2,1)S(1)}, u32[]{:S(2)}, u32[]{:S(2)}) %collective-permute-start.12) | collective-permute-done | bytes 262176 | tf_op jit(solution)/shard_map/ppermute | solution.py:634
  113.7 9.5 %all-to-all-start.2 = ((bf16[32,8,3072]{2,1,0:T(8,128)(2,1)}), bf16[32,8,3072]{2,1,0:T(8,128)(2,1)S(1)}, u32[]{:S(2)}, u32[]{:S(2)}) async-start(bf16[32,8,3072]{2,1,0:T(8,128)(2,1)} %bitcast.27), calls=%async_computation.2 | async-start | bytes 3145728 | tf_op jit(solution)/shard_map/all_to_all | solution.py:630
  123.2 4.0 %merge.1 = bf16[256,2048]{1,0:T(8,128)(2,1)} custom-call(s32[16]{0:T(128)} %bitcast.43, s32[16]{0:T(128)} %bitcast.47, bf16[256,2048]{1,0:T(8,128)(2,1)} %get-tuple-element.46.own_ref, bf16[256,2048]{1,0:T(8,128)(2,1)S(1)} %bitcast.25), custom_call_target="tpu_custom_call" | custom-call | flops 500000000 | bytes 3000000 | tf_op jit(solution)/shard_map/merge/pallas_call | solution.py:553
  127.2 18.3 %all-to-all-done.2 = bf16[32,8,3072]{2,1,0:T(8,128)(2,1)S(1)} async-done(((bf16[32,8,3072]{2,1,0:T(8,128)(2,1)}), bf16[32,8,3072]{2,1,0:T(8,128)(2,1)S(1)}, u32[]{:S(2)}, u32[]{:S(2)}) %all-to-all-start.2) | async-done | bytes 1572896 | tf_op jit(solution)/shard_map/all_to_all | solution.py:630
  145.5 3.4 %finish.1 = (bf16[256,2048]{1,0:T(8,128)(2,1)}, bf16[256,512]{1,0:T(8,128)(2,1)}, bf16[256,512]{1,0:T(8,128)(2,1)}) custom-call(s32[16]{0:T(128)} %bitcast.44, s32[16]{0:T(128)} %bitcast.48, bf16[256,2048]{1,0:T(8,128)(2,1)} %get-tuple-element.57.dq_hbm, bf16[256,3072]{1,0:T(8,128)(2,1)S(1)} %bitcast.24, bf16[2,128,1024]{2,1,0:T(8,128)(2,1)} %get-tuple-element.54.own_hbm, ...), custom_call_target="tpu_custom_call" | custom-call | flops 800000000 | bytes 5000000 | tf_op jit(solution)/shard_map/finish/pallas_call | solution.py:609
  (5 shorter events, 0.0 us)
Async XLA Ops:
  2.6 10.5 %collective-permute-start = (bf16[128,1024]{1,0:T(8,128)(2,1)S(1)}, bf16[128,1024]{1,0:T(8,128)(2,1)S(1)}, u32[]{:S(2)}, u32[]{:S(2)}) collective-permute-start(bf16[128,1024]{1,0:T(8,128)(2,1)S(1)} %staying.1.stay_own), channel_id=1, source_target_pairs={{0,2},{1,3},{2,0},{3,1},{4,6},{5,7},{6,4},{7,5},{8,10},{9,11},{10,... | collective-permute-start | bytes 786440 | tf_op jit(solution)/shard_map/ppermute | solution.py:634
  13.1 9.6 %copy-start = (s32[1,1,16]{2,1,0:T(1,128)S(1)}, s32[1,1,16]{2,1,0:T(1,128)}, u32[]{:S(2)}) copy-start(s32[1,1,16]{2,1,0:T(1,128)} %param.13) | copy-start | bytes 196
  13.1 9.6 %copy-start.1 = (s32[1,256]{1,0:T(1,128)S(1)}, s32[1,256]{1,0:T(1,128)}, u32[]{:S(2)}) copy-start(s32[1,256]{1,0:T(1,128)} %param.11) | copy-start | bytes 3076
  13.1 41.2 %all-to-all-start = ((bf16[32,8,5120]{2,1,0:T(8,128)(2,1)}), bf16[32,8,5120]{2,1,0:T(8,128)(2,1)S(1)}, u32[]{:S(2)}, u32[]{:S(2)}) async-start(bf16[32,8,5120]{2,1,0:T(8,128)(2,1)} %bitcast.26), calls=%async_computation | async-start | bytes 5242880 | tf_op jit(solution)/shard_map/all_to_all | solution.py:630
  20.7 17.1 %collective-permute-start.1 = (bf16[128,1024]{1,0:T(8,128)(2,1)S(1)}, bf16[128,1024]{1,0:T(8,128)(2,1)S(1)}, u32[]{:S(2)}, u32[]{:S(2)}) collective-permute-start(bf16[128,1024]{1,0:T(8,128)(2,1)S(1)} %staying.1.stay_own), channel_id=1, source_target_pairs={{0,1},{1,0},{2,3},{3,2},{4,5},{5,4},{6,7},{7,6},{8,9},{9,8},{10,11... | collective-permute-start | bytes 786440 | tf_op jit(solution)/shard_map/ppermute | solution.py:638
  22.6 15.2 %collective-permute-start.2 = (bf16[128,1024]{1,0:T(8,128)(2,1)S(1)}, bf16[128,1024]{1,0:T(8,128)(2,1)}, u32[]{:S(2)}, u32[]{:S(2)}) collective-permute-start(bf16[128,1024]{1,0:T(8,128)(2,1)S(1)} %collective-permute-done.stay_far), channel_id=1, source_target_pairs={{0,1},{1,0},{2,3},{3,2},{4,5},{5,4},{6,7},{7,6},{8,9},{9,8},{10,11... | collective-permute-start | bytes 786440 | tf_op jit(solution)/shard_map/ppermute | solution.py:638
  22.8 15.0 %collective-permute-start.5 = (s32[384]{0:T(512)S(1)}, s32[384]{0:T(512)S(1)}, u32[]{:S(2)}, u32[]{:S(2)}) collective-permute-start(s32[384]{0:T(512)S(1)} %pad_add_fusion.meta_own), channel_id=1, source_target_pairs={{0,3},{1,2},{2,1},{3,0},{4,7},{5,6},{6,5},{7,4},{8,11},{9,10},{10,... | collective-permute-start | bytes 4616 | tf_op jit(solution)/shard_map/ppermute | solution.py:666
  26.4 11.3 %collective-permute-start.4 = (s32[384]{0:T(512)S(1)}, s32[384]{0:T(512)S(1)}, u32[]{:S(2)}, u32[]{:S(2)}) collective-permute-start(s32[384]{0:T(512)S(1)} %pad_add_fusion.meta_own), channel_id=1, source_target_pairs={{0,2},{1,3},{2,0},{3,1},{4,6},{5,7},{6,4},{7,5},{8,10},{9,11},{10,... | collective-permute-start | bytes 4616 | tf_op jit(solution)/shard_map/ppermute | solution.py:634
  26.4 11.3 %collective-permute-start.3 = (s32[384]{0:T(512)S(1)}, s32[384]{0:T(512)S(1)}, u32[]{:S(2)}, u32[]{:S(2)}) collective-permute-start(s32[384]{0:T(512)S(1)} %pad_add_fusion.meta_own), channel_id=1, source_target_pairs={{0,1},{1,0},{2,3},{3,2},{4,5},{5,4},{6,7},{7,6},{8,9},{9,8},{10,11... | collective-permute-start | bytes 4616 | tf_op jit(solution)/shard_map/ppermute | solution.py:638
  55.2 7.5 %collective-permute-start.7 = (bf16[128,1024]{1,0:T(8,128)(2,1)S(1)}, bf16[128,1024]{1,0:T(8,128)(2,1)S(1)}, u32[]{:S(2)}, u32[]{:S(2)}) collective-permute-start(bf16[128,1024]{1,0:T(8,128)(2,1)S(1)} %traded_pairs.1.turn_own), channel_id=1, source_target_pairs={{0,2},{1,3},{2,0},{3,1},{4,6},{5,7},{6,4},{7,5},{8,10},{9,11},{10,... | collective-permute-start | bytes 786440 | tf_op jit(solution)/shard_map/ppermute | solution.py:634
  58.6 8.5 %collective-permute-start.6 = (bf16[128,1024]{1,0:T(8,128)(2,1)S(1)}, bf16[128,1024]{1,0:T(8,128)(2,1)S(1)}, u32[]{:S(2)}, u32[]{:S(2)}) collective-permute-start(bf16[128,1024]{1,0:T(8,128)(2,1)S(1)} %traded_pairs.1.turn_own), channel_id=1, source_target_pairs={{0,1},{1,0},{2,3},{3,2},{4,5},{5,4},{6,7},{7,6},{8,9},{9,8},{10,11... | collective-permute-start | bytes 786440 | tf_op jit(solution)/shard_map/ppermute | solution.py:638
  62.8 5.5 %collective-permute-start.8 = (bf16[128,1024]{1,0:T(8,128)(2,1)S(1)}, bf16[128,1024]{1,0:T(8,128)(2,1)S(1)}, u32[]{:S(2)}, u32[]{:S(2)}) collective-permute-start(bf16[128,1024]{1,0:T(8,128)(2,1)S(1)} %collective-permute-done.7.turn_far), channel_id=1, source_target_pairs={{0,1},{1,0},{2,3},{3,2},{4,5},{5,4},{6,7},{7,6},{8,9},{9,8},{10,11... | collective-permute-start | bytes 786440 | tf_op jit(solution)/shard_map/ppermute | solution.py:638
  77.6 22.0 %all-to-all-start.1 = ((bf16[32,8,2048]{2,1,0:T(8,128)(2,1)}), bf16[32,8,2048]{2,1,0:T(8,128)(2,1)S(1)}, u32[]{:S(2)}, u32[]{:S(2)}) async-start(bf16[32,8,2048]{2,1,0:T(8,128)(2,1)} %bitcast.28), calls=%async_computation.1 | async-start | bytes 2097152 | tf_op jit(solution)/shard_map/all_to_all | solution.py:630
  93.9 2.0 %collective-permute-start.9 = (bf16[2,128,1024]{2,1,0:T(8,128)(2,1)S(1)}, bf16[2,128,1024]{2,1,0:T(8,128)(2,1)S(1)}, u32[]{:S(2)}, u32[]{:S(2)}) collective-permute-start(bf16[2,128,1024]{2,1,0:T(8,128)(2,1)S(1)} %get-tuple-element.53), channel_id=1, source_target_pairs={{0,1},{1,0},{2,3},{3,2},{4,5},{5,4},{6,7},{7,6},{8,9},{9,8},{10,11... | collective-permute-start | bytes 1572872 | tf_op jit(solution)/shard_map/ppermute | solution.py:638
  94.0 2.9 %collective-permute-start.10 = (bf16[2,128,1024]{2,1,0:T(8,128)(2,1)}, bf16[2,128,1024]{2,1,0:T(8,128)(2,1)S(1)}, u32[]{:S(2)}, u32[]{:S(2)}) collective-permute-start(bf16[2,128,1024]{2,1,0:T(8,128)(2,1)} %get-tuple-element.55), channel_id=1, source_target_pairs={{0,1},{1,0},{2,3},{3,2},{4,5},{5,4},{6,7},{7,6},{8,9},{9,8},{10,11... | collective-permute-start | bytes 1572872 | tf_op jit(solution)/shard_map/ppermute | solution.py:638
  99.6 8.5 %collective-permute-start.11 = (bf16[128,1024]{1,0:T(8,128)(2,1)}, bf16[128,1024]{1,0:T(8,128)(2,1)S(1)}, u32[]{:S(2)}, u32[]{:S(2)}) collective-permute-start(bf16[128,1024]{1,0:T(8,128)(2,1)} %fusion), channel_id=1, source_target_pairs={{0,2},{1,3},{2,0},{3,1},{4,6},{5,7},{6,4},{7,5},{8,10},{9,11},{10,... | collective-permute-start | bytes 786440 | tf_op jit(solution)/shard_map/ppermute | solution.py:634
  102.0 11.7 %collective-permute-start.12 = (bf16[128,1024]{1,0:T(8,128)(2,1)S(1)}, bf16[128,1024]{1,0:T(8,128)(2,1)S(1)}, u32[]{:S(2)}, u32[]{:S(2)}) collective-permute-start(bf16[128,1024]{1,0:T(8,128)(2,1)S(1)} %fusion.1), channel_id=1, source_target_pairs={{0,2},{1,3},{2,0},{3,1},{4,6},{5,7},{6,4},{7,5},{8,10},{9,11},{10,... | collective-permute-start | bytes 786440 | tf_op jit(solution)/shard_map/ppermute | solution.py:634
  113.7 31.8 %all-to-all-start.2 = ((bf16[32,8,3072]{2,1,0:T(8,128)(2,1)}), bf16[32,8,3072]{2,1,0:T(8,128)(2,1)S(1)}, u32[]{:S(2)}, u32[]{:S(2)}) async-start(bf16[32,8,3072]{2,1,0:T(8,128)(2,1)} %bitcast.27), calls=%async_computation.2 | async-start | bytes 3145728 | tf_op jit(solution)/shard_map/all_to_all | solution.py:630
